TPU v7x, 32 devices: a whole 2x2x4 slice. The times are simulated.
32 devices in a mesh: rows: 8 (over z, x), tp: 4 (over y, core).
Axes of the slice: x: 2, y: 2, z: 4, core: 2. Of those that a mesh axis runs over, the one named last changes fastest.
Arguments:
- tokens: bfloat16 [24576, 768], P(('rows', 'tp')), may hold values from -6 to 6
- frame_id: int32 [24576], P(('rows', 'tp')), may hold values from 0 to 15, as said below
- lead_index: int32 [16], P('rows'), may hold values from 0 to 31
- lead_embed: bfloat16 [32, 768], replicated, may hold values from -3 to 3
- ln1_gain: bfloat16 [768], replicated, may hold values from 0.5 to 1.5
- ln1_bias: bfloat16 [768], replicated, may hold values from -1 to 1
- qkv_weight: bfloat16 [3, 768, 768], P(None, None, 'tp'), may hold values from -0.21875 to 0.21875
- qv_bias: bfloat16 [2, 768], P(None, 'tp'), may hold values from -1.5 to 1.5
- out_weight: bfloat16 [768, 768], P('tp'), may hold values from -6 to 6
- out_bias: bfloat16 [768], replicated, may hold values from -1 to 1
- ln2_gain: bfloat16 [768], replicated, may hold values from 0.5 to 1.5
- ln2_bias: bfloat16 [768], replicated, may hold values from -1 to 1
- up_weight: bfloat16 [768, 3072], P(None, 'tp'), may hold values from -0.21875 to 0.21875
- up_bias: bfloat16 [3072], P('tp'), may hold values from -1.5 to 1.5
- down_weight: bfloat16 [3072, 768], P('tp'), may hold values from -0.109375 to 0.109375
- down_bias: bfloat16 [768], replicated, may hold values from -1 to 1
- out_grad: bfloat16 [24576, 768], P(('rows', 'tp')), may hold values from -6 to 6
Outputs:
- layer_out: bfloat16 [24576, 768], P(('rows', 'tp'))
- tokens_grad: float32 [24576, 768], P(('rows', 'tp'))
- lead_embed_grad: float32 [32, 768], replicated
- ln1_gain_grad: float32 [768], replicated
- ln1_bias_grad: float32 [768], replicated
- qkv_weight_grad: float32 [3, 768, 768], P(None, None, 'tp')
- qv_bias_grad: float32 [2, 768], P(None, 'tp')
- out_weight_grad: float32 [768, 768], P('tp')
- out_bias_grad: float32 [768], replicated
- ln2_gain_grad: float32 [768], replicated
- ln2_bias_grad: float32 [768], replicated
- up_weight_grad: float32 [768, 3072], P(None, 'tp')
- up_bias_grad: float32 [3072], P('tp')
- down_weight_grad: float32 [3072, 768], P('tp')
- down_bias_grad: float32 [768], replicated
Inputs may be any that keep to these rules, and one draw needn't show every extreme that they name: `frame_id`: patches 3072 * r to 3072 * r + 3071 carry frame ids 2 * r to 2 * r + 1; of these, id 2 * r names exactly 2048 patches and id 2 * r + 1 exactly 1024, in any order.
All inputs are finite; a program needn't handle non-finite values.
Results may differ from a plain program's by a relative error of at most 0.012.
Values may be sent and summed in bfloat16 or wider, within the bound.
No kernel may reach another device: no remote copies, remote signals or barrier semaphores. Data moves between devices by JAX's collectives and lax.ppermute only.
A program may use at most 192 MiB of HBM per device.

v0:
```python
import math

import jax
import jax.numpy as jnp
from jax import lax
from jax.sharding import PartitionSpec as P

HEAD = 64


def norm_parts(values, norm_gain, norm_shift):
    average = jnp.mean(values, axis=-1, keepdims=True)
    centred = values - average
    spread = jnp.mean(centred * centred, axis=-1, keepdims=True)
    return centred * lax.rsqrt(spread + 1e-05) * norm_gain + norm_shift


def on_device(
    tokens,
    frame_id,
    lead_index,
    lead_embed,
    ln1_gain,
    ln1_bias,
    qkv_weight,
    qv_bias,
    out_weight,
    out_bias,
    ln2_gain,
    ln2_bias,
    up_weight,
    up_bias,
    down_weight,
    down_bias,
    out_grad,
):
    f32 = jnp.float32
    bf16 = jnp.bfloat16
    local_width = qkv_weight.shape[2]
    local_heads = local_width // HEAD
    frames_here = lead_index.shape[0]
    leads = lead_embed.shape[0]
    scale = 1.0 / math.sqrt(HEAD)
    local_frame = frame_id - lax.axis_index("rows") * frames_here
    frame_hot = local_frame[:, None] == jnp.arange(frames_here, dtype=jnp.int32)[None, :]
    token_lead = jnp.sum(jnp.where(frame_hot, lead_index[None, :], 0), axis=1)
    lead_hot = (token_lead[:, None] == jnp.arange(leads, dtype=jnp.int32)[None, :]).astype(bf16)
    input_rows = tokens.astype(f32) + jnp.dot(lead_hot, lead_embed, preferred_element_type=f32)
    gain_one = ln1_gain.astype(f32)
    shift_one = ln1_bias.astype(f32)
    gain_two = ln2_gain.astype(f32)
    shift_two = ln2_bias.astype(f32)
    normed_one = norm_parts(input_rows, gain_one, shift_one).astype(bf16)
    normed_all, frame_all = (
        lax.all_gather(normed_one, "tp", axis=0, tiled=True),
        lax.all_gather(local_frame.astype(bf16), "tp", axis=0, tiled=True),
    )
    group = normed_all.shape[0]
    query_rows = (
        jnp.dot(normed_all, qkv_weight[0], preferred_element_type=f32) + qv_bias[0].astype(f32)
    ).astype(bf16)
    key_rows = jnp.dot(normed_all, qkv_weight[1], preferred_element_type=f32).astype(bf16)
    value_rows = (
        jnp.dot(normed_all, qkv_weight[2], preferred_element_type=f32) + qv_bias[1].astype(f32)
    ).astype(bf16)
    query_heads = query_rows.reshape(group, local_heads, HEAD)
    key_heads = key_rows.reshape(group, local_heads, HEAD)
    value_heads = value_rows.reshape(group, local_heads, HEAD)
    block = min(512, group)
    block_count = group // block

    def block_scores(first_row, query_block):
        frame_block = lax.dynamic_slice_in_dim(frame_all, first_row, block, 0)
        scores = (
            jnp.einsum("qhd,khd->hqk", query_block, key_heads, preferred_element_type=f32) * scale
        )
        live = frame_block[:, None] == frame_all[None, :]
        return jnp.where(live[None], scores, -1e30)

    def attend(block_index):
        first_row = block_index * block
        query_block = lax.dynamic_slice_in_dim(query_heads, first_row, block, 0)
        scores = block_scores(first_row, query_block)
        largest = jnp.max(scores, axis=-1, keepdims=True)
        raised = jnp.exp(scores - largest)
        totals = jnp.sum(raised, axis=-1, keepdims=True)
        probs = (raised / totals).astype(bf16)
        mixed = jnp.einsum("hqk,khd->qhd", probs, value_heads, preferred_element_type=f32)
        return (mixed.astype(bf16), largest[..., 0] + jnp.log(totals[..., 0]))

    mixed_blocks, log_totals = lax.map(attend, jnp.arange(block_count, dtype=jnp.int32))
    attended = mixed_blocks.reshape(group, local_width)
    attn_out = lax.psum_scatter(
        jnp.dot(attended, out_weight, preferred_element_type=f32),
        "tp",
        scatter_dimension=0,
        tiled=True,
    )
    x_one = input_rows + attn_out + out_bias.astype(f32)
    normed_two = norm_parts(x_one, gain_two, shift_two).astype(bf16)
    up_shift = up_bias.astype(f32)
    second_all = lax.all_gather(normed_two, "tp", axis=0, tiled=True)
    hidden = jnp.dot(second_all, up_weight, preferred_element_type=f32) + up_shift
    activated = jax.nn.gelu(hidden).astype(bf16)
    x_two = (
        x_one
        + lax.psum_scatter(
            jnp.dot(activated, down_weight, preferred_element_type=f32).astype(jnp.bfloat16),
            "tp",
            scatter_dimension=0,
            tiled=True,
        ).astype(jnp.float32)
        + down_bias.astype(f32)
    )
    layer_out = x_two.astype(bf16)
    grad_out = out_grad.astype(f32)
    down_bias_part = jnp.sum(grad_out, axis=0)
    grad_all = lax.all_gather(out_grad, "tp", axis=0, tiled=True)
    act_grad = jnp.einsum("gd,fd->gf", grad_all, down_weight, preferred_element_type=f32)
    down_weight_part = jnp.einsum("gf,gd->fd", activated, grad_all, preferred_element_type=f32)
    gelu_out, gelu_back = jax.vjp(jax.nn.gelu, hidden)
    hidden_grad = gelu_back(act_grad)[0].astype(bf16)
    up_weight_part = jnp.einsum("gd,gf->df", second_all, hidden_grad, preferred_element_type=f32)
    up_bias_part = jnp.sum(hidden_grad.astype(f32), axis=0)
    normed_two_grad = lax.psum_scatter(
        jnp.einsum("gf,df->gd", hidden_grad, up_weight, preferred_element_type=f32),
        "tp",
        scatter_dimension=0,
        tiled=True,
    )
    norm_out, norm_two_back = jax.vjp(norm_parts, x_one, gain_two, shift_two)
    x_one_part, gain_two_part, shift_two_part = norm_two_back(normed_two_grad)
    x_one_grad = grad_out + x_one_part
    attn_grad = x_one_grad.astype(bf16)
    out_bias_part = jnp.sum(attn_grad.astype(f32), axis=0)
    attn_grad_all = lax.all_gather(attn_grad, "tp", axis=0, tiled=True)
    attended_grad = jnp.einsum(
        "gd,cd->gc", attn_grad_all, out_weight, preferred_element_type=f32
    ).astype(bf16)
    out_weight_part = jnp.einsum("gc,gd->cd", attended, attn_grad_all, preferred_element_type=f32)
    attended_heads = attended_grad.reshape(group, local_heads, HEAD)

    def back_step(carry, stepped):
        key_acc, value_acc = carry
        block_index, block_totals = stepped
        first_row = block_index * block
        query_block = lax.dynamic_slice_in_dim(query_heads, first_row, block, 0)
        upper_block = lax.dynamic_slice_in_dim(attended_heads, first_row, block, 0)
        scores = block_scores(first_row, query_block)
        probs = jnp.exp(scores - block_totals[:, :, None])
        probs_grad = jnp.einsum(
            "qhd,khd->hqk", upper_block, value_heads, preferred_element_type=f32
        )
        inner = jnp.sum(probs * probs_grad, axis=-1, keepdims=True)
        scores_grad = (probs * (probs_grad - inner)).astype(bf16)
        query_block_grad = (
            jnp.einsum("hqk,khd->qhd", scores_grad, key_heads, preferred_element_type=f32) * scale
        )
        key_acc = (
            key_acc
            + jnp.einsum("hqk,qhd->khd", scores_grad, query_block, preferred_element_type=f32)
            * scale
        )
        value_acc = value_acc + jnp.einsum(
            "hqk,qhd->khd", probs.astype(bf16), upper_block, preferred_element_type=f32
        )
        return ((key_acc, value_acc), query_block_grad)

    empty = jnp.zeros((group, local_heads, HEAD), f32)
    (key_total, value_total), query_blocks = lax.scan(
        back_step, (empty, empty), (jnp.arange(block_count, dtype=jnp.int32), log_totals)
    )
    query_grad = query_blocks.reshape(group, local_width).astype(bf16)
    key_grad = key_total.reshape(group, local_width).astype(bf16)
    value_grad = value_total.reshape(group, local_width).astype(bf16)
    qkv_part = jnp.stack(
        [
            jnp.einsum("gd,gc->dc", normed_all, query_grad, preferred_element_type=f32),
            jnp.einsum("gd,gc->dc", normed_all, key_grad, preferred_element_type=f32),
            jnp.einsum("gd,gc->dc", normed_all, value_grad, preferred_element_type=f32),
        ]
    )
    qv_part = jnp.stack(
        [jnp.sum(query_grad.astype(f32), axis=0), jnp.sum(value_grad.astype(f32), axis=0)]
    )
    total = jnp.einsum("gc,dc->gd", query_grad, qkv_weight[0], preferred_element_type=f32)
    total = total + jnp.einsum("gc,dc->gd", key_grad, qkv_weight[1], preferred_element_type=f32)
    normed_one_grad = lax.psum_scatter(
        (
            total + jnp.einsum("gc,dc->gd", value_grad, qkv_weight[2], preferred_element_type=f32)
        ).astype(jnp.bfloat16),
        "tp",
        scatter_dimension=0,
        tiled=True,
    ).astype(jnp.float32)
    norm_first, norm_one_back = jax.vjp(norm_parts, input_rows, gain_one, shift_one)
    input_part, gain_one_part, shift_one_part = norm_one_back(normed_one_grad)
    tokens_grad = x_one_grad + input_part
    lead_part = jnp.einsum(
        "tl,td->ld", lead_hot.astype(f32), tokens_grad, precision=lax.Precision.HIGHEST
    )
    qkv_sum, qv_sum, out_w_sum, up_w_sum, up_b_sum, down_w_sum = lax.psum(
        (qkv_part, qv_part, out_weight_part, up_weight_part, up_bias_part, down_weight_part), "rows"
    )
    lead_sum, gain_one_sum, shift_one_sum, gain_two_sum, shift_two_sum, out_b_sum, down_b_sum = (
        lax.psum(
            (
                lead_part,
                gain_one_part,
                shift_one_part,
                gain_two_part,
                shift_two_part,
                out_bias_part,
                down_bias_part,
            ),
            ("rows", "tp"),
        )
    )
    return (
        layer_out,
        tokens_grad,
        lead_sum,
        gain_one_sum,
        shift_one_sum,
        qkv_sum,
        qv_sum,
        out_w_sum,
        out_b_sum,
        gain_two_sum,
        shift_two_sum,
        up_w_sum,
        up_b_sum,
        down_w_sum,
        down_b_sum,
    )


def solution(mesh):
    placed = (
        P(("rows", "tp"), None),
        P(("rows", "tp")),
        P("rows"),
        P(),
        P(),
        P(),
        P(None, None, "tp"),
        P(None, "tp"),
        P("tp", None),
        P(),
        P(),
        P(),
        P(None, "tp"),
        P("tp"),
        P("tp", None),
        P(),
        P(("rows", "tp"), None),
    )
    return jax.shard_map(
        on_device,
        mesh=mesh,
        in_specs=placed,
        out_specs=(
            P(("rows", "tp"), None),
            P(("rows", "tp"), None),
            P(),
            P(),
            P(),
            P(None, None, "tp"),
            P(None, "tp"),
            P("tp", None),
            P(),
            P(),
            P(),
            P(None, "tp"),
            P("tp"),
            P("tp", None),
            P(),
        ),
        check_vma=False,
    )
```

profile of v0, /device:TPU:0, one launch (start us, length us, event | category | flops | bytes accessed | tf_op | source)
XLA Modules:
  0.0 1363.3 jit_solution(3470976319618890217)
XLA Ops:
  14.0 6.2 all-gather
  20.3 34.0 %all-gather.6.cloned.1.call-done = bf16[3072,768]{0,1:T(8,128)(2,1)} async-done(((bf16[768,768]{0,1:T(8,128)(2,1)}), bf16[3072,768]{0,1:T(8,128)(2,1)}) %all-gather.6.cloned.1.call-update) | async-done | bytes 4718608 | tf_op jit(solution)/shard_map/all_gather | solution.py:55
  63.2 132.6 %while.27 = (s32[]{:T(128)}, bf16[6,512,3,64]{1,3,2,0:T(8,128)(2,1)}, f32[6,3,512]{2,1,0:T(4,128)}, s32[6]{0:T(128)S(1)}, bf16[3072]{0:T(1024)(128)(2,1)S(1)}, /...) while((s32[]{:T(128)}, ...), condition=%wide.region_6.7_spmd, body=%wide.region_3.6_spmd.sunk | while | flops 1266252288 | bytes 72019176 | solution.py:91
  65.8 5.8 fusion.145
  71.6 5.3 fusion.146
  76.9 8.1 fusion.147
  87.8 5.8 fusion.145
  93.7 5.3 fusion.146
  99.0 8.1 fusion.147
  109.8 5.8 fusion.145
  115.7 5.3 fusion.146
  121.0 8.1 fusion.147
  131.9 5.8 fusion.145
  137.8 5.3 fusion.146
  143.0 8.1 fusion.147
  153.9 5.8 fusion.145
  159.8 5.3 fusion.146
  165.1 8.1 fusion.147
  176.0 5.8 fusion.145
  181.8 5.3 fusion.146
  187.1 8.1 fusion.147
  207.1 75.9 %reduce-scatter.5.cloned.1.call-done = f32[768,768]{0,1:T(8,128)} async-done(((f32[3072,768]{0,1:T(8,128)}), f32[768,768]{0,1:T(8,128)}) %reduce-scatter.5.cloned.1.call-update) | async-done | bytes 2359312 | tf_op jit(solution)/shard_map/reduce_scatter | solution.py:93
  289.1 37.0 %all-gather.8.cloned.1.call-done = bf16[3072,768]{0,1:T(8,128)(2,1)} async-done(((bf16[768,768]{0,1:T(8,128)(2,1)}), bf16[3072,768]{0,1:T(8,128)(2,1)}) %all-gather.8.cloned.1.call-update) | async-done | bytes 4718608 | tf_op jit(solution)/shard_map/all_gather | solution.py:102
  326.1 9.3 fusion.81
  335.4 29.6 %all-gather.10.cloned.1.call-done = bf16[3072,768]{1,0:T(8,128)(2,1)} async-done(((bf16[768,768]{1,0:T(8,128)(2,1)}), bf16[3072,768]{1,0:T(8,128)(2,1)}) %all-gather.10.cloned.1.call-update) | async-done | bytes 4718608 | tf_op jit(solution)/shard_map/all_gather | solution.py:118
  365.0 14.9 %convert_reduce_fusion = (f32[768]{0:T(1024)}, bf16[3072,768]{1,0:T(8,128)(2,1)S(1)}, bf16[3072,768]{1,0:T(8,128)(2,1)}) fusion(f32[3072,768]{1,0:T(8,128)} %fusion.81, f32[768]{0:T(1024)S(1)} %convert_element_type.142, bf16[3072,768]{1,0:T(8,128)(2,1)} %all-gather.10.cloned.1.call-done, bf16[768,768]{1,0:T(8,128)(2,1)S(1)} %copy-done), kind=kOutput, calls=%fused_computation.53 | convolution fusion | flops 3682860288 | bytes 24778752 | tf_op jit(solution)/shard_map/gd,fd->gf/dot_general | solution.py:119
  382.0 6.3 fusion.82
  388.3 7.9 convolution_convert_fusion
  399.7 67.2 %reduce-scatter.9.cloned.1.call-done = f32[768,768]{0,1:T(8,128)} async-done(((f32[3072,768]{0,1:T(8,128)}), f32[768,768]{0,1:T(8,128)}) %reduce-scatter.9.cloned.1.call-update) | async-done | bytes 2359312 | tf_op jit(solution)/shard_map/reduce_scatter | solution.py:125
  470.6 46.6 %reduce-scatter.7.cloned.1.call-done = bf16[768,768]{0,1:T(8,128)(2,1)} async-done(((bf16[3072,768]{0,1:T(8,128)(2,1)}), bf16[768,768]{0,1:T(8,128)(2,1)}) %reduce-scatter.7.cloned.1.call-update) | async-done | bytes 1179664 | tf_op jit(solution)/shard_map/reduce_scatter | solution.py:107
  523.5 37.5 %all-gather.12.cloned.1.call-done = bf16[3072,768]{0,1:T(8,128)(2,1)} async-done(((bf16[768,768]{0,1:T(8,128)(2,1)}), bf16[3072,768]{0,1:T(8,128)(2,1)}) %all-gather.12.cloned.1.call-update) | async-done | bytes 4718608 | tf_op jit(solution)/shard_map/all_gather | solution.py:136
  565.5 350.7 %while.28 = (s32[]{:T(128)}, f32[3072,3,64]{0,2,1:T(8,128)}, f32[3072,3,64]{0,2,1:T(8,128)}, bf16[6,512,3,64]{1,3,2,0:T(8,128)(2,1)}, s32[6]{0:T(128)S(1)}, /*in...) while((s32[]{:T(128)}, f32[3072,3,64]{0,2,1:T(8,128)}, ...), condition=%wide.region_16.17_spmd.clone, body=%wide.region_14.16_spmd.clone.sunk | while | flops 3095296512 | bytes 237554960 | solution.py:170
  572.1 6.4 copy-done.2
  578.6 7.9 fusion.159
  586.5 14.3 %multiply_reduce_fusion.6 = (f32[3,512]{1,0:T(4,128)S(1)}, f32[3,512,3072]{2,1,0:T(8,128)}) fusion(f32[3,512,3072]{2,1,0:T(8,128)} %copy-done.2, f32[3,512]{1,0:T(4,128)S(1)} %dynamic-slice_bitcast_fusion.2, pred[512,3072]{1,0:T(8,128)(4,1)S(1)} %broadcast_compare_fusion.5, bf16[3072,3,64]{0,2,1:T(8,128)(2,1)} %get-tuple-element.499, ...), kind=kOutput, calls=%fused_computation.17.clone.1 | convolution fusion | flops 627571200 | bytes 40710148 | tf_op jit(solution)/shard_map/while/body/eval_jaxpr/qhd,khd->hqk/dot_general | solution.py:151
  600.8 13.9 %multiply_convert_fusion.3 = bf16[3,512,3072]{2,1,0:T(8,128)(2,1)S(1)} fusion(f32[3,512,3072]{2,1,0:T(8,128)} %get-tuple-element.421, f32[3,512,3072]{2,1,0:T(8,128)} %copy-done.2, f32[3,512]{1,0:T(4,128)S(1)} %get-tuple-element.422, f32[3,512]{1,0:T(4,128)S(1)} %dynamic-slice_bitcast_fusion.2, pred[512,3072]{1,0:T(8,128)(4,1)S(1)} %broadcast_compare_fusion.5), kind=kLoop, calls=%fused_computation.16.clone.1 | loop fusion | flops 28311552 | bytes 48771072 | tf_op jit(solution)/shard_map/while/body/eval_jaxpr/convert_element_type | solution.py:155
  629.1 6.4 copy-done.2
  635.5 8.8 fusion.159
  644.3 14.3 %multiply_reduce_fusion.6 = (f32[3,512]{1,0:T(4,128)S(1)}, f32[3,512,3072]{2,1,0:T(8,128)}) fusion(f32[3,512,3072]{2,1,0:T(8,128)} %copy-done.2, f32[3,512]{1,0:T(4,128)S(1)} %dynamic-slice_bitcast_fusion.2, pred[512,3072]{1,0:T(8,128)(4,1)S(1)} %broadcast_compare_fusion.5, bf16[3072,3,64]{0,2,1:T(8,128)(2,1)} %get-tuple-element.499, ...), kind=kOutput, calls=%fused_computation.17.clone.1 | convolution fusion | flops 627571200 | bytes 40710148 | tf_op jit(solution)/shard_map/while/body/eval_jaxpr/qhd,khd->hqk/dot_general | solution.py:151
  658.6 13.9 %multiply_convert_fusion.3 = bf16[3,512,3072]{2,1,0:T(8,128)(2,1)S(1)} fusion(f32[3,512,3072]{2,1,0:T(8,128)} %get-tuple-element.421, f32[3,512,3072]{2,1,0:T(8,128)} %copy-done.2, f32[3,512]{1,0:T(4,128)S(1)} %get-tuple-element.422, f32[3,512]{1,0:T(4,128)S(1)} %dynamic-slice_bitcast_fusion.2, pred[512,3072]{1,0:T(8,128)(4,1)S(1)} %broadcast_compare_fusion.5), kind=kLoop, calls=%fused_computation.16.clone.1 | loop fusion | flops 28311552 | bytes 48771072 | tf_op jit(solution)/shard_map/while/body/eval_jaxpr/convert_element_type | solution.py:155
  687.7 6.4 copy-done.2
  694.1 8.8 fusion.159
  702.9 14.3 %multiply_reduce_fusion.6 = (f32[3,512]{1,0:T(4,128)S(1)}, f32[3,512,3072]{2,1,0:T(8,128)}) fusion(f32[3,512,3072]{2,1,0:T(8,128)} %copy-done.2, f32[3,512]{1,0:T(4,128)S(1)} %dynamic-slice_bitcast_fusion.2, pred[512,3072]{1,0:T(8,128)(4,1)S(1)} %broadcast_compare_fusion.5, bf16[3072,3,64]{0,2,1:T(8,128)(2,1)} %get-tuple-element.499, ...), kind=kOutput, calls=%fused_computation.17.clone.1 | convolution fusion | flops 627571200 | bytes 40710148 | tf_op jit(solution)/shard_map/while/body/eval_jaxpr/qhd,khd->hqk/dot_general | solution.py:151
  717.2 13.9 %multiply_convert_fusion.3 = bf16[3,512,3072]{2,1,0:T(8,128)(2,1)S(1)} fusion(f32[3,512,3072]{2,1,0:T(8,128)} %get-tuple-element.421, f32[3,512,3072]{2,1,0:T(8,128)} %copy-done.2, f32[3,512]{1,0:T(4,128)S(1)} %get-tuple-element.422, f32[3,512]{1,0:T(4,128)S(1)} %dynamic-slice_bitcast_fusion.2, pred[512,3072]{1,0:T(8,128)(4,1)S(1)} %broadcast_compare_fusion.5), kind=kLoop, calls=%fused_computation.16.clone.1 | loop fusion | flops 28311552 | bytes 48771072 | tf_op jit(solution)/shard_map/while/body/eval_jaxpr/convert_element_type | solution.py:155
  746.3 6.4 copy-done.2
  752.7 8.8 fusion.159
  761.5 14.3 %multiply_reduce_fusion.6 = (f32[3,512]{1,0:T(4,128)S(1)}, f32[3,512,3072]{2,1,0:T(8,128)}) fusion(f32[3,512,3072]{2,1,0:T(8,128)} %copy-done.2, f32[3,512]{1,0:T(4,128)S(1)} %dynamic-slice_bitcast_fusion.2, pred[512,3072]{1,0:T(8,128)(4,1)S(1)} %broadcast_compare_fusion.5, bf16[3072,3,64]{0,2,1:T(8,128)(2,1)} %get-tuple-element.499, ...), kind=kOutput, calls=%fused_computation.17.clone.1 | convolution fusion | flops 627571200 | bytes 40710148 | tf_op jit(solution)/shard_map/while/body/eval_jaxpr/qhd,khd->hqk/dot_general | solution.py:151
  775.9 13.9 %multiply_convert_fusion.3 = bf16[3,512,3072]{2,1,0:T(8,128)(2,1)S(1)} fusion(f32[3,512,3072]{2,1,0:T(8,128)} %get-tuple-element.421, f32[3,512,3072]{2,1,0:T(8,128)} %copy-done.2, f32[3,512]{1,0:T(4,128)S(1)} %get-tuple-element.422, f32[3,512]{1,0:T(4,128)S(1)} %dynamic-slice_bitcast_fusion.2, pred[512,3072]{1,0:T(8,128)(4,1)S(1)} %broadcast_compare_fusion.5), kind=kLoop, calls=%fused_computation.16.clone.1 | loop fusion | flops 28311552 | bytes 48771072 | tf_op jit(solution)/shard_map/while/body/eval_jaxpr/convert_element_type | solution.py:155
  805.0 6.4 copy-done.2
  811.4 8.8 fusion.159
  820.2 14.3 %multiply_reduce_fusion.6 = (f32[3,512]{1,0:T(4,128)S(1)}, f32[3,512,3072]{2,1,0:T(8,128)}) fusion(f32[3,512,3072]{2,1,0:T(8,128)} %copy-done.2, f32[3,512]{1,0:T(4,128)S(1)} %dynamic-slice_bitcast_fusion.2, pred[512,3072]{1,0:T(8,128)(4,1)S(1)} %broadcast_compare_fusion.5, bf16[3072,3,64]{0,2,1:T(8,128)(2,1)} %get-tuple-element.499, ...), kind=kOutput, calls=%fused_computation.17.clone.1 | convolution fusion | flops 627571200 | bytes 40710148 | tf_op jit(solution)/shard_map/while/body/eval_jaxpr/qhd,khd->hqk/dot_general | solution.py:151
  834.6 13.9 %multiply_convert_fusion.3 = bf16[3,512,3072]{2,1,0:T(8,128)(2,1)S(1)} fusion(f32[3,512,3072]{2,1,0:T(8,128)} %get-tuple-element.421, f32[3,512,3072]{2,1,0:T(8,128)} %copy-done.2, f32[3,512]{1,0:T(4,128)S(1)} %get-tuple-element.422, f32[3,512]{1,0:T(4,128)S(1)} %dynamic-slice_bitcast_fusion.2, pred[512,3072]{1,0:T(8,128)(4,1)S(1)} %broadcast_compare_fusion.5), kind=kLoop, calls=%fused_computation.16.clone.1 | loop fusion | flops 28311552 | bytes 48771072 | tf_op jit(solution)/shard_map/while/body/eval_jaxpr/convert_element_type | solution.py:155
  863.7 6.4 copy-done.2
  870.1 8.8 fusion.159
  878.9 14.3 %multiply_reduce_fusion.6 = (f32[3,512]{1,0:T(4,128)S(1)}, f32[3,512,3072]{2,1,0:T(8,128)}) fusion(f32[3,512,3072]{2,1,0:T(8,128)} %copy-done.2, f32[3,512]{1,0:T(4,128)S(1)} %dynamic-slice_bitcast_fusion.2, pred[512,3072]{1,0:T(8,128)(4,1)S(1)} %broadcast_compare_fusion.5, bf16[3072,3,64]{0,2,1:T(8,128)(2,1)} %get-tuple-element.499, ...), kind=kOutput, calls=%fused_computation.17.clone.1 | convolution fusion | flops 627571200 | bytes 40710148 | tf_op jit(solution)/shard_map/while/body/eval_jaxpr/qhd,khd->hqk/dot_general | solution.py:151
  893.2 13.9 %multiply_convert_fusion.3 = bf16[3,512,3072]{2,1,0:T(8,128)(2,1)S(1)} fusion(f32[3,512,3072]{2,1,0:T(8,128)} %get-tuple-element.421, f32[3,512,3072]{2,1,0:T(8,128)} %copy-done.2, f32[3,512]{1,0:T(4,128)S(1)} %get-tuple-element.422, f32[3,512]{1,0:T(4,128)S(1)} %dynamic-slice_bitcast_fusion.2, pred[512,3072]{1,0:T(8,128)(4,1)S(1)} %broadcast_compare_fusion.5), kind=kLoop, calls=%fused_computation.16.clone.1 | loop fusion | flops 28311552 | bytes 48771072 | tf_op jit(solution)/shard_map/while/body/eval_jaxpr/convert_element_type | solution.py:155
  924.4 5.1 add_convert_fusion
  929.7 9.4 fusion.85
  939.0 9.5 fusion.84
  964.4 13.2 reduce-scatter.11.cloned.1.call-done
  987.2 23.5 %all-reduce.1 = (f32[2,192]{1,0:T(2,128)}, f32[768]{0:T(1024)}) all-reduce(f32[2,192]{1,0:T(2,128)S(1)} %pad_maximum_fusion.1, f32[768]{0:T(1024)S(1)} %copy-done.54), channel_id=1, replica_groups=mesh['rows'=8,'tp'=4] {'rows'}, use_global_device_ids=true, to_apply=%region_28.29 | all-reduce | flops 1152 | bytes 9216 | tf_op jit(solution)/shard_map/psum | solution.py:202
  1013.9 41.5 %all-reduce = (f32[768]{0:T(1024)}, f32[768]{0:T(1024)}, f32[768]{0:T(1024)}, f32[768]{0:T(1024)}, f32[768]{0:T(1024)}, /*index=5*/f32[768]{0:T(1024)}) all-reduce(f32[768]{0:T(1024)S(1)} %copy-done.53, f32[768]{0:T(1024)S(1)} %copy-done.52, f32[768]{0:T(1024)S(1)} %copy-done.51, ...), channel_id=1, replica_groups=mesh['rows'=8,'tp'=4] {'rows','tp'}, use_global_device_ids=true, to_apply=%region_22.23 | all-reduce | flops 4608 | bytes 36864 | tf_op jit(solution)/shard_map/psum | solution.py:206
  1055.4 165.2 %all-reduce.8.cloned.1.call-done = (f32[3,768,192]{1,2,0:T(8,128)}, f32[192,768]{1,0:T(8,128)}, f32[768,768]{1,0:T(8,128)}, f32[768,768]{1,0:T(8,128)}) async-done(((f32[3,768,192]{1,2,0:T(8,128)}, f32[192,768]{1,0:T(8,128)}, f32[768,768]{1,0:T(8,128)}, f32[768,768]{1,0:T(8,128)}), (f32[3,768,192]{1,2,0:T(8,128)}, f32[192,768]{1,0:T(8,128)}, f32[768,768]{1,0:T(8,128)}, ...) | async-done | bytes 7077904 | tf_op jit(solution)/shard_map/psum | solution.py:202
  1220.6 126.5 %all-reduce.6.cloned.1.call-done = f32[32,768]{1,0:T(8,128)} async-done(((f32[32,768]{1,0:T(8,128)}), f32[32,768]{1,0:T(8,128)}) %all-reduce.6.cloned.1.call-update) | async-done | bytes 98320 | tf_op jit(solution)/shard_map/psum | solution.py:206
  (310 shorter events, 198.3 us)
Async XLA Ops:
  7.2 357.8 %copy-start = (bf16[768,768]{1,0:T(8,128)(2,1)S(1)}, bf16[768,768]{1,0:T(8,128)(2,1)}, u32[]{:S(2)}) copy-start(bf16[768,768]{1,0:T(8,128)(2,1)} %param.35) | copy-start | bytes 3538948
  7.2 3.1 copy-start.55
  7.2 3.1 copy-start.61
  7.2 3.2 copy-start.39
  7.2 47.0 %all-gather.6.cloned.1.call-start = ((), (), s32[]{:S(2)}) async-start(), calls=%async_computation.4 | async-start | bytes 5898240 | tf_op jit(solution)/shard_map/all_gather | solution.py:55
  8.0 3.4 copy-start.34
  11.4 2.5 copy-start.44
  12.5 7.8 copy-start.56
  12.5 41.7 %copy-start.27 = (bf16[3,768,192]{1,2,0:T(8,128)(2,1)S(1)}, bf16[3,768,192]{1,2,0:T(8,128)(2,1)}, u32[]{:S(2)}) copy-start(bf16[3,768,192]{1,2,0:T(8,128)(2,1)} %param.27) | copy-start | bytes 2654212
  14.0 269.1 %reduce-scatter.5.cloned.1.call-start = ((), (), s32[]{:S(2)}) async-start(), calls=%async_computation.5 | async-start | bytes 11796480 | tf_op jit(solution)/shard_map/reduce_scatter | solution.py:93
  54.3 4.6 copy-start.21
  65.8 5.9 copy-start.3
  87.8 5.9 copy-start.3
  109.8 5.9 copy-start.3
  131.9 5.9 copy-start.3
  153.9 5.9 copy-start.3
  176.0 5.9 copy-start.3
  195.8 3.5 copy-start.29
  204.4 78.6 %copy-start.6 = (f32[768,768]{0,1:T(8,128)S(1)}, f32[768,768]{0,1:T(8,128)}, u32[]{:S(2)}) copy-start(f32[768,768]{0,1:T(8,128)} %copy-done.5) | copy-start | bytes 7077892
  204.4 121.6 %all-gather.8.cloned.1.call-start = ((), (), s32[]{:S(2)}) async-start(), calls=%async_computation.6 | async-start | bytes 5898240 | tf_op jit(solution)/shard_map/all_gather | solution.py:102
  287.0 39.1 %copy-start.62 = (bf16[768,768]{1,0:T(8,128)(2,1)S(1)}, bf16[768,768]{1,0:T(8,128)(2,1)}, u32[]{:S(2)}) copy-start(bf16[768,768]{1,0:T(8,128)(2,1)} %param.33) | copy-start | bytes 3538948
  288.4 76.5 %all-gather.10.cloned.1.call-start = ((), (), s32[]{:S(2)}) async-start(), calls=%async_computation.8 | async-start | bytes 5898240 | tf_op jit(solution)/shard_map/all_gather | solution.py:118
  289.0 177.9 %reduce-scatter.9.cloned.1.call-start = ((), (), s32[]{:S(2)}) async-start(), calls=%async_computation.9 | async-start | bytes 11796480 | tf_op jit(solution)/shard_map/reduce_scatter | solution.py:125
  388.3 128.9 %reduce-scatter.7.cloned.1.call-start = ((), (), s32[]{:S(2)}) async-start(), calls=%async_computation.7 | async-start | bytes 5898240 | tf_op jit(solution)/shard_map/reduce_scatter | solution.py:107
  396.3 70.6 %copy-start.9 = (f32[768,768]{0,1:T(8,128)S(1)}, f32[768,768]{0,1:T(8,128)}, u32[]{:S(2)}) copy-start(f32[768,768]{0,1:T(8,128)} %copy-done.8) | copy-start | bytes 7077892
  396.3 164.7 %all-gather.12.cloned.1.call-start = ((), (), s32[]{:S(2)}) async-start(), calls=%async_computation.10 | async-start | bytes 5898240 | tf_op jit(solution)/shard_map/all_gather | solution.py:136
  398.4 122.7 %copy-start.14 = (bf16[768,768]{0,1:T(8,128)(2,1)}, bf16[768,768]{0,1:T(8,128)(2,1)S(1)}, u32[]{:S(2)}) copy-start(bf16[768,768]{0,1:T(8,128)(2,1)S(1)} %copy.70) | copy-start | bytes 3538948
  466.9 3.1 copy-start.47
  521.1 40.0 %copy-start.30 = (bf16[192,768]{1,0:T(8,128)(2,1)S(1)}, bf16[192,768]{1,0:T(8,128)(2,1)}, u32[]{:S(2)}) copy-start(bf16[192,768]{1,0:T(8,128)(2,1)} %param.29) | copy-start | bytes 884740
  523.4 454.2 %reduce-scatter.11.cloned.1.call-start = ((), (), s32[]{:S(2)}) async-start(), calls=%async_computation.11 | async-start | bytes 5898240 | tf_op jit(solution)/shard_map/reduce_scatter | solution.py:188
  523.5 42.0 %copy-start.4 = (bf16[3072,3,64]{0,2,1:T(8,128)(2,1)S(1)}, bf16[3072,3,64]{0,2,1:T(8,128)(2,1)}, u32[]{:S(2)}) copy-start(bf16[3072,3,64]{0,2,1:T(8,128)(2,1)} %get-tuple-element.536) | copy-start | bytes 3538948
  572.1 6.4 copy-start.2
  629.0 6.4 copy-start.2
  687.7 6.4 copy-start.2
  746.3 6.4 copy-start.2
  805.0 6.4 copy-start.2
  863.7 6.4 copy-start.2
  919.3 3.7 copy-start.18
  929.6 291.0 %all-reduce.8.cloned.1.call-start = ((), (), s32[]{:S(2)}) async-start(), calls=%async_computation.13 | async-start | bytes 14155776 | tf_op jit(solution)/shard_map/psum | solution.py:202
  929.7 18.9 %slice-start = ((s8[4718592]{0:T(1024)(128)(4,1)}), s8[4194304]{0:T(1024)(128)(4,1)S(1)}, s32[]{:S(2)}) async-start(s8[4718592]{0:T(1024)(128)(4,1)} %bitcast.146), calls=%async_computation.14 | async-start | bytes 8388608
  939.0 9.5 copy-start.19
  939.0 9.5 slice-start.1
  950.3 4.8 slice-start.2
  952.0 3.1 slice-start.3
  958.2 19.4 %copy-start.7 = (f32[768,768]{0,1:T(8,128)S(1)}, f32[768,768]{0,1:T(8,128)}, u32[]{:S(2)}) copy-start(f32[768,768]{0,1:T(8,128)} %copy-done.5) | copy-start | bytes 7077892
  958.2 19.4 %copy-start.33 = (f32[768]{0:T(1024)S(1)}, f32[768]{0:T(1024)}, u32[]{:S(2)}) copy-start(f32[768]{0:T(1024)} %copy-done.32) | copy-start | bytes 9220
  958.2 19.4 %copy-start.35 = (f32[768]{0:T(1024)S(1)}, f32[768]{0:T(1024)}, u32[]{:S(2)}) copy-start(f32[768]{0:T(1024)} %copy-done.34) | copy-start | bytes 9220
  958.2 388.9 %all-reduce.6.cloned.1.call-start = ((), (), s32[]{:S(2)}) async-start(), calls=%async_computation.12 | async-start | bytes 196608 | tf_op jit(solution)/shard_map/psum | solution.py:206
  960.9 19.5 %copy-start.45 = (f32[768]{0:T(1024)S(1)}, f32[768]{0:T(1024)}, u32[]{:S(2)}) copy-start(f32[768]{0:T(1024)} %copy-done.44) | copy-start | bytes 9220
  960.9 19.5 %copy-start.37 = (f32[768]{0:T(1024)S(1)}, f32[768]{0:T(1024)}, u32[]{:S(2)}) copy-start(f32[768]{0:T(1024)} %copy-done.36) | copy-start | bytes 9220
  977.6 2.8 copy-start.13
  982.3 2.7 copy-start.43
  983.7 3.5 copy-start.57
  983.7 3.5 copy-start.58
  983.7 3.5 copy-start.54
  1010.7 3.1 copy-start.49
  1010.7 3.1 copy-start.50
  1010.7 3.1 copy-start.51
  1010.7 3.1 copy-start.52
  1010.7 3.1 copy-start.53
  1220.6 131.0 %copy-start.31 = (f32[192,768]{1,0:T(8,128)S(1)}, f32[192,768]{1,0:T(8,128)}, u32[]{:S(2)}) copy-start(f32[192,768]{1,0:T(8,128)} %get-tuple-element.511) | copy-start | bytes 1769476
  1348.6 3.8 copy-start.25
  1352.4 2.5 copy-start.24
  1352.4 3.9 copy-start.1
  (24 other events, 38.3 us)
Sparse Core Ops, SparseCore 0:
  14.1 40.1 all-gather.5
  204.5 78.4 reduce-scatter.4
  288.6 37.4 all-gather.7
  327.5 37.4 all-gather.9
  388.4 78.4 reduce-scatter.8
  469.3 47.8 reduce-scatter.6
  523.5 37.4 all-gather.11
  929.7 47.8 reduce-scatter.10
  983.2 237.3 all-reduce.7
  1227.5 119.5 all-reduce.5
where the time goes:
time: 1370 us; the launch traced here: 1360 us
  waiting for transfers between devices  633 us (46%)
  matrix products  388 us (28%)
  other arithmetic  162 us (12%)
  local copies, waits for them, and re-layouts  84 us (6%)
  blocking collectives  71.2 us (5%)
  between operations  15.1 us (1%)
    psum x1, waiting for transfers between devices, on_device(): lax.psum((qkv_part, qv_part, out_weight_part, up_weight_part, up_bias_par...  165 us
    psum x1, waiting for transfers between devices, on_device(): lax.psum((lead_part, gain_one_part, shift_one_part, gain_two_part, shift_...  127 us
    dot_general x6, matrix products, back_step(): jnp.einsum('qhd,khd->hqk', upper_block, value_heads, preferred_element_ty...  86 us
    convert_element_type x6, other arithmetic, back_step(): scores_grad = (probs * (probs_grad - inner)).astype(bf16)  83.2 us
    reduce_scatter x1, waiting for transfers between devices, on_device(): lax.psum_scatter(jnp.dot(attended, out_weight, preferred_element_type=f32...  75.9 us
    reduce_scatter x1, waiting for transfers between devices, on_device(): lax.psum_scatter(jnp.einsum('gf,df->gd', hidden_grad, up_weight, preferre...  67.2 us
    dot_general x12, matrix products, block_scores(): jnp.einsum('qhd,khd->hqk', query_block, key_heads, preferred_element_type...  56.5 us
    dot_general x6, matrix products, back_step(): jnp.einsum('hqk,qhd->khd', probs.astype(bf16), upper_block, preferred_ele...  51.9 us
  transfers between devices with their start and end apart: 10, of which 10 were waited for; matrix products, arithmetic and copies ran while one was open for 5% of the time, Pallas kernels for 0%

commit v1 on v0

v1 whole, which is shorter than its diff:
```python
import functools
import math

import jax
import jax.numpy as jnp
from jax import lax
from jax.experimental import pallas as pl
from jax.experimental.pallas import tpu as pltpu
from jax.sharding import PartitionSpec as P

HEAD = 64
EPS = 1e-05
LOG2E = math.log2(math.e)
LN2 = math.log(2.0)
TILE = 256
PAD = 16
VMEM_LIMIT = 60 * 1024 * 1024

f32 = jnp.float32
bf16 = jnp.bfloat16
i32 = jnp.int32

CORE = ((0, 1), (1, 0), (2, 3), (3, 2))
NEXT = ((0, 2), (2, 0), (1, 3), (3, 1))
DIAG = ((0, 3), (3, 0), (1, 2), (2, 1))

PARAMS = pltpu.CompilerParams(vmem_limit_bytes=VMEM_LIMIT)


def iota(shape, axis):
    return lax.broadcasted_iota(i32, shape, axis)


def dot(left, right, dims):
    return lax.dot_general(left, right, (dims, ((), ())), preferred_element_type=f32)


NN = ((1,), (0,))
NT = ((1,), (1,))
TN = ((0,), (0,))


def shape_of(shape, dtype):
    return jax.ShapeDtypeStruct(shape, dtype)


def whole_specs(count):
    return [pl.BlockSpec(memory_space=pltpu.VMEM)] * count


SMEM = pl.BlockSpec(memory_space=pltpu.SMEM)
VMEM = pl.BlockSpec(memory_space=pltpu.VMEM)
HBM = pl.BlockSpec(memory_space=pl.ANY)


def call(body, out_shape, in_specs, out_specs, name, flops=0, nbytes=0, scratch=(), grid=()):
    return pl.pallas_call(
        body,
        out_shape=out_shape,
        grid=grid,
        in_specs=in_specs,
        out_specs=out_specs,
        scratch_shapes=scratch,
        compiler_params=PARAMS,
        name=name,
        cost_estimate=pl.CostEstimate(
            flops=int(flops), bytes_accessed=int(nbytes), transcendentals=0
        ),
    )


def lead_hot(frame_ref, lead_ref, leads):
    frame = frame_ref[...]
    lead = jnp.where(frame == 0, lead_ref[0], lead_ref[1])
    return (iota((leads, frame.shape[1]), 0) == lead).astype(bf16)


def rows_with_lead(tok_ref, frame_ref, lead_ref, table_ref):
    hot = lead_hot(frame_ref, lead_ref, table_ref.shape[0])
    return tok_ref[...].astype(f32) + dot(hot, table_ref[...], TN), hot


def norm_stats(values):
    average = jnp.mean(values, axis=-1, keepdims=True)
    centred = values - average
    spread = jnp.mean(centred * centred, axis=-1, keepdims=True)
    inverse = lax.rsqrt(spread + EPS)
    return centred * inverse, inverse


def pre_kernel(tok_ref, frame_ref, lead_ref, table_ref, gain_ref, shift_ref, out_ref, perm_ref):
    rows = tok_ref.shape[0]
    values, _ = rows_with_lead(tok_ref, frame_ref, lead_ref, table_ref)
    unit, _ = norm_stats(values)
    normed = (unit * gain_ref[...] + shift_ref[...]).astype(bf16)
    first = (frame_ref[...] == 0).astype(f32)
    before = (iota((rows, rows), 0) < iota((rows, rows), 1)).astype(bf16)
    earlier = dot(jnp.broadcast_to(first, (8, rows)).astype(bf16), before, NN)[0:1]
    count = jnp.sum(first, axis=1, keepdims=True)
    place = jnp.where(first > 0, earlier, count + iota((1, rows), 1).astype(f32) - earlier)
    perm = (iota((rows, rows), 0) == place.astype(i32)).astype(bf16)
    perm_ref[...] = perm
    out_ref[0:rows, :] = dot(perm, normed, NN).astype(bf16)
    high = jnp.floor(count * (1.0 / 16))
    low = count - 16 * high
    tail = iota((PAD, out_ref.shape[1]), 0)
    out_ref[rows : rows + PAD, :] = jnp.where(
        tail == 0, high, jnp.where(tail == 1, low, 0.0)
    ).astype(bf16)


def read_count(block_ref, rows):
    part = block_ref[rows : rows + PAD, 0:128].astype(f32)
    place, lane = iota(part.shape, 0), iota(part.shape, 1)
    worth = jnp.where(place == 0, 16.0, jnp.where(place == 1, 1.0, 0.0))
    return jnp.sum(jnp.where(lane == 0, part * worth, 0.0)).astype(i32)


def tile_moves(counts, rows, long, block, tile):
    count = counts[block]
    longs_before = sum(counts[:block], jnp.int32(0))
    shorts_before = block * rows - longs_before
    limit = jnp.clip(count - tile * TILE, 0, TILE)
    moves = []
    base = longs_before + tile * TILE
    spot = base // TILE
    shift = base - spot * TILE
    moves.append((spot, shift, 0, limit, limit > 0))
    moves.append((spot + 1, shift - TILE, 0, limit, shift + limit > TILE))
    base = long + shorts_before - count + tile * TILE
    spot = base // TILE
    shift = base - spot * TILE
    some = limit < TILE
    moves.append((spot, shift, limit, TILE, some & (shift + limit < TILE)))
    moves.append((spot + 1, shift - TILE, limit, TILE, some & (shift > 0)))
    return moves


def aligned(index, size):
    return pl.ds(pl.multiple_of(index * size, size), size)


def to_group(value, dst_ref, moves, columns=slice(None)):
    for spot, shift, low, high, some in moves:

        @pl.when(some)
        def _():
            dest, source = iota((TILE, TILE), 0), iota((TILE, TILE), 1)
            hot = (dest - source == shift) & (source >= low) & (source < high)
            moved = dot(hot.astype(bf16), value, NN)
            place = (aligned(spot, TILE), columns)
            dst_ref[place] = (dst_ref[place].astype(f32) + moved).astype(dst_ref.dtype)


def from_group(src_ref, acc_ref, moves):
    acc_ref[...] = jnp.zeros(acc_ref.shape, acc_ref.dtype)
    for spot, shift, low, high, some in moves:

        @pl.when(some)
        def _():
            source, dest = iota((TILE, TILE), 0), iota((TILE, TILE), 1)
            hot = (dest - source == shift) & (source >= low) & (source < high)
            acc_ref[...] += dot(hot.astype(bf16), src_ref[aligned(spot, TILE), :], NN)


def attend_kernel(
    x0_ref, x1_ref, x2_ref, x3_ref, weight_ref, bias_ref, scale_ref,
    att_ref, attended_ref, q_ref, k_ref, v_ref, counts_ref,
    qkv_ref, acc_ref,
):
    blocks = (x0_ref, x1_ref, x2_ref, x3_ref)
    rows = x0_ref.shape[0] - PAD
    group = len(blocks) * rows
    long = 2 * group // 3
    width = weight_ref.shape[1] // 3
    heads = width // HEAD
    counts = [read_count(ref, rows) for ref in blocks]
    for index, count in enumerate(counts):
        counts_ref[index] = count
    qkv_ref[...] = jnp.zeros(qkv_ref.shape, qkv_ref.dtype)
    for index, ref in enumerate(blocks):

        def project(tile, _, index=index, ref=ref):
            value = dot(ref[aligned(tile, TILE), :], weight_ref[...], NN)
            value = ((value + bias_ref[...]) * scale_ref[...]).astype(bf16)
            to_group(value, qkv_ref, tile_moves(counts, rows, long, index, tile))
            return 0

        lax.fori_loop(0, rows // TILE, project, 0)
    for head in range(heads):
        lane = iota((group, 128), 1)
        for part, ref, fill in ((0, q_ref, 0.0), (1, k_ref, 1.0), (2, v_ref, 1.0)):
            start = part * width + head * HEAD
            first = start // 128 * 128
            piece = qkv_ref[:, first : first + 128].astype(f32) if first + 128 <= 3 * width else None
            if piece is None:
                piece = jnp.concatenate(
                    [qkv_ref[:, first : first + HEAD].astype(f32)] * 2, axis=1
                )
            if start != first:
                piece = pltpu.roll(piece, HEAD, 1)
            ref[head] = jnp.where(lane < HEAD, piece, fill).astype(bf16)

    def one_block(first, block, low, high):
        place = pl.ds(pl.multiple_of(first, block), block)
        outs = []
        lane = iota((block, 128), 1)
        for head in range(heads):
            query = q_ref[head, place, :]
            scores = dot(query, k_ref[head, low:high, :], NT)
            largest = jnp.max(scores, axis=1, keepdims=True)
            raised = jnp.exp2(scores - largest).astype(bf16)
            mixed = dot(raised, v_ref[head, low:high, :], NN)
            totals = mixed[:, HEAD : HEAD + 1]
            outs.append(jnp.where(lane < HEAD, mixed / totals, 0.0))
            less = -(largest + jnp.log2(totals))
            one = less.astype(bf16).astype(f32)
            two = (less - one).astype(bf16).astype(f32)
            three = less - one - two
            extra = jnp.where(
                lane == HEAD, one, jnp.where(lane == HEAD + 1, two, jnp.where(lane == HEAD + 2, three, 0.0))
            )
            q_ref[head, place, :] = jnp.where(lane < HEAD, query.astype(f32), extra).astype(bf16)
        for pair in range((heads + 1) // 2):
            value = outs[2 * pair]
            if 2 * pair + 1 < heads:
                value = value + pltpu.roll(outs[2 * pair + 1], HEAD, 1)
            att_ref[place, pair * 128 : (pair + 1) * 128] = value.astype(bf16)

    block = TILE

    def long_step(step, _):
        one_block(step * block, block, 0, long)
        return 0

    def short_step(step, _):
        one_block(long + step * block, block, long, group)
        return 0

    lax.fori_loop(0, long // block, long_step, 0)
    lax.fori_loop(0, (group - long) // block, short_step, 0)
    for index in range(len(blocks)):

        def hand_back(tile, _, index=index):
            from_group(att_ref, acc_ref, tile_moves(counts, rows, long, index, tile))
            attended_ref[index, aligned(tile, TILE), :] = acc_ref[:, 0:width].astype(bf16)
            return 0

        lax.fori_loop(0, rows // TILE, hand_back, 0)


def middle_kernel(
    tok_ref, frame_ref, lead_ref, table_ref, perm_ref,
    at0_ref, at1_ref, at2_ref, at3_ref,
    wo0_ref, wo1_ref, wo2_ref, wo3_ref,
    up0_ref, up1_ref, up2_ref, up3_ref,
    ub0_ref, ub1_ref, ub2_ref, ub3_ref,
    dn0_ref, dn1_ref, dn2_ref, dn3_ref,
    vec_ref, og_ref,
    layer_ref, xgrad_ref, agrad_ref, normed_ref, act_ref, hid_ref, attu_ref, send_ref, sums_ref, upb_ref,
    y_ref, back_ref,
):
    ats = (at0_ref, at1_ref, at2_ref, at3_ref)
    wos = (wo0_ref, wo1_ref, wo2_ref, wo3_ref)
    ups = (up0_ref, up1_ref, up2_ref, up3_ref)
    ubs = (ub0_ref, ub1_ref, ub2_ref, ub3_ref)
    dns = (dn0_ref, dn1_ref, dn2_ref, dn3_ref)
    gain, shift, out_bias, down_bias = (vec_ref[i : i + 1, :] for i in range(4))
    values, _ = rows_with_lead(tok_ref, frame_ref, lead_ref, table_ref)
    perm = perm_ref[...]
    x_one = values + out_bias
    for index in range(4):
        mine = dot(perm, ats[index][...], TN).astype(bf16)
        attu_ref[index] = mine
        x_one = x_one + dot(mine, wos[index][...], NN)
    unit, inverse = norm_stats(x_one)
    normed_ref[...] = (unit * gain + shift).astype(bf16)
    y_ref[...] = x_one + down_bias
    back_ref[...] = jnp.zeros(back_ref.shape, f32)
    hidden = up0_ref.shape[1]
    chunk = TILE
    for index in range(4):

        def step(part, _, index=index):
            cols = aligned(part, chunk)
            up = ups[index][:, cols]
            down = dns[index][cols, :]
            h = dot(normed_ref[...], up, NN) + ubs[index][0:1, cols].astype(f32)
            g = dot(og_ref[...], down, NT)
            c = math.sqrt(2.0 / math.pi)
            h2 = h * h
            t = jnp.tanh(h * (c + (c * 0.044715) * h2))
            half = 0.5 + 0.5 * t
            act = h * half
            slope = half + act * (1.0 - t) * (c + (3 * c * 0.044715) * h2)
            hid = (slope * g).astype(bf16)
            actb = act.astype(bf16)
            act_ref[index, :, cols] = actb
            hid_ref[index, :, cols] = hid
            upb_ref[index, 0:8, cols] = jnp.broadcast_to(
                jnp.sum(hid.astype(f32), axis=0, keepdims=True), (8, chunk)
            )
            y_ref[...] += dot(actb, down, NN)
            back_ref[...] += dot(hid, up, NT)
            return 0

        lax.fori_loop(0, hidden // chunk, step, 0)
    layer_ref[...] = y_ref[...].astype(bf16)
    grad = back_ref[...]
    e = grad * gain
    spread_mean = jnp.mean(e, axis=-1, keepdims=True)
    along = jnp.mean(e * unit, axis=-1, keepdims=True)
    og = og_ref[...].astype(f32)
    xgrad = og + inverse * (e - spread_mean - unit * along)
    xgrad_ref[...] = xgrad
    agrad = xgrad.astype(bf16)
    agrad_ref[...] = agrad
    sums_ref[...] = jnp.concatenate(
        [
            jnp.sum(grad * unit, axis=0, keepdims=True),
            jnp.sum(grad, axis=0, keepdims=True),
            jnp.sum(agrad.astype(f32), axis=0, keepdims=True),
            jnp.sum(og, axis=0, keepdims=True),
            jnp.zeros((4, og.shape[1]), f32),
        ],
        axis=0,
    )
    for index in range(4):
        back = dot(agrad, wos[index][...], NT).astype(bf16)
        send_ref[index] = dot(perm, back, NN).astype(bf16)


def down_grad_kernel(act_ref, og_ref, send_ref, keep_ref):
    value = dot(act_ref[0], og_ref[...], TN).astype(bf16)
    step = pl.program_id(0)

    @pl.when(step < 2)
    def _():
        send_ref[0] = value

    @pl.when(step >= 2)
    def _():
        keep_ref[0] = value


def up_grad_kernel(normed_ref, hid_ref, attu_ref, agrad_ref, send_ref, keep_ref):
    one = dot(normed_ref[...], hid_ref[0], TN).astype(bf16)
    two = dot(attu_ref[0], agrad_ref[...], TN).astype(bf16)
    rows = one.shape[0]
    step = pl.program_id(0)

    @pl.when(step < 2)
    def _():
        send_ref[0, 0:rows, :] = one
        send_ref[0, rows:, :] = two

    @pl.when(step >= 2)
    def _():
        keep_ref[0, 0:rows, :] = one
        keep_ref[0, rows:, :] = two


def gather_grad_kernel(counts_ref, b0_ref, b1_ref, b2_ref, b3_ref, att_ref, out_ref, sorted_ref):
    blocks = (b0_ref, b1_ref, b2_ref, b3_ref)
    rows, width = b0_ref.shape
    group = 4 * rows
    long = 2 * group // 3
    heads = width // HEAD
    counts = [counts_ref[i] for i in range(4)]
    sorted_ref[...] = jnp.zeros(sorted_ref.shape, sorted_ref.dtype)
    for index, ref in enumerate(blocks):

        def place(tile, _, index=index, ref=ref):
            to_group(
                ref[aligned(tile, TILE), :], sorted_ref,
                tile_moves(counts, rows, long, index, tile), slice(0, width),
            )
            return 0

        lax.fori_loop(0, rows // TILE, place, 0)
    lane = iota((group, 128), 1)
    for head in range(heads):
        first = head // 2 * 128
        grad = sorted_ref[:, first : first + 128].astype(f32)
        value = att_ref[:, first : first + 128].astype(f32)
        inside = (lane >= (head % 2) * HEAD) & (lane < (head % 2 + 1) * HEAD)
        less = -jnp.sum(jnp.where(inside, grad * value, 0.0), axis=1, keepdims=True)
        if head % 2:
            grad = pltpu.roll(grad, HEAD, 1)
        one = less.astype(bf16).astype(f32)
        two = less - one
        extra = jnp.where(lane == HEAD, one, jnp.where(lane == HEAD + 1, two, 0.0))
        out_ref[head] = jnp.where(lane < HEAD, grad, extra).astype(bf16)


def attend_back_kernel(q_ref, k_ref, v_ref, g_ref, out_ref, dq_ref):
    group = q_ref.shape[1]
    long = 2 * group // 3
    block = 512
    lane = iota((block, 128), 1)

    def frame(low, high):
        count = (high - low) // block

        def key_step(kb, _):
            keys = pl.ds(pl.multiple_of(low + kb * block, block), block)
            key = k_ref[0, keys, :]
            value = v_ref[0, keys, :]

            def query_step(qb, carry):
                key_grad, value_grad = carry
                queries = pl.ds(pl.multiple_of(low + qb * block, block), block)
                query = q_ref[0, queries, :]
                grad = g_ref[0, queries, :]
                probs = jnp.exp2(dot(key, query, NT))
                score_grad = (probs * dot(value, grad, NT)).astype(bf16)
                value_grad = value_grad + dot(probs.astype(bf16), grad, NN)
                key_grad = key_grad + dot(score_grad, query, NN)
                dq_ref[queries, :] += dot(score_grad, key, TN)
                return key_grad, value_grad

            empty = jnp.zeros((block, 128), f32)
            key_grad, value_grad = lax.fori_loop(0, count, query_step, (empty, empty))
            key_grad = jnp.where(lane < HEAD, key_grad * LN2, 0.0)
            out_ref[keys, 0:128] = pltpu.roll(key_grad, HEAD, 1).astype(bf16)
            out_ref[keys, 128:256] = jnp.where(lane < HEAD, value_grad, 0.0).astype(bf16)
            return 0

        lax.fori_loop(0, count, key_step, 0)

    dq_ref[...] = jnp.zeros(dq_ref.shape, f32)
    frame(0, long)
    frame(long, group)
    wide = iota((group, 128), 1)
    query_grad = jnp.where(wide < HEAD, dq_ref[...] * (1.0 / math.sqrt(HEAD)), 0.0)
    out_ref[:, 0:128] = (query_grad + out_ref[:, 0:128].astype(f32)).astype(bf16)


def project_back_kernel(counts_ref, h0_ref, h1_ref, h2_ref, weight_ref, local_ref, back_ref, acc_ref):
    heads = (h0_ref, h1_ref, h2_ref)
    rows = local_ref.shape[1]
    group = 4 * rows
    long = 2 * group // 3
    counts = [counts_ref[i] for i in range(4)]
    for index in (3, 1, 2, 0):

        def step(tile, _, index=index):
            moves = tile_moves(counts, rows, long, index, tile)
            here = aligned(tile, TILE)
            total = None
            for head, ref in enumerate(heads):
                from_group(ref, acc_ref, moves)
                local = acc_ref[...].astype(bf16)
                local_ref[index, here, head * 256 : (head + 1) * 256] = local
                part = dot(local, weight_ref[:, head * 256 : (head + 1) * 256], NT)
                total = part if total is None else total + part
            back_ref[index, here, :] = total.astype(bf16)
            return 0

        lax.fori_loop(0, rows // TILE, step, 0)


def project_grad_kernel(x0_ref, x1_ref, x2_ref, x3_ref, local_ref, out_ref, sums_ref):
    rows = local_ref.shape[1]
    total, sums = None, None
    for index, ref in enumerate((x0_ref, x1_ref, x2_ref, x3_ref)):
        part = dot(ref[0:rows, :], local_ref[index], TN)
        total = part if total is None else total + part
        one = jnp.sum(local_ref[index].astype(f32), axis=0, keepdims=True)
        sums = one if sums is None else sums + one
    out_ref[...] = total.astype(bf16)
    sums_ref[...] = jnp.broadcast_to(sums, sums_ref.shape)


def last_kernel(
    tok_ref, frame_ref, lead_ref, table_ref, gain_ref, perm_ref, mine_ref, other_ref, xgrad_ref, out_ref, sums_ref,
):
    values, hot = rows_with_lead(tok_ref, frame_ref, lead_ref, table_ref)
    unit, inverse = norm_stats(values)
    local = (mine_ref[...].astype(f32) + other_ref[...].astype(f32)).astype(bf16)
    grad = dot(perm_ref[...], local, TN)
    e = grad * gain_ref[...]
    mean_e = jnp.mean(e, axis=-1, keepdims=True)
    along = jnp.mean(e * unit, axis=-1, keepdims=True)
    out = xgrad_ref[...] + inverse * (e - mean_e - unit * along)
    out_ref[...] = out
    leads = table_ref.shape[0]
    one = out.astype(bf16)
    rest = out - one.astype(f32)
    two = rest.astype(bf16)
    three = (rest - two.astype(f32)).astype(bf16)
    sums_ref[0:leads, :] = dot(hot, one, NN) + dot(hot, two, NN) + dot(hot, three, NN)
    sums_ref[leads : leads + 8, :] = jnp.concatenate(
        [
            jnp.sum(grad * unit, axis=0, keepdims=True),
            jnp.sum(grad, axis=0, keepdims=True),
            jnp.zeros((6, grad.shape[1]), f32),
        ],
        axis=0,
    )


def bits_of(size):
    bits = []
    step = 1
    while step < size:
        bits.append(step)
        step *= 2
    return bits


def swap(value, axis, size, bit):
    return lax.ppermute(value, axis, [(i, i ^ bit) for i in range(size)])


def add_low(left, right):
    return (left.astype(f32) + right.astype(f32)).astype(bf16)


def sum_over_tp(send, keep):
    got = lax.ppermute(send, "tp", CORE)
    other = add_low(keep[1], got[1])
    far = lax.ppermute(other, "tp", NEXT)
    return add_low(add_low(keep[0], got[0]), far)


def sum_over_rows(value, size):
    me = lax.axis_index("rows")
    bits = bits_of(size)
    for bit in bits:
        half = value.shape[0] // 2
        high = (me // bit) % 2
        away = lax.dynamic_slice_in_dim(value, (1 - high) * half, half, 0)
        here = lax.dynamic_slice_in_dim(value, high * half, half, 0)
        value = add_low(here, swap(away, "rows", size, bit))
    for bit in reversed(bits):
        half = value.shape[0]
        high = (me // bit) % 2
        got = swap(value, "rows", size, bit)
        value = jnp.where(
            high == 1, jnp.concatenate([got, value], 0), jnp.concatenate([value, got], 0)
        )
    return value


def sum_everywhere(value, size):
    for pairs in (CORE, NEXT):
        value = value + lax.ppermute(value, "tp", pairs)
    for bit in bits_of(size):
        value = value + swap(value, "rows", size, bit)
    return value


def on_device(
    rows_size,
    tokens, frame_id, lead_index, lead_embed, ln1_gain, ln1_bias, qkv_weight, qv_bias,
    out_weight, out_bias, ln2_gain, ln2_bias, up_weight, up_bias, down_weight, down_bias, out_grad,
):
    rows, width_all = tokens.shape
    width = qkv_weight.shape[2]
    heads = width // HEAD
    hidden = up_weight.shape[1]
    leads = lead_embed.shape[0]
    group = 4 * rows
    long = 2 * group // 3
    pairs = long * long + (group - long) * (group - long)
    frames_here = lead_index.shape[0]
    frame = (frame_id - lax.axis_index("rows") * frames_here).reshape(1, rows)
    gain_one = ln1_gain.astype(f32).reshape(1, width_all)
    shift_one = ln1_bias.astype(f32).reshape(1, width_all)

    mine, perm = call(
        pre_kernel,
        (shape_of((rows + PAD, width_all), bf16), shape_of((rows, rows), bf16)),
        [VMEM, VMEM, SMEM, VMEM, VMEM, VMEM], (VMEM, VMEM), "pre",
        4 * rows * rows * width_all, 4 * rows * width_all * 2,
    )(tokens, frame, lead_index, lead_embed, gain_one, shift_one)

    near = lax.ppermute(mine, "tp", CORE)
    far = lax.ppermute(mine, "tp", NEXT)
    across = lax.ppermute(far, "tp", CORE)
    parts = (mine, near, far, across)

    up_bias_row = jnp.broadcast_to(up_bias.reshape(1, hidden), (PAD, hidden))

    def weight_set(value):
        near_w = lax.ppermute(value, "tp", CORE)
        far_w = lax.ppermute(value, "tp", NEXT)
        across_w = lax.ppermute(far_w, "tp", CORE)
        return (value, near_w, far_w, across_w)

    outs_w = weight_set(out_weight)
    ups_w = weight_set(up_weight)
    ubs_w = weight_set(up_bias_row)
    downs_w = weight_set(down_weight)

    weight_qkv = jnp.concatenate([qkv_weight[0], qkv_weight[1], qkv_weight[2]], axis=1)
    zero = jnp.zeros((width,), f32)
    bias_qkv = jnp.concatenate([qv_bias[0].astype(f32), zero, qv_bias[1].astype(f32)]).reshape(1, 3 * width)
    scale_qkv = jnp.concatenate(
        [jnp.full((width,), LOG2E / math.sqrt(HEAD), f32), jnp.ones((2 * width,), f32)]
    ).reshape(1, 3 * width)
    headed = qkv_weight.reshape(3, width_all, heads, HEAD).transpose(1, 2, 0, 3)
    weight_heads = jnp.pad(headed, ((0, 0), (0, 0), (0, 1), (0, 0))).reshape(width_all, heads * 4 * HEAD)

    wide = (heads + 1) // 2 * 128
    att, attended, q_all, k_all, v_all, counts = call(
        attend_kernel,
        (
            shape_of((group, wide), bf16),
            shape_of((4, rows, width), bf16),
            shape_of((heads, group, 128), bf16),
            shape_of((heads, group, 128), bf16),
            shape_of((heads, group, 128), bf16),
            shape_of((8,), i32),
        ),
        whole_specs(7), (VMEM,) * 5 + (SMEM,), "attend",
        4 * pairs * 256 * heads, 20 * group * width,
        scratch=[pltpu.VMEM((group, 3 * width), bf16), pltpu.VMEM((TILE, wide), f32)],
    )(*parts, weight_qkv, bias_qkv, scale_qkv)

    got = [attended[0]] + [
        lax.ppermute(attended[i], "tp", ring) for i, ring in ((1, CORE), (2, NEXT), (3, DIAG))
    ]

    vectors = jnp.concatenate(
        [item.astype(f32).reshape(1, width_all) for item in (ln2_gain, ln2_bias, out_bias, down_bias)]
        + [jnp.zeros((4, width_all), f32)]
    )
    layer_out, xgrad, agrad, normed_two, act, hid, attu, back_send, sums_two, up_b = call(
        middle_kernel,
        (
            shape_of((rows, width_all), bf16),
            shape_of((rows, width_all), f32),
            shape_of((rows, width_all), bf16),
            shape_of((rows, width_all), bf16),
            shape_of((4, rows, hidden), bf16),
            shape_of((4, rows, hidden), bf16),
            shape_of((4, rows, width), bf16),
            shape_of((4, rows, width), bf16),
            shape_of((8, width_all), f32),
            shape_of((4, 8, hidden), f32),
        ),
        [VMEM, VMEM, SMEM] + whole_specs(24), (VMEM,) * 10, "middle",
        32 * rows * width_all * hidden, 40 * rows * width_all,
        scratch=[pltpu.VMEM((rows, width_all), f32), pltpu.VMEM((rows, width_all), f32)],
    )(
        tokens, frame, lead_index, lead_embed, perm, *got, *outs_w, *ups_w, *ubs_w, *downs_w, vectors, out_grad,
    )

    got_grad = [back_send[0]] + [
        lax.ppermute(back_send[i], "tp", ring) for i, ring in ((1, CORE), (2, NEXT), (3, DIAG))
    ]

    def block_of(step):
        return jnp.where(step < 2, 2 * step + 1, 2 * step - 4)

    def share_specs(shape):
        return (
            pl.BlockSpec((1,) + shape, lambda s: (jnp.minimum(s, 1), 0, 0)),
            pl.BlockSpec((1,) + shape, lambda s: (jnp.maximum(s - 2, 0), 0, 0)),
        )

    def full(shape):
        return pl.BlockSpec(shape, lambda s: (0,) * len(shape))

    def picked(shape):
        return pl.BlockSpec((1,) + shape, lambda s: (block_of(s), 0, 0))

    down_send, down_keep = call(
        down_grad_kernel,
        (shape_of((2, hidden, width_all), bf16),) * 2,
        [picked((rows, hidden)), full((rows, width_all))],
        share_specs((hidden, width_all)), "down_grad",
        8 * rows * hidden * width_all, 16 * rows * width_all, grid=(4,),
    )(act, out_grad)
    tall = width_all + width
    up_send, up_keep = call(
        up_grad_kernel,
        (shape_of((2, tall, hidden), bf16),) * 2,
        [full((rows, width_all)), picked((rows, hidden)), picked((rows, width)), full((rows, width_all))],
        share_specs((tall, hidden)), "up_grad",
        10 * rows * hidden * width_all, 20 * rows * width_all, grid=(4,),
    )(normed_two, hid, attu, agrad)

    down_sum = sum_over_rows(sum_over_tp(down_send, down_keep), rows_size)
    up_sum = sum_over_rows(sum_over_tp(up_send, up_keep), rows_size)

    grad_all = call(
        gather_grad_kernel,
        shape_of((heads, group, 128), bf16),
        [SMEM] + whole_specs(5), VMEM, "gather_grad",
        2 * 4 * TILE * group * 256, 6 * group * 256,
        scratch=[pltpu.VMEM((group, wide), bf16)],
    )(counts, *got_grad, att)

    head_grads = []
    for head in range(heads):
        spec = pl.BlockSpec((1, group, 128), lambda s, head=head: (head, 0, 0))
        head_grads.append(
            call(
                attend_back_kernel,
                shape_of((group, 256), bf16),
                [spec] * 4, pl.BlockSpec((group, 256), lambda s: (0, 0)), "attend_back",
                10 * pairs * 256, 12 * group * 128,
                scratch=[pltpu.VMEM((group, 128), f32)], grid=(1,),
            )(q_all, k_all, v_all, grad_all)
        )

    local, back = call(
        project_back_kernel,
        (shape_of((4, rows, heads * 256), bf16), shape_of((4, rows, width_all), bf16)),
        [SMEM] + whole_specs(4), (VMEM, VMEM), "project_back",
        4 * group * width_all * 256 * heads, 8 * group * width_all,
        scratch=[pltpu.VMEM((TILE, 256), f32)],
    )(counts, *head_grads, weight_heads)

    over_core = lax.ppermute(back[3], "tp", CORE)
    over_core_two = lax.ppermute(back[1], "tp", CORE)
    from_far = lax.ppermute(add_low(back[2], over_core), "tp", NEXT)
    here = add_low(back[0], over_core_two)

    qkv_grad, qkv_sums = call(
        project_grad_kernel,
        (shape_of((width_all, heads * 256), bf16), shape_of((8, heads * 256), f32)),
        whole_specs(5), (VMEM, VMEM), "project_grad",
        2 * group * width_all * 256 * heads, 4 * group * width_all,
    )(*parts, local)

    tokens_grad, sums_one = call(
        last_kernel,
        (shape_of((rows, width_all), f32), shape_of((leads + 8, width_all), f32)),
        [VMEM, VMEM, SMEM] + whole_specs(6), (VMEM, VMEM), "last",
        2 * rows * rows * width_all, 16 * rows * width_all,
    )(tokens, frame, lead_index, lead_embed, gain_one, perm, here, from_far, xgrad)

    qkv_sum = sum_over_rows(qkv_grad, rows_size)
    small = jnp.concatenate([sums_one, sums_two], axis=0)
    small = sum_everywhere(small, rows_size)

    up_b = up_b[:, 0:1, :]
    near_b = lax.ppermute(jnp.stack([up_b[1], up_b[3]]), "tp", CORE)
    far_b = lax.ppermute(up_b[2] + near_b[1], "tp", NEXT)
    up_b_here = up_b[0] + near_b[0] + far_b
    split_sums = jnp.concatenate([up_b_here, qkv_sums[0:1]], axis=1)
    for bit in bits_of(rows_size):
        split_sums = split_sums + swap(split_sums, "rows", rows_size, bit)

    up_b_sum = split_sums[0, 0:hidden]
    qkv_bias = split_sums[0, hidden:].reshape(heads, 4, HEAD)
    qv_sum = jnp.stack([qkv_bias[:, 0].reshape(width), qkv_bias[:, 2].reshape(width)])
    qkv_out = (
        qkv_sum.reshape(width_all, heads, 4, HEAD)[:, :, 0:3]
        .transpose(2, 0, 1, 3)
        .reshape(3, width_all, width)
        .astype(f32)
    )
    return (
        layer_out,
        tokens_grad,
        small[0:leads],
        small[leads],
        small[leads + 1],
        qkv_out,
        qv_sum,
        up_sum[width_all:].astype(f32),
        small[leads + 10],
        small[leads + 8],
        small[leads + 9],
        up_sum[0:width_all].astype(f32),
        up_b_sum,
        down_sum.astype(f32),
        small[leads + 11],
    )


def solution(mesh):
    rows_size = mesh.shape["rows"]
    split = P(("rows", "tp"), None)
    placed = (
        split, P(("rows", "tp")), P("rows"), P(), P(), P(), P(None, None, "tp"), P(None, "tp"),
        P("tp", None), P(), P(), P(), P(None, "tp"), P("tp"), P("tp", None), P(), split,
    )
    return jax.shard_map(
        functools.partial(on_device, rows_size),
        mesh=mesh,
        in_specs=placed,
        out_specs=(
            split, split, P(), P(), P(), P(None, None, "tp"), P(None, "tp"), P("tp", None), P(), P(), P(),
            P(None, "tp"), P("tp"), P("tp", None), P(),
        ),
        check_vma=False,
    )
```

time: 1370 us -> 595 us (0.43)
  matrix products: 388 us -> 0 us
  waiting for transfers between devices: 633 us -> 248 us
  Pallas kernels: 0 us -> 237 us
  other arithmetic: 162 us -> 25.1 us
  blocking collectives: 71.2 us -> 0 us
  local copies, waits for them, and re-layouts: 84 us -> 24.8 us
  starting transfers between devices: 0.58 us -> 53.4 us
    dot_general x62 -> x0, matrix products: 388 us -> none  [the longest x6 86 us: back_step(): jnp.einsum('qhd,khd->hqk', upper_block, value_heads, preferred_element_ty...]
    psum x2 -> x0, waiting for transfers between devices: 292 us -> none  [the longest x1 165 us: on_device(): lax.psum((qkv_part, qv_part, out_weight_part, up_weight_part, up_bias_par...]
    ppermute x0 -> x56, waiting for transfers between devices: none -> 248 us  [the longest x24 76.9 us: swap(): return lax.ppermute(value, axis, [(i, i ^ bit) for i in range(size)])]
    pallas_call x0 -> x12, Pallas kernels: none -> 237 us  [the longest x3 66.2 us: on_device(): call(attend_back_kernel, shape_of((group, 256), bf16), [spec] * 4, pl.Blo...]
    reduce_scatter x4 -> x0, waiting for transfers between devices: 203 us -> none  [the longest x1 75.9 us: on_device(): lax.psum_scatter(jnp.dot(attended, out_weight, preferred_element_type=f32...]
    all_gather x4 -> x0, waiting for transfers between devices: 138 us -> none  [the longest x1 37.5 us: on_device(): attn_grad_all = lax.all_gather(attn_grad, 'tp', axis=0, tiled=True)]
    convert_element_type x17 -> x19, other arithmetic: 92.7 us -> 16.6 us  [the longest x14 11.1 us: add_low(): return (left.astype(f32) + right.astype(f32)).astype(bf16)]
    psum x2 -> x0, blocking collectives: 65 us -> none  [the longest x1 41.5 us: on_device(): lax.psum((lead_part, gain_one_part, shift_one_part, gain_two_part, shift_...]
  transfers between devices with their start and end apart: 10 -> 56, of which waited for: 10 -> 30; matrix products, arithmetic and copies ran while one was open for 5% -> 7% of each run, Pallas kernels for 0% -> 32%
where the time goes in v1:
time: 595 us; the launch traced here: 590 us
  waiting for transfers between devices  248 us (42%)
  Pallas kernels  237 us (40%)
  starting transfers between devices  53.4 us (9%)
  other arithmetic  25.1 us (4%)
  local copies, waits for them, and re-layouts  24.8 us (4%)
    ppermute x24, waiting for transfers between devices, swap(): return lax.ppermute(value, axis, [(i, i ^ bit) for i in range(size)])  76.9 us
    pallas_call x3, Pallas kernels, on_device(): call(attend_back_kernel, shape_of((group, 256), bf16), [spec] * 4, pl.Blo...  66.2 us
    ppermute x4, waiting for transfers between devices, weight_set(): far_w = lax.ppermute(value, 'tp', NEXT)  57.8 us
    pallas_call x1, Pallas kernels, on_device(): call(attend_kernel, (shape_of((group, wide), bf16), shape_of((4, rows, wi...  53.8 us
    ppermute x2, waiting for transfers between devices, sum_over_tp(): far = lax.ppermute(other, 'tp', NEXT)  37.9 us
    pallas_call x1, Pallas kernels, on_device(): call(middle_kernel, (shape_of((rows, width_all), bf16), shape_of((rows, w...  37.7 us
    ppermute x24, starting transfers between devices, swap(): return lax.ppermute(value, axis, [(i, i ^ bit) for i in range(size)])  34.9 us
    pallas_call x1, Pallas kernels, on_device(): call(project_back_kernel, (shape_of((4, rows, heads * 256), bf16), shape_...  29.2 us
  transfers between devices with their start and end apart: 56, of which 30 were waited for; matrix products, arithmetic and copies ran while one was open for 7% of the time, Pallas kernels for 32%

profile of v1, /device:TPU:0, one launch (start us, length us, event | category | flops | bytes accessed | tf_op | source)
XLA Modules:
  0.0 590.5 jit_solution(12586085437570545481)
XLA Ops:
  4.5 5.1 pre.1
  9.5 3.0 collective-permute-start.1
  12.5 26.8 %collective-permute-done.1.x2_ref = bf16[784,768]{1,0:T(8,128)(2,1)} collective-permute-done((bf16[784,768]{1,0:T(8,128)(2,1)}, bf16[784,768]{1,0:T(8,128)(2,1)}, u32[]{:S(2)}, u32[]{:S(2)}) %collective-permute-start.1) | collective-permute-done | bytes 1204256 | tf_op jit(solution)/shard_map/ppermute | solution.py:580
  39.3 1.7 collective-permute-start.10
  41.4 1.8 collective-permute-start.13
  43.2 50.5 %collective-permute-done.13.ub2_ref = bf16[16,768]{1,0:T(8,128)(2,1)S(1)} collective-permute-done((bf16[16,768]{1,0:T(8,128)(2,1)S(1)}, bf16[16,768]{1,0:T(8,128)(2,1)S(1)}, u32[]{:S(2)}, u32[]{:S(2)}) %collective-permute-start.13) | collective-permute-done | bytes 24608 | tf_op jit(solution)/shard_map/ppermute | solution.py:588
  96.1 1.7 collective-permute-start.7
  97.9 7.3 %collective-permute-done.7.wo2_ref = bf16[192,768]{1,0:T(8,128)(2,1)S(1)} collective-permute-done((bf16[192,768]{1,0:T(8,128)(2,1)S(1)}, bf16[192,768]{1,0:T(8,128)(2,1)S(1)}, u32[]{:S(2)}, u32[]{:S(2)}) %collective-permute-start.7) | collective-permute-done | bytes 294944 | tf_op jit(solution)/shard_map/ppermute | solution.py:588
  109.3 53.8 %attend.1 = (bf16[3072,256]{1,0:T(8,128)(2,1)}, bf16[4,768,192]{2,1,0:T(8,128)(2,1)}, bf16[3,3072,128]{2,1,0:T(8,128)(2,1)}, bf16[3,3072,128]{2,1,0:T(8,128)(2,1...) custom-call(bf16[784,768]{1,0:T(8,128)(2,1)} %get-tuple-element.44.x0_ref, bf16[784,768]{1,0:T(8,128)(2,1)} %collective-permute-done.x1_ref, ...), custom_call_target="tpu_custom_call" | custom-call | flops 16106127360 | bytes 11796480 | tf_op jit(solution)/shard_map/attend/pallas_call | solution.py:607
  163.1 2.2 slice_bitcast_fusion.6
  165.5 1.7 collective-permute-start.4
  169.9 7.6 %collective-permute-done.4.at2_ref = bf16[768,192]{1,0:T(8,128)(2,1)} collective-permute-done((bf16[768,192]{1,0:T(8,128)(2,1)S(1)}, bf16[768,192]{1,0:T(8,128)(2,1)}, u32[]{:S(2)}, u32[]{:S(2)}) %collective-permute-start.4) | collective-permute-done | bytes 294944 | tf_op jit(solution)/shard_map/ppermute | solution.py:623
  177.5 7.5 %collective-permute-done.5.at3_ref = bf16[768,192]{1,0:T(8,128)(2,1)} collective-permute-done((bf16[768,192]{1,0:T(8,128)(2,1)S(1)}, bf16[768,192]{1,0:T(8,128)(2,1)}, u32[]{:S(2)}, u32[]{:S(2)}) %collective-permute-start.5) | collective-permute-done | bytes 294944 | tf_op jit(solution)/shard_map/ppermute | solution.py:623
  185.0 37.7 %middle.1 = (bf16[768,768]{1,0:T(8,128)(2,1)}, f32[768,768]{1,0:T(8,128)}, bf16[768,768]{1,0:T(8,128)(2,1)}, bf16[768,768]{1,0:T(8,128)(2,1)}, bf16[4,768,768]{2...) custom-call(bf16[768,768]{1,0:T(8,128)(2,1)} %tok_ref.5, ...), custom_call_target="tpu_custom_call" | custom-call | flops 14495514624 | bytes 23592960 | tf_op jit(solution)/shard_map/middle/pallas_call | solution.py:630
  222.7 8.5 %down_grad.1 = (bf16[2,768,768]{2,1,0:T(8,128)(2,1)}, bf16[2,768,768]{2,1,0:T(8,128)(2,1)}) custom-call(bf16[4,768,768]{2,1,0:T(8,128)(2,1)} %get-tuple-element.68.act_ref, bf16[768,768]{1,0:T(8,128)(2,1)} %og_ref.3), custom_call_target="tpu_custom_call" | custom-call | flops 3623878656 | bytes 9437184 | tf_op jit(solution)/shard_map/down_grad/pallas_call | solution.py:670
  231.6 10.2 %up_grad.1 = (bf16[2,960,768]{2,1,0:T(8,128)(2,1)}, bf16[2,960,768]{2,1,0:T(8,128)(2,1)}) custom-call(bf16[768,768]{1,0:T(8,128)(2,1)} %get-tuple-element.62.normed_ref, bf16[4,768,768]{2,1,0:T(8,128)(2,1)} %get-tuple-element.63.hid_ref, bf16[4,768,192]{2,1,0:T(8,128)(2,1)} %get-tuple-element.64.attu_ref, bf16[768,768]{1,0:T(8,128)(2,1)} %get-tuple-element.65.agrad_ref), custom_call_target="tpu_custom_call" | custom-call | flops 4529848320 | bytes 11796480 | tf_op jit(solution)/shard_map/up_grad/pallas_call | solution.py:678
  242.0 2.2 slice_bitcast_fusion.2
  244.5 1.7 collective-permute-start.19
  247.9 8.5 %collective-permute-done.19.b2_ref = bf16[768,192]{1,0:T(8,128)(2,1)S(1)} collective-permute-done((bf16[768,192]{1,0:T(8,128)(2,1)S(1)}, bf16[768,192]{1,0:T(8,128)(2,1)S(1)}, u32[]{:S(2)}, u32[]{:S(2)}) %collective-permute-start.19) | collective-permute-done | bytes 294944 | tf_op jit(solution)/shard_map/ppermute | solution.py:652
  256.4 7.0 %collective-permute-done.20.b3_ref = bf16[768,192]{1,0:T(8,128)(2,1)S(1)} collective-permute-done((bf16[768,192]{1,0:T(8,128)(2,1)S(1)}, bf16[768,192]{1,0:T(8,128)(2,1)S(1)}, u32[]{:S(2)}, u32[]{:S(2)}) %collective-permute-start.20) | collective-permute-done | bytes 294944 | tf_op jit(solution)/shard_map/ppermute | solution.py:652
  264.2 10.2 %gather_grad.1.g_ref = bf16[3,3072,128]{2,1,0:T(8,128)(2,1)} custom-call(s32[8]{0:T(128)} %get-tuple-element.47.counts_ref, bf16[768,192]{1,0:T(8,128)(2,1)} %get-tuple-element.88.b0_ref, bf16[768,192]{1,0:T(8,128)(2,1)} %copy-done.15, bf16[768,192]{1,0:T(8,128)(2,1)} %copy-done.16, bf16[768,192]{1,0:T(8,128)(2,1)} %copy-done.17, ...), custom_call_target="tpu_custom_call" | custom-call | flops 1610612736 | bytes 4718592 | tf_op jit(solution)/shard_map/gather_grad/pallas_call | solution.py:689
  274.4 22.2 %attend_back.5.h2_ref = bf16[3072,256]{1,0:T(8,128)(2,1)} custom-call(bf16[3,3072,128]{2,1,0:T(8,128)(2,1)} %get-tuple-element.48.q_ref, bf16[3,3072,128]{2,1,0:T(8,128)(2,1)} %get-tuple-element.49.k_ref, bf16[3,3072,128]{2,1,0:T(8,128)(2,1)} %get-tuple-element.50.v_ref, bf16[3,3072,128]{2,1,0:T(8,128)(2,1)} %gather_grad.1.g_ref), custom_call_target="tpu_custom_call" | custom-call | flops 13421772800 | bytes 4718592 | tf_op jit(solution)/shard_map/attend_back/pallas_call | solution.py:701
  296.6 22.0 %attend_back.4.h1_ref = bf16[3072,256]{1,0:T(8,128)(2,1)} custom-call(bf16[3,3072,128]{2,1,0:T(8,128)(2,1)} %get-tuple-element.48.q_ref, bf16[3,3072,128]{2,1,0:T(8,128)(2,1)} %get-tuple-element.49.k_ref, bf16[3,3072,128]{2,1,0:T(8,128)(2,1)} %get-tuple-element.50.v_ref, bf16[3,3072,128]{2,1,0:T(8,128)(2,1)} %gather_grad.1.g_ref), custom_call_target="tpu_custom_call" | custom-call | flops 13421772800 | bytes 4718592 | tf_op jit(solution)/shard_map/attend_back/pallas_call | solution.py:701
  318.6 22.0 %attend_back.3.h0_ref = bf16[3072,256]{1,0:T(8,128)(2,1)} custom-call(bf16[3,3072,128]{2,1,0:T(8,128)(2,1)} %get-tuple-element.48.q_ref, bf16[3,3072,128]{2,1,0:T(8,128)(2,1)} %get-tuple-element.49.k_ref, bf16[3,3072,128]{2,1,0:T(8,128)(2,1)} %get-tuple-element.50.v_ref, bf16[3,3072,128]{2,1,0:T(8,128)(2,1)} %gather_grad.1.g_ref), custom_call_target="tpu_custom_call" | custom-call | flops 13421772800 | bytes 4718592 | tf_op jit(solution)/shard_map/attend_back/pallas_call | solution.py:701
  340.6 29.2 %project_back.1 = (bf16[4,768,768]{2,1,0:T(8,128)(2,1)}, bf16[4,768,768]{2,1,0:T(8,128)(2,1)}) custom-call(s32[8]{0:T(128)} %get-tuple-element.47.counts_ref, bf16[3072,256]{1,0:T(8,128)(2,1)} %attend_back.3.h0_ref, bf16[3072,256]{1,0:T(8,128)(2,1)} %attend_back.4.h1_ref, bf16[3072,256]{1,0:T(8,128)(2,1)} %attend_back.5.h2_ref, bf16[768,768]{1,0:T(8,128)(2,1)} %copy.49.weight_ref), custom_call_target="tpu_custom_call" | custom-call | flops 7247757312 | bytes 18874368 | tf_op jit(solution)/shard_map/project_back/pallas_call | solution.py:710
  369.8 8.7 %project_grad.1 = (bf16[768,768]{1,0:T(8,128)(2,1)}, f32[8,768]{1,0:T(8,128)}) custom-call(bf16[784,768]{1,0:T(8,128)(2,1)} %get-tuple-element.44.x0_ref, bf16[784,768]{1,0:T(8,128)(2,1)} %collective-permute-done.x1_ref, bf16[784,768]{1,0:T(8,128)(2,1)} %collective-permute-done.1.x2_ref, bf16[784,768]{1,0:T(8,128)(2,1)} %collective-permute-done.2.x3_ref, ...), custom_call_target="tpu_custom_call" | custom-call | flops 3623878656 | bytes 9437184 | tf_op jit(solution)/shard_map/project_grad/pallas_call | solution.py:723
  379.6 3.0 collective-permute-start.29
  383.3 3.6 collective-permute-done.36
  388.4 1.9 slice_bitcast_fusion
  390.9 5.8 collective-permute-done.29
  399.3 1.8 fusion.7
  404.7 2.3 collective-permute-done.30
  407.2 1.9 collective-permute-start.31
  409.1 7.1 %collective-permute-done.31 = bf16[96,768]{1,0:T(8,128)(2,1)S(1)} collective-permute-done((bf16[96,768]{1,0:T(8,128)(2,1)S(1)}, bf16[96,768]{1,0:T(8,128)(2,1)S(1)}, u32[]{:S(2)}, u32[]{:S(2)}) %collective-permute-start.31) | collective-permute-done | bytes 147488 | tf_op jit(solution)/shard_map/ppermute | solution.py:513
  417.6 2.1 fusion.2
  420.1 9.8 %collective-permute-done.49 = bf16[768,768]{1,0:T(8,128)(2,1)S(1)} collective-permute-done((bf16[768,768]{1,0:T(8,128)(2,1)S(1)}, bf16[768,768]{1,0:T(8,128)(2,1)S(1)}, u32[]{:S(2)}, u32[]{:S(2)}) %collective-permute-start.49) | collective-permute-done | bytes 1179680 | tf_op jit(solution)/shard_map/ppermute | solution.py:523
  430.0 1.9 fusion.1
  433.5 28.1 %collective-permute-done.41 = bf16[960,768]{1,0:T(8,128)(2,1)S(1)} collective-permute-done((bf16[960,768]{1,0:T(8,128)(2,1)S(1)}, bf16[960,768]{1,0:T(8,128)(2,1)S(1)}, u32[]{:S(2)}, u32[]{:S(2)}) %collective-permute-start.41) | collective-permute-done | bytes 1474592 | tf_op jit(solution)/shard_map/ppermute | solution.py:523
  463.9 2.1 collective-permute-start.38
  465.9 1.6 collective-permute-done.38
  467.6 3.0 collective-permute-start.39
  470.5 1.7 collective-permute-done.39
  472.4 2.1 collective-permute-start.33
  474.5 10.4 %collective-permute-done.23.other_ref = bf16[768,768]{1,0:T(8,128)(2,1)} collective-permute-done((bf16[768,768]{1,0:T(8,128)(2,1)}, bf16[768,768]{1,0:T(8,128)(2,1)}, u32[]{:S(2)}, u32[]{:S(2)}) %collective-permute-start.23) | collective-permute-done | bytes 1179680 | tf_op jit(solution)/shard_map/ppermute | solution.py:720
  484.9 7.7 %last.1 = (f32[768,768]{1,0:T(8,128)}, f32[40,768]{1,0:T(8,128)}) custom-call(bf16[768,768]{1,0:T(8,128)(2,1)} %tok_ref.5, s32[1,768]{1,0:T(1,128)} %reshape.164.frame_ref, s32[2]{0:T(128)} %lead_ref.5, bf16[32,768]{1,0:T(8,128)(2,1)} %table_ref.5, f32[1,768]{1,0:T(1,128)} %reshape.181.gain_ref, bf16[768,768]{1,0:T(8,128)(2,1)} %get-tuple-element.43.perm_ref, ...), custom_call_target="tpu_custom_call" | custom-call | flops 905969664 | bytes 9437184 | tf_op jit(solution)/shard_map/last/pallas_call | solution.py:730
  493.9 1.8 collective-permute-start.51
  497.6 6.3 %collective-permute-done.51 = bf16[192,768]{1,0:T(8,128)(2,1)S(1)} collective-permute-done((bf16[192,768]{1,0:T(8,128)(2,1)S(1)}, bf16[192,768]{1,0:T(8,128)(2,1)S(1)}, u32[]{:S(2)}, u32[]{:S(2)}) %collective-permute-start.51) | collective-permute-done | bytes 294944 | tf_op jit(solution)/shard_map/ppermute | solution.py:513
  504.0 3.3 collective-permute-start.52
  507.3 5.4 collective-permute-done.43
  512.8 1.9 collective-permute-start.44
  515.9 10.8 %collective-permute-done.44 = bf16[120,768]{1,0:T(8,128)(2,1)S(1)} collective-permute-done((bf16[120,768]{1,0:T(8,128)(2,1)S(1)}, bf16[120,768]{1,0:T(8,128)(2,1)S(1)}, u32[]{:S(2)}, u32[]{:S(2)}) %collective-permute-start.44) | collective-permute-done | bytes 184352 | tf_op jit(solution)/shard_map/ppermute | solution.py:513
  527.0 6.4 %collective-permute-done.53 = bf16[96,768]{1,0:T(8,128)(2,1)S(1)} collective-permute-done((bf16[96,768]{1,0:T(8,128)(2,1)S(1)}, bf16[96,768]{1,0:T(8,128)(2,1)S(1)}, u32[]{:S(2)}, u32[]{:S(2)}) %collective-permute-start.53) | collective-permute-done | bytes 147488 | tf_op jit(solution)/shard_map/ppermute | solution.py:513
  533.5 3.5 collective-permute-done.45
  539.3 2.9 collective-permute-start.34
  545.8 3.7 collective-permute-done.46
  549.7 2.3 collective-permute-start.47
  553.0 6.9 %collective-permute-done.26 = f32[48,768]{1,0:T(8,128)S(1)} collective-permute-done((f32[48,768]{1,0:T(8,128)S(1)}, f32[48,768]{1,0:T(8,128)S(1)}, u32[]{:S(2)}, u32[]{:S(2)}) %collective-permute-start.26) | collective-permute-done | bytes 147488 | tf_op jit(solution)/shard_map/ppermute | solution.py:513
  563.2 3.4 collective-permute-done.27
  566.7 1.8 collective-permute-start.28
  570.0 4.4 collective-permute-done.28
  575.7 2.9 fusion.8
  578.5 7.5 %collective-permute-done.47 = bf16[480,768]{1,0:T(8,128)(2,1)} collective-permute-done((bf16[480,768]{1,0:T(8,128)(2,1)S(1)}, bf16[480,768]{1,0:T(8,128)(2,1)}, u32[]{:S(2)}, u32[]{:S(2)}) %collective-permute-start.47) | collective-permute-done | bytes 737312 | tf_op jit(solution)/shard_map/ppermute | solution.py:513
  586.0 1.9 maximum_select_fusion
  587.9 1.6 slice_convert_fusion
  (204 shorter events, 51.5 us)
Async XLA Ops:
  4.4 36.9 %copy-start.13 = (bf16[768]{0:T(1024)(128)(2,1)S(1)}, bf16[768]{0:T(1024)(128)(2,1)}, u32[]{:S(2)}) copy-start(bf16[768]{0:T(1024)(128)(2,1)} %param.30) | copy-start | bytes 4612
  4.4 91.7 %copy-start.18 = (bf16[192,768]{1,0:T(8,128)(2,1)S(1)}, bf16[192,768]{1,0:T(8,128)(2,1)}, u32[]{:S(2)}) copy-start(bf16[192,768]{1,0:T(8,128)(2,1)} %wo0_ref.1) | copy-start | bytes 884740
  4.5 93.4 %copy-start = (bf16[3,768,192]{1,2,0:T(8,128)(2,1)S(1)}, bf16[3,768,192]{1,2,0:T(8,128)(2,1)}, u32[]{:S(2)}) copy-start(bf16[3,768,192]{1,2,0:T(8,128)(2,1)} %param.23) | copy-start | bytes 2654212
  9.5 95.7 %copy-start.8 = (bf16[2,192]{1,0:T(2,128)(2,1)S(1)}, bf16[2,192]{1,0:T(2,128)(2,1)}, u32[]{:S(2)}) copy-start(bf16[2,192]{1,0:T(2,128)(2,1)} %param.24) | copy-start | bytes 2308
  9.5 29.8 %collective-permute-start.1 = (bf16[784,768]{1,0:T(8,128)(2,1)}, bf16[784,768]{1,0:T(8,128)(2,1)}, u32[]{:S(2)}, u32[]{:S(2)}) collective-permute-start(bf16[784,768]{1,0:T(8,128)(2,1)} %get-tuple-element.44.x0_ref), channel_id=1, source_target_pairs={{0,2},{2,0},{1,3},{3,1},{4,6},{6,4},{5,7},{7,5},{8,10},{10,8},{9,1... | collective-permute-start | bytes 3612680 | tf_op jit(solution)/shard_map/ppermute | solution.py:580
  12.5 96.3 %collective-permute-start = (bf16[784,768]{1,0:T(8,128)(2,1)}, bf16[784,768]{1,0:T(8,128)(2,1)}, u32[]{:S(2)}, u32[]{:S(2)}) collective-permute-start(bf16[784,768]{1,0:T(8,128)(2,1)} %get-tuple-element.44.x0_ref), channel_id=1, source_target_pairs={{0,1},{1,0},{2,3},{3,2},{4,5},{5,4},{6,7},{7,6},{8,9},{9,8},{10,11... | collective-permute-start | bytes 3612680 | tf_op jit(solution)/shard_map/ppermute | solution.py:579
  39.3 69.5 %collective-permute-start.2 = (bf16[784,768]{1,0:T(8,128)(2,1)}, bf16[784,768]{1,0:T(8,128)(2,1)}, u32[]{:S(2)}, u32[]{:S(2)}) collective-permute-start(bf16[784,768]{1,0:T(8,128)(2,1)} %collective-permute-done.1.x2_ref), channel_id=1, source_target_pairs={{0,1},{1,0},{2,3},{3,2},{4,5},{5,4},{6,7},{7,6},{8,9},{9,8},{10,11... | collective-permute-start | bytes 3612680 | tf_op jit(solution)/shard_map/ppermute | solution.py:581
  39.3 68.9 %collective-permute-start.10 = (bf16[768,768]{1,0:T(8,128)(2,1)}, bf16[768,768]{1,0:T(8,128)(2,1)}, u32[]{:S(2)}, u32[]{:S(2)}) collective-permute-start(bf16[768,768]{1,0:T(8,128)(2,1)} %up0_ref.1), channel_id=1, source_target_pairs={{0,2},{2,0},{1,3},{3,1},{4,6},{6,4},{5,7},{7,5},{8,10},{10,8},{9,1... | collective-permute-start | bytes 3538952 | tf_op jit(solution)/shard_map/ppermute | solution.py:588
  41.1 67.3 %collective-permute-start.16 = (bf16[768,768]{1,0:T(8,128)(2,1)}, bf16[768,768]{1,0:T(8,128)(2,1)}, u32[]{:S(2)}, u32[]{:S(2)}) collective-permute-start(bf16[768,768]{1,0:T(8,128)(2,1)} %dn0_ref.1), channel_id=1, source_target_pairs={{0,2},{2,0},{1,3},{3,1},{4,6},{6,4},{5,7},{7,5},{8,10},{10,8},{9,1... | collective-permute-start | bytes 3538952 | tf_op jit(solution)/shard_map/ppermute | solution.py:588
  41.3 64.2 %copy-start.7 = (bf16[16,768]{1,0:T(8,128)(2,1)}, bf16[16,768]{1,0:T(8,128)(2,1)S(1)}, u32[]{:S(2)}) copy-start(bf16[16,768]{1,0:T(8,128)(2,1)S(1)} %broadcast_in_dim.12.ub0_ref) | copy-start | bytes 73732
  41.4 52.4 %collective-permute-start.13 = (bf16[16,768]{1,0:T(8,128)(2,1)S(1)}, bf16[16,768]{1,0:T(8,128)(2,1)S(1)}, u32[]{:S(2)}, u32[]{:S(2)}) collective-permute-start(bf16[16,768]{1,0:T(8,128)(2,1)S(1)} %broadcast_in_dim.12.ub0_ref), channel_id=1, source_target_pairs={{0,2},{2,0},{1,3},{3,1},{4,6},{6,4},{5,7},{7,5},{8,10},{10,8},{9,1... | collective-permute-start | bytes 73736 | tf_op jit(solution)/shard_map/ppermute | solution.py:588
  93.7 1.2 collective-permute-start.12
  94.9 1.2 collective-permute-start.14
  96.1 9.1 %collective-permute-start.7 = (bf16[192,768]{1,0:T(8,128)(2,1)S(1)}, bf16[192,768]{1,0:T(8,128)(2,1)S(1)}, u32[]{:S(2)}, u32[]{:S(2)}) collective-permute-start(bf16[192,768]{1,0:T(8,128)(2,1)S(1)} %copy-done.18), channel_id=1, source_target_pairs={{0,2},{2,0},{1,3},{3,1},{4,6},{6,4},{5,7},{7,5},{8,10},{10,8},{9,1... | collective-permute-start | bytes 884744 | tf_op jit(solution)/shard_map/ppermute | solution.py:588
  105.2 2.6 collective-permute-start.6
  107.7 57.7 %collective-permute-start.15 = (bf16[768,768]{1,0:T(8,128)(2,1)}, bf16[768,768]{1,0:T(8,128)(2,1)S(1)}, u32[]{:S(2)}, u32[]{:S(2)}) collective-permute-start(bf16[768,768]{1,0:T(8,128)(2,1)} %dn0_ref.1), channel_id=1, source_target_pairs={{0,1},{1,0},{2,3},{3,2},{4,5},{5,4},{6,7},{7,6},{8,9},{9,8},{10,11... | collective-permute-start | bytes 3538952 | tf_op jit(solution)/shard_map/ppermute | solution.py:587
  108.2 59.0 %collective-permute-start.9 = (bf16[768,768]{1,0:T(8,128)(2,1)}, bf16[768,768]{1,0:T(8,128)(2,1)}, u32[]{:S(2)}, u32[]{:S(2)}) collective-permute-start(bf16[768,768]{1,0:T(8,128)(2,1)} %up0_ref.1), channel_id=1, source_target_pairs={{0,1},{1,0},{2,3},{3,2},{4,5},{5,4},{6,7},{7,6},{8,9},{9,8},{10,11... | collective-permute-start | bytes 3538952 | tf_op jit(solution)/shard_map/ppermute | solution.py:587
  108.3 57.0 %collective-permute-start.8 = (bf16[192,768]{1,0:T(8,128)(2,1)S(1)}, bf16[192,768]{1,0:T(8,128)(2,1)S(1)}, u32[]{:S(2)}, u32[]{:S(2)}) collective-permute-start(bf16[192,768]{1,0:T(8,128)(2,1)S(1)} %collective-permute-done.7.wo2_ref), channel_id=1, source_target_pairs={{0,1},{1,0},{2,3},{3,2},{4,5},{5,4},{6,7},{7,6},{8,9},{9,8},{10,11... | collective-permute-start | bytes 884744 | tf_op jit(solution)/shard_map/ppermute | solution.py:589
  108.8 61.1 %collective-permute-start.11 = (bf16[768,768]{1,0:T(8,128)(2,1)}, bf16[768,768]{1,0:T(8,128)(2,1)}, u32[]{:S(2)}, u32[]{:S(2)}) collective-permute-start(bf16[768,768]{1,0:T(8,128)(2,1)} %collective-permute-done.10.up2_ref), channel_id=1, source_target_pairs={{0,1},{1,0},{2,3},{3,2},{4,5},{5,4},{6,7},{7,6},{8,9},{9,8},{10,11... | collective-permute-start | bytes 3538952 | tf_op jit(solution)/shard_map/ppermute | solution.py:589
  108.8 61.0 %collective-permute-start.17 = (bf16[768,768]{1,0:T(8,128)(2,1)}, bf16[768,768]{1,0:T(8,128)(2,1)}, u32[]{:S(2)}, u32[]{:S(2)}) collective-permute-start(bf16[768,768]{1,0:T(8,128)(2,1)} %collective-permute-done.16.dn2_ref), channel_id=1, source_target_pairs={{0,1},{1,0},{2,3},{3,2},{4,5},{5,4},{6,7},{7,6},{8,9},{9,8},{10,11... | collective-permute-start | bytes 3538952 | tf_op jit(solution)/shard_map/ppermute | solution.py:589
  165.4 4.5 collective-permute-start.3
  165.5 12.0 %collective-permute-start.4 = (bf16[768,192]{1,0:T(8,128)(2,1)S(1)}, bf16[768,192]{1,0:T(8,128)(2,1)}, u32[]{:S(2)}, u32[]{:S(2)}) collective-permute-start(bf16[768,192]{1,0:T(8,128)(2,1)S(1)} %get-tuple-element.90), channel_id=1, source_target_pairs={{0,2},{2,0},{1,3},{3,1},{4,6},{6,4},{5,7},{7,5},{8,10},{10,8},{9,1... | collective-permute-start | bytes 884744 | tf_op jit(solution)/shard_map/ppermute | solution.py:623
  167.2 17.8 %collective-permute-start.5 = (bf16[768,192]{1,0:T(8,128)(2,1)S(1)}, bf16[768,192]{1,0:T(8,128)(2,1)}, u32[]{:S(2)}, u32[]{:S(2)}) collective-permute-start(bf16[768,192]{1,0:T(8,128)(2,1)S(1)} %get-tuple-element.89), channel_id=1, source_target_pairs={{0,3},{3,0},{1,2},{2,1},{4,7},{7,4},{5,6},{6,5},{8,11},{11,8},{9,1... | collective-permute-start | bytes 884744 | tf_op jit(solution)/shard_map/ppermute | solution.py:623
  231.3 168.0 %collective-permute-start.48 = (bf16[2,768,768]{2,1,0:T(8,128)(2,1)}, bf16[2,768,768]{2,1,0:T(8,128)(2,1)}, u32[]{:S(2)}, u32[]{:S(2)}) collective-permute-start(bf16[2,768,768]{2,1,0:T(8,128)(2,1)} %get-tuple-element.70), channel_id=1, source_target_pairs={{0,1},{1,0},{2,3},{3,2},{4,5},{5,4},{6,7},{7,6},{8,9},{9,8},{10,11... | collective-permute-start | bytes 7077896 | tf_op jit(solution)/shard_map/ppermute | solution.py:521
  241.8 159.9 %collective-permute-start.40 = (bf16[2,960,768]{2,1,0:T(8,128)(2,1)}, bf16[2,960,768]{2,1,0:T(8,128)(2,1)S(1)}, u32[]{:S(2)}, u32[]{:S(2)}) collective-permute-start(bf16[2,960,768]{2,1,0:T(8,128)(2,1)} %get-tuple-element.67), channel_id=1, source_target_pairs={{0,1},{1,0},{2,3},{3,2},{4,5},{5,4},{6,7},{7,6},{8,9},{9,8},{10,11... | collective-permute-start | bytes 8847368 | tf_op jit(solution)/shard_map/ppermute | solution.py:521
  244.2 3.5 collective-permute-start.18
  244.5 11.9 %collective-permute-start.19 = (bf16[768,192]{1,0:T(8,128)(2,1)S(1)}, bf16[768,192]{1,0:T(8,128)(2,1)S(1)}, u32[]{:S(2)}, u32[]{:S(2)}) collective-permute-start(bf16[768,192]{1,0:T(8,128)(2,1)S(1)} %get-tuple-element.86), channel_id=1, source_target_pairs={{0,2},{2,0},{1,3},{3,1},{4,6},{6,4},{5,7},{7,5},{8,10},{10,8},{9,1... | collective-permute-start | bytes 884744 | tf_op jit(solution)/shard_map/ppermute | solution.py:652
  246.2 17.2 %collective-permute-start.20 = (bf16[768,192]{1,0:T(8,128)(2,1)S(1)}, bf16[768,192]{1,0:T(8,128)(2,1)S(1)}, u32[]{:S(2)}, u32[]{:S(2)}) collective-permute-start(bf16[768,192]{1,0:T(8,128)(2,1)S(1)} %get-tuple-element.85), channel_id=1, source_target_pairs={{0,3},{3,0},{1,2},{2,1},{4,7},{7,4},{5,6},{6,5},{8,11},{11,8},{9,1... | collective-permute-start | bytes 884744 | tf_op jit(solution)/shard_map/ppermute | solution.py:652
  247.7 134.9 %collective-permute-start.35 = (f32[2,1,768]{2,1,0:T(1,128)S(1)}, f32[2,1,768]{2,1,0:T(1,128)S(1)}, u32[]{:S(2)}, u32[]{:S(2)}) collective-permute-start(f32[2,1,768]{2,1,0:T(1,128)S(1)} %pad_maximum_fusion.3), channel_id=1, source_target_pairs={{0,1},{1,0},{2,3},{3,2},{4,5},{5,4},{6,7},{7,6},{8,9},{9,8},{10,11... | collective-permute-start | bytes 18440 | tf_op jit(solution)/shard_map/ppermute | solution.py:742
  379.6 17.1 %collective-permute-start.29 = (bf16[384,768]{1,0:T(8,128)(2,1)S(1)}, bf16[384,768]{1,0:T(8,128)(2,1)}, u32[]{:S(2)}, u32[]{:S(2)}) collective-permute-start(bf16[384,768]{1,0:T(8,128)(2,1)S(1)} %constant_dynamic-slice_fusion.8), channel_id=1, source_target_pairs={{0,4},{4,0},{8,12},{12,8},{16,20},{20,16},{24,28},{28,24},{1,5},{5... | collective-permute-start | bytes 1769480 | tf_op jit(solution)/shard_map/ppermute | solution.py:513
  383.3 3.6 collective-permute-start.36
  388.4 29.2 %slice-start = ((s8[4718592]{0:T(1024)(128)(4,1)}), s8[4194304]{0:T(1024)(128)(4,1)S(1)}, s32[]{:S(2)}) async-start(s8[4718592]{0:T(1024)(128)(4,1)} %bitcast.62), calls=%async_computation | async-start | bytes 8388608
  390.3 27.2 %collective-permute-start.21 = (bf16[768,768]{1,0:T(8,128)(2,1)S(1)}, bf16[768,768]{1,0:T(8,128)(2,1)S(1)}, u32[]{:S(2)}, u32[]{:S(2)}) collective-permute-start(bf16[768,768]{1,0:T(8,128)(2,1)S(1)} %get-tuple-element.84), channel_id=1, source_target_pairs={{0,1},{1,0},{2,3},{3,2},{4,5},{5,4},{6,7},{7,6},{8,9},{9,8},{10,11... | collective-permute-start | bytes 3538952 | tf_op jit(solution)/shard_map/ppermute | solution.py:719
  390.4 27.2 %collective-permute-start.22 = (bf16[768,768]{1,0:T(8,128)(2,1)S(1)}, bf16[768,768]{1,0:T(8,128)(2,1)S(1)}, u32[]{:S(2)}, u32[]{:S(2)}) collective-permute-start(bf16[768,768]{1,0:T(8,128)(2,1)S(1)} %get-tuple-element.83), channel_id=1, source_target_pairs={{0,1},{1,0},{2,3},{3,2},{4,5},{5,4},{6,7},{7,6},{8,9},{9,8},{10,11... | collective-permute-start | bytes 3538952 | tf_op jit(solution)/shard_map/ppermute | solution.py:718
  398.1 8.9 %collective-permute-start.30 = (bf16[192,768]{1,0:T(8,128)(2,1)S(1)}, bf16[192,768]{1,0:T(8,128)(2,1)S(1)}, u32[]{:S(2)}, u32[]{:S(2)}) collective-permute-start(bf16[192,768]{1,0:T(8,128)(2,1)S(1)} %constant_dynamic-slice_fusion.7), channel_id=1, source_target_pairs={{0,8},{4,12},{8,0},{12,4},{16,24},{20,28},{24,16},{28,20},{1,9},{5... | collective-permute-start | bytes 884744 | tf_op jit(solution)/shard_map/ppermute | solution.py:513
  401.0 29.0 %collective-permute-start.49 = (bf16[768,768]{1,0:T(8,128)(2,1)S(1)}, bf16[768,768]{1,0:T(8,128)(2,1)S(1)}, u32[]{:S(2)}, u32[]{:S(2)}) collective-permute-start(bf16[768,768]{1,0:T(8,128)(2,1)S(1)} %fusion.7), channel_id=1, source_target_pairs={{0,2},{2,0},{1,3},{3,1},{4,6},{6,4},{5,7},{7,5},{8,10},{10,8},{9,1... | collective-permute-start | bytes 3538952 | tf_op jit(solution)/shard_map/ppermute | solution.py:523
  403.3 58.3 %collective-permute-start.41 = (bf16[960,768]{1,0:T(8,128)(2,1)S(1)}, bf16[960,768]{1,0:T(8,128)(2,1)S(1)}, u32[]{:S(2)}, u32[]{:S(2)}) collective-permute-start(bf16[960,768]{1,0:T(8,128)(2,1)S(1)} %fusion.5), channel_id=1, source_target_pairs={{0,2},{2,0},{1,3},{3,1},{4,6},{6,4},{5,7},{7,5},{8,10},{10,8},{9,1... | collective-permute-start | bytes 4423688 | tf_op jit(solution)/shard_map/ppermute | solution.py:523
  407.2 9.0 %collective-permute-start.31 = (bf16[96,768]{1,0:T(8,128)(2,1)S(1)}, bf16[96,768]{1,0:T(8,128)(2,1)S(1)}, u32[]{:S(2)}, u32[]{:S(2)}) collective-permute-start(bf16[96,768]{1,0:T(8,128)(2,1)S(1)} %constant_dynamic-slice_fusion.6), channel_id=1, source_target_pairs={{0,16},{4,20},{8,24},{12,28},{16,0},{20,4},{24,8},{28,12},{1,17},{... | collective-permute-start | bytes 442376 | tf_op jit(solution)/shard_map/ppermute | solution.py:513
  416.2 47.7 %collective-permute-start.37 = (f32[1,1536]{1,0:T(1,128)S(1)}, f32[1,1536]{1,0:T(1,128)S(1)}, u32[]{:S(2)}, u32[]{:S(2)}) collective-permute-start(f32[1,1536]{1,0:T(1,128)S(1)} %pad_maximum_fusion.4), channel_id=1, source_target_pairs={{0,4},{4,0},{8,12},{12,8},{16,20},{20,16},{24,28},{28,24},{1,5},{5... | collective-permute-start | bytes 18440 | tf_op jit(solution)/shard_map/ppermute | solution.py:513
  417.5 54.8 %collective-permute-start.32 = (bf16[96,768]{1,0:T(8,128)(2,1)S(1)}, bf16[96,768]{1,0:T(8,128)(2,1)S(1)}, u32[]{:S(2)}, u32[]{:S(2)}) collective-permute-start(bf16[96,768]{1,0:T(8,128)(2,1)S(1)} %add_convert_fusion.12), channel_id=1, source_target_pairs={{0,16},{4,20},{8,24},{12,28},{16,0},{20,4},{24,8},{28,12},{1,17},{... | collective-permute-start | bytes 442376 | tf_op jit(solution)/shard_map/ppermute | solution.py:513
  419.7 65.2 %collective-permute-start.23 = (bf16[768,768]{1,0:T(8,128)(2,1)}, bf16[768,768]{1,0:T(8,128)(2,1)}, u32[]{:S(2)}, u32[]{:S(2)}) collective-permute-start(bf16[768,768]{1,0:T(8,128)(2,1)} %get-tuple-element.81), channel_id=1, source_target_pairs={{0,2},{2,0},{1,3},{3,1},{4,6},{6,4},{5,7},{7,5},{8,10},{10,8},{9,1... | collective-permute-start | bytes 3538952 | tf_op jit(solution)/shard_map/ppermute | solution.py:720
  430.0 31.6 %copy-start.3 = (bf16[2,960,768]{2,1,0:T(8,128)(2,1)S(1)}, bf16[2,960,768]{2,1,0:T(8,128)(2,1)}, u32[]{:S(2)}) copy-start(bf16[2,960,768]{2,1,0:T(8,128)(2,1)} %copy-done.2) | copy-start | bytes 8847364
  432.8 59.8 %collective-permute-start.50 = (bf16[384,768]{1,0:T(8,128)(2,1)}, bf16[384,768]{1,0:T(8,128)(2,1)}, u32[]{:S(2)}, u32[]{:S(2)}) collective-permute-start(bf16[384,768]{1,0:T(8,128)(2,1)} %constant_dynamic-slice_fusion.2), channel_id=1, source_target_pairs={{0,4},{4,0},{8,12},{12,8},{16,20},{20,16},{24,28},{28,24},{1,5},{5... | collective-permute-start | bytes 1769480 | tf_op jit(solution)/shard_map/ppermute | solution.py:513
  463.1 32.5 %collective-permute-start.42 = (bf16[480,768]{1,0:T(8,128)(2,1)}, bf16[480,768]{1,0:T(8,128)(2,1)}, u32[]{:S(2)}, u32[]{:S(2)}) collective-permute-start(bf16[480,768]{1,0:T(8,128)(2,1)} %constant_dynamic-slice_fusion.5), channel_id=1, source_target_pairs={{0,4},{4,0},{8,12},{12,8},{16,20},{20,16},{24,28},{28,24},{1,5},{5... | collective-permute-start | bytes 2211848 | tf_op jit(solution)/shard_map/ppermute | solution.py:513
  463.9 3.7 collective-permute-start.38
  467.6 4.7 collective-permute-start.39
  472.4 66.0 %collective-permute-start.33 = (bf16[192,768]{1,0:T(8,128)(2,1)S(1)}, bf16[192,768]{1,0:T(8,128)(2,1)S(1)}, u32[]{:S(2)}, u32[]{:S(2)}) collective-permute-start(bf16[192,768]{1,0:T(8,128)(2,1)S(1)} %maximum_select_fusion.8), channel_id=1, source_target_pairs={{0,8},{4,12},{8,0},{12,4},{16,24},{20,28},{24,16},{28,20},{1,9},{5... | collective-permute-start | bytes 884744 | tf_op jit(solution)/shard_map/ppermute | solution.py:513
  493.9 10.0 %collective-permute-start.51 = (bf16[192,768]{1,0:T(8,128)(2,1)S(1)}, bf16[192,768]{1,0:T(8,128)(2,1)S(1)}, u32[]{:S(2)}, u32[]{:S(2)}) collective-permute-start(bf16[192,768]{1,0:T(8,128)(2,1)S(1)} %constant_dynamic-slice_fusion.1), channel_id=1, source_target_pairs={{0,8},{4,12},{8,0},{12,4},{16,24},{20,28},{24,16},{28,20},{1,9},{5... | collective-permute-start | bytes 884744 | tf_op jit(solution)/shard_map/ppermute | solution.py:513
  497.0 15.7 %collective-permute-start.43 = (bf16[240,768]{1,0:T(8,128)(2,1)S(1)}, bf16[240,768]{1,0:T(8,128)(2,1)S(1)}, u32[]{:S(2)}, u32[]{:S(2)}) collective-permute-start(bf16[240,768]{1,0:T(8,128)(2,1)S(1)} %constant_dynamic-slice_fusion.4), channel_id=1, source_target_pairs={{0,8},{4,12},{8,0},{12,4},{16,24},{20,28},{24,16},{28,20},{1,9},{5... | collective-permute-start | bytes 1105928 | tf_op jit(solution)/shard_map/ppermute | solution.py:513
  504.0 22.9 %copy-start.6 = (f32[8,768]{1,0:T(8,128)S(1)}, f32[8,768]{1,0:T(8,128)}, u32[]{:S(2)}) copy-start(f32[8,768]{1,0:T(8,128)} %get-tuple-element.57) | copy-start | bytes 73732
  504.0 10.7 %collective-permute-start.52 = (bf16[96,768]{1,0:T(8,128)(2,1)S(1)}, bf16[96,768]{1,0:T(8,128)(2,1)S(1)}, u32[]{:S(2)}, u32[]{:S(2)}) collective-permute-start(bf16[96,768]{1,0:T(8,128)(2,1)S(1)} %constant_dynamic-slice_fusion), channel_id=1, source_target_pairs={{0,16},{4,20},{8,24},{12,28},{16,0},{20,4},{24,8},{28,12},{1,17},{... | collective-permute-start | bytes 442376 | tf_op jit(solution)/shard_map/ppermute | solution.py:513
  512.8 13.9 %collective-permute-start.44 = (bf16[120,768]{1,0:T(8,128)(2,1)S(1)}, bf16[120,768]{1,0:T(8,128)(2,1)S(1)}, u32[]{:S(2)}, u32[]{:S(2)}) collective-permute-start(bf16[120,768]{1,0:T(8,128)(2,1)S(1)} %constant_dynamic-slice_fusion.3), channel_id=1, source_target_pairs={{0,16},{4,20},{8,24},{12,28},{16,0},{20,4},{24,8},{28,12},{1,17},{... | collective-permute-start | bytes 552968 | tf_op jit(solution)/shard_map/ppermute | solution.py:513
  514.8 18.6 %collective-permute-start.53 = (bf16[96,768]{1,0:T(8,128)(2,1)S(1)}, bf16[96,768]{1,0:T(8,128)(2,1)S(1)}, u32[]{:S(2)}, u32[]{:S(2)}) collective-permute-start(bf16[96,768]{1,0:T(8,128)(2,1)S(1)} %add_convert_fusion.11), channel_id=1, source_target_pairs={{0,16},{4,20},{8,24},{12,28},{16,0},{20,4},{24,8},{28,12},{1,17},{... | collective-permute-start | bytes 442376 | tf_op jit(solution)/shard_map/ppermute | solution.py:513
  526.8 10.2 %collective-permute-start.45 = (bf16[120,768]{1,0:T(8,128)(2,1)S(1)}, bf16[120,768]{1,0:T(8,128)(2,1)S(1)}, u32[]{:S(2)}, u32[]{:S(2)}) collective-permute-start(bf16[120,768]{1,0:T(8,128)(2,1)S(1)} %add_convert_fusion.10), channel_id=1, source_target_pairs={{0,16},{4,20},{8,24},{12,28},{16,0},{20,4},{24,8},{28,12},{1,17},{... | collective-permute-start | bytes 552968 | tf_op jit(solution)/shard_map/ppermute | solution.py:513
  526.9 10.9 %collective-permute-start.24 = (f32[48,768]{1,0:T(8,128)S(1)}, f32[48,768]{1,0:T(8,128)S(1)}, u32[]{:S(2)}, u32[]{:S(2)}) collective-permute-start(f32[48,768]{1,0:T(8,128)S(1)} %constant_dynamic-update-slice_fusion), channel_id=1, source_target_pairs={{0,1},{1,0},{2,3},{3,2},{4,5},{5,4},{6,7},{7,6},{8,9},{9,8},{10,11... | collective-permute-start | bytes 442376 | tf_op jit(solution)/shard_map/ppermute | solution.py:548
  533.4 10.9 %collective-permute-start.54 = (bf16[192,768]{1,0:T(8,128)(2,1)S(1)}, bf16[192,768]{1,0:T(8,128)(2,1)S(1)}, u32[]{:S(2)}, u32[]{:S(2)}) collective-permute-start(bf16[192,768]{1,0:T(8,128)(2,1)S(1)} %maximum_select_fusion.9), channel_id=1, source_target_pairs={{0,8},{4,12},{8,0},{12,4},{16,24},{20,28},{24,16},{28,20},{1,9},{5... | collective-permute-start | bytes 884744 | tf_op jit(solution)/shard_map/ppermute | solution.py:513
  537.1 12.4 %collective-permute-start.46 = (bf16[240,768]{1,0:T(8,128)(2,1)S(1)}, bf16[240,768]{1,0:T(8,128)(2,1)S(1)}, u32[]{:S(2)}, u32[]{:S(2)}) collective-permute-start(bf16[240,768]{1,0:T(8,128)(2,1)S(1)} %maximum_select_fusion.7), channel_id=1, source_target_pairs={{0,8},{4,12},{8,0},{12,4},{16,24},{20,28},{24,16},{28,20},{1,9},{5... | collective-permute-start | bytes 1105928 | tf_op jit(solution)/shard_map/ppermute | solution.py:513
  537.9 5.5 collective-permute-start.25
  539.3 22.6 %collective-permute-start.34 = (bf16[384,768]{1,0:T(8,128)(2,1)}, bf16[384,768]{1,0:T(8,128)(2,1)}, u32[]{:S(2)}, u32[]{:S(2)}) collective-permute-start(bf16[384,768]{1,0:T(8,128)(2,1)} %maximum_select_fusion.3), channel_id=1, source_target_pairs={{0,4},{4,0},{8,12},{12,8},{16,20},{20,16},{24,28},{28,24},{1,5},{5... | collective-permute-start | bytes 1769480 | tf_op jit(solution)/shard_map/ppermute | solution.py:513
  543.4 16.4 %collective-permute-start.26 = (f32[48,768]{1,0:T(8,128)S(1)}, f32[48,768]{1,0:T(8,128)S(1)}, u32[]{:S(2)}, u32[]{:S(2)}) collective-permute-start(f32[48,768]{1,0:T(8,128)S(1)} %add.185), channel_id=1, source_target_pairs={{0,4},{4,0},{8,12},{12,8},{16,20},{20,16},{24,28},{28,24},{1,5},{5... | collective-permute-start | bytes 442376 | tf_op jit(solution)/shard_map/ppermute | solution.py:513
  544.5 31.1 %collective-permute-start.55 = (bf16[384,768]{1,0:T(8,128)(2,1)S(1)}, bf16[384,768]{1,0:T(8,128)(2,1)}, u32[]{:S(2)}, u32[]{:S(2)}) collective-permute-start(bf16[384,768]{1,0:T(8,128)(2,1)S(1)} %maximum_select_fusion.5), channel_id=1, source_target_pairs={{0,4},{4,0},{8,12},{12,8},{16,20},{20,16},{24,28},{28,24},{1,5},{5... | collective-permute-start | bytes 1769480 | tf_op jit(solution)/shard_map/ppermute | solution.py:513
  549.7 36.3 %collective-permute-start.47 = (bf16[480,768]{1,0:T(8,128)(2,1)S(1)}, bf16[480,768]{1,0:T(8,128)(2,1)}, u32[]{:S(2)}, u32[]{:S(2)}) collective-permute-start(bf16[480,768]{1,0:T(8,128)(2,1)S(1)} %maximum_select_fusion.2), channel_id=1, source_target_pairs={{0,4},{4,0},{8,12},{12,8},{16,20},{20,16},{24,28},{28,24},{1,5},{5... | collective-permute-start | bytes 2211848 | tf_op jit(solution)/shard_map/ppermute | solution.py:513
  559.9 6.8 %collective-permute-start.27 = (f32[48,768]{1,0:T(8,128)S(1)}, f32[48,768]{1,0:T(8,128)S(1)}, u32[]{:S(2)}, u32[]{:S(2)}) collective-permute-start(f32[48,768]{1,0:T(8,128)S(1)} %add.186), channel_id=1, source_target_pairs={{0,8},{4,12},{8,0},{12,4},{16,24},{20,28},{24,16},{28,20},{1,9},{5... | collective-permute-start | bytes 442376 | tf_op jit(solution)/shard_map/ppermute | solution.py:513
  566.7 7.7 %collective-permute-start.28 = (f32[48,768]{1,0:T(8,128)S(1)}, f32[48,768]{1,0:T(8,128)S(1)}, u32[]{:S(2)}, u32[]{:S(2)}) collective-permute-start(f32[48,768]{1,0:T(8,128)S(1)} %add.187), channel_id=1, source_target_pairs={{0,16},{4,20},{8,24},{12,28},{16,0},{20,4},{24,8},{28,12},{1,17},{... | collective-permute-start | bytes 442376 | tf_op jit(solution)/shard_map/ppermute | solution.py:513
  (18 other events, 114.9 us)

commit v2 on v1

v2 whole, which is shorter than its diff:
```python
import functools
import math

import jax
import jax.numpy as jnp
from jax import lax
from jax.experimental import pallas as pl
from jax.experimental.pallas import tpu as pltpu
from jax.sharding import PartitionSpec as P

HEAD = 64
EPS = 1e-05
LOG2E = math.log2(math.e)
LN2 = math.log(2.0)
TILE = 256
PAD = 16
VMEM_LIMIT = 60 * 1024 * 1024

f32 = jnp.float32
bf16 = jnp.bfloat16
i32 = jnp.int32

CORE = ((0, 1), (1, 0), (2, 3), (3, 2))
NEXT = ((0, 2), (2, 0), (1, 3), (3, 1))
DIAG = ((0, 3), (3, 0), (1, 2), (2, 1))

PARAMS = pltpu.CompilerParams(vmem_limit_bytes=VMEM_LIMIT)


def iota(shape, axis):
    return lax.broadcasted_iota(i32, shape, axis)


def dot(left, right, dims):
    return lax.dot_general(left, right, (dims, ((), ())), preferred_element_type=f32)


NN = ((1,), (0,))
NT = ((1,), (1,))
TN = ((0,), (0,))


def shape_of(shape, dtype):
    return jax.ShapeDtypeStruct(shape, dtype)


def whole_specs(count):
    return [pl.BlockSpec(memory_space=pltpu.VMEM)] * count


SMEM = pl.BlockSpec(memory_space=pltpu.SMEM)
VMEM = pl.BlockSpec(memory_space=pltpu.VMEM)
HBM = pl.BlockSpec(memory_space=pl.ANY)


def call(body, out_shape, in_specs, out_specs, name, micros, scratch=(), grid=()):
    return pl.pallas_call(
        body,
        out_shape=out_shape,
        grid=grid,
        in_specs=in_specs,
        out_specs=out_specs,
        scratch_shapes=scratch,
        compiler_params=PARAMS,
        name=name,
        cost_estimate=pl.CostEstimate(
            flops=int(micros * 1.15e9), bytes_accessed=1024, transcendentals=0
        ),
    )


def local_frame(frame_ref):
    return frame_ref[...].reshape(1, frame_ref.shape[0]) % 2


def row_of(ref):
    return ref[...].astype(f32).reshape(1, ref.shape[0])


def rows_with_lead(tok_ref, frame_ref, lead_ref, table_ref):
    frame = local_frame(frame_ref)
    lead = jnp.where(frame == 0, lead_ref[0], lead_ref[1])
    hot = (iota((table_ref.shape[0], frame.shape[1]), 0) == lead).astype(bf16)
    return tok_ref[...].astype(f32) + dot(hot, table_ref[...], TN), hot


def norm_stats(values):
    average = jnp.mean(values, axis=-1, keepdims=True)
    centred = values - average
    spread = jnp.mean(centred * centred, axis=-1, keepdims=True)
    inverse = lax.rsqrt(spread + EPS)
    return centred * inverse, inverse


def pre_kernel(tok_ref, frame_ref, lead_ref, table_ref, gain_ref, shift_ref, out_ref, perm_ref):
    rows = tok_ref.shape[0]
    values, _ = rows_with_lead(tok_ref, frame_ref, lead_ref, table_ref)
    unit, _ = norm_stats(values)
    normed = (unit * row_of(gain_ref) + row_of(shift_ref)).astype(bf16)
    first = (local_frame(frame_ref) == 0).astype(f32)
    before = (iota((rows, rows), 0) < iota((rows, rows), 1)).astype(bf16)
    earlier = dot(jnp.broadcast_to(first, (8, rows)).astype(bf16), before, NN)[0:1]
    count = jnp.sum(first, axis=1, keepdims=True)
    place = jnp.where(first > 0, earlier, count + iota((1, rows), 1).astype(f32) - earlier)
    perm = (iota((rows, rows), 0) == place.astype(i32)).astype(bf16)
    perm_ref[...] = perm
    out_ref[0:rows, :] = dot(perm, normed, NN).astype(bf16)
    high = jnp.floor(count * (1.0 / 16))
    low = count - 16 * high
    tail = iota((PAD, out_ref.shape[1]), 0)
    out_ref[rows : rows + PAD, :] = jnp.where(
        tail == 0, high, jnp.where(tail == 1, low, 0.0)
    ).astype(bf16)


def read_count(block_ref, rows):
    part = block_ref[rows : rows + PAD, 0:128].astype(f32)
    place, lane = iota(part.shape, 0), iota(part.shape, 1)
    worth = jnp.where(place == 0, 16.0, jnp.where(place == 1, 1.0, 0.0))
    return jnp.sum(jnp.where(lane == 0, part * worth, 0.0)).astype(i32)


def tile_moves(counts, rows, block, tile):
    group = 4 * rows
    count = counts[block]
    longs_before = sum(counts[:block], jnp.int32(0))
    limit = jnp.clip(count - tile * TILE, 0, TILE)
    moves = []
    for some, base, low, high in (
        (limit > 0, longs_before + tile * TILE, 0, limit),
        (limit < TILE, 2 * group // 3 + block * rows - longs_before - count + tile * TILE, limit, TILE),
    ):
        spot = jnp.minimum(base // TILE, group // TILE - 2)
        window = pl.ds(pl.multiple_of(spot * TILE, TILE), 2 * TILE)
        moves.append((some, window, base - spot * TILE, low, high))
    return moves


def aligned(index, size):
    return pl.ds(pl.multiple_of(index * size, size), size)


def to_group(value, dst_ref, moves):
    width = value.shape[1]
    for some, window, shift, low, high in moves:

        @pl.when(some)
        def _():
            dest, source = iota((2 * TILE, TILE), 0), iota((2 * TILE, TILE), 1)
            hot = (dest - source == shift) & (source >= low) & (source < high)
            moved = dot(hot.astype(bf16), value, NN).astype(bf16)
            dst_ref[window, 0:width] = dst_ref[window, 0:width] + moved


def from_group(src_refs, acc_refs, moves):
    (some_long, *long), (some_short, *short) = moves

    def moved(window, shift, low, high):
        source, dest = iota((TILE, 2 * TILE), 0), iota((TILE, 2 * TILE), 1)
        hot = ((dest - source == shift) & (source >= low) & (source < high)).astype(bf16)
        return [dot(hot, ref[window, :], NN).astype(bf16) for ref in src_refs]

    @pl.when(some_long)
    def _():
        for ref, value in zip(acc_refs, moved(*long)):
            ref[...] = value

    @pl.when(jnp.logical_not(some_long))
    def _():
        for ref, value in zip(acc_refs, moved(*short)):
            ref[...] = value

    @pl.when(some_long & some_short)
    def _():
        for ref, value in zip(acc_refs, moved(*short)):
            ref[...] = ref[...] + value


def head_columns(ref, start, width):
    first = start // 128 * 128
    if first + 128 <= width:
        piece = ref[:, first : first + 128].astype(f32)
    else:
        piece = jnp.concatenate([ref[:, first : first + HEAD].astype(f32)] * 2, axis=1)
    return pltpu.roll(piece, HEAD, 1) if start != first else piece


def attend_kernel(
    weight_ref, bias_ref, scale_ref, x0_ref, x1_ref, x2_ref, x3_ref,
    att_ref, lse_ref, counts_ref, a0_ref, a1_ref, a2_ref, a3_ref, q_out, k_out, v_out,
    x_buf, qkv_ref, q_ref, k_ref, v_ref, scores_ref, load_sems, store_sems,
):
    blocks = (x0_ref, x1_ref, x2_ref, x3_ref)
    rows = x0_ref.shape[0] - PAD
    group = len(blocks) * rows
    long = 2 * group // 3
    width = weight_ref.shape[1] // 3
    heads = width // HEAD
    loads = [pltpu.make_async_copy(blocks[i], x_buf.at[i], load_sems.at[i]) for i in range(4)]
    for load in loads:
        load.start()
    qkv_ref[...] = jnp.zeros(qkv_ref.shape, qkv_ref.dtype)
    for load in loads:
        load.wait()
    counts = [read_count(x_buf.at[i], rows) for i in range(4)]
    for index, count in enumerate(counts):
        counts_ref[index] = count
    for index in range(4):

        def project(tile, _, index=index):
            value = dot(x_buf[index, aligned(tile, TILE), :], weight_ref[...], NN)
            value = ((value + bias_ref[...]) * scale_ref[...]).astype(bf16)
            to_group(value, qkv_ref, tile_moves(counts, rows, index, tile))
            return 0

        lax.fori_loop(0, rows // TILE, project, 0)
    lane = iota((group, 128), 1)
    stores = []
    for part, ref, out, fill in ((1, k_ref, k_out, 0.0), (2, v_ref, v_out, 1.0), (0, q_ref, q_out, 0.0)):
        for head in range(heads):
            piece = head_columns(qkv_ref, part * width + head * HEAD, 3 * width)
            ref[head] = jnp.where(lane < HEAD, piece, fill).astype(bf16)
        store = pltpu.make_async_copy(ref, out, store_sems.at[part])
        store.start()
        stores.append(store)

    block = 512
    row = iota((128, block), 0)
    half = iota((block, 128), 1)
    tasks = [
        (head, first, low, high)
        for low, high in ((0, long), (long, group))
        for first in range(low, high, block)
        for head in range(heads)
    ]

    def scores(task, part):
        head, first, low, high = tasks[task]
        keys = slice(low + part * block, low + (part + 1) * block)
        value = dot(k_ref[head, keys, :], q_ref[head, first : first + block, :], NT)
        scores_ref[task % 2, part * block : (part + 1) * block, :] = value
        return jnp.max(value.reshape(block // 8, 8, block), axis=0)

    def parts_of(task):
        return (tasks[task][3] - tasks[task][2]) // block if task < len(tasks) else 0

    largest = functools.reduce(jnp.maximum, [scores(0, part) for part in range(parts_of(0))])
    outs = []
    for task, (head, first, low, high) in enumerate(tasks):
        top = jnp.max(largest, axis=0, keepdims=True)
        following, mixed = [], None
        for part in range(max(parts_of(task), parts_of(task + 1))):
            if part < parts_of(task + 1):
                following.append(scores(task + 1, part))
            if part < parts_of(task):
                raised = jnp.exp2(scores_ref[task % 2, part * block : (part + 1) * block, :] - top)
                keys = slice(low + part * block, low + (part + 1) * block)
                value = dot(v_ref[head, keys, :], raised.astype(bf16), TN)
                mixed = value if mixed is None else mixed + value
        if following:
            largest = functools.reduce(jnp.maximum, following)
        totals = mixed[HEAD : HEAD + 1, :]
        lse_ref[head : head + 1, first : first + block] = top + jnp.log2(totals)
        outs.append(jnp.where(row < HEAD, mixed / totals, 0.0))
        if head == heads - 1:
            for pair in range((heads + 1) // 2):
                value = outs[2 * pair].T
                if 2 * pair + 1 < heads:
                    value = value + pltpu.roll(outs[2 * pair + 1].T, HEAD, 1)
                att_ref[first : first + block, pair * 128 : (pair + 1) * 128] = value.astype(bf16)
            outs = []
    for index, out in enumerate((a0_ref, a1_ref, a2_ref, a3_ref)):

        def hand_back(tile, _, index=index, out=out):
            moves = tile_moves(counts, rows, index, tile)
            from_group((att_ref,), (qkv_ref.at[0:TILE, 0 : att_ref.shape[1]],), moves)
            out[aligned(tile, TILE), :] = qkv_ref[0:TILE, 0:width]
            return 0

        lax.fori_loop(0, rows // TILE, hand_back, 0)
    for store in stores:
        store.wait()


def middle_kernel(
    tok_ref, frame_ref, lead_ref, table_ref, perm_ref,
    at0_ref, at1_ref, at2_ref, at3_ref,
    wo0_ref, wo1_ref, wo2_ref, wo3_ref,
    gain_ref, shift_ref, out_bias_ref, down_bias_ref, og_ref, side_ref,
    up0_ref, up1_ref, ff2_ref, ff3_ref, dn0_ref, dn1_ref, dx2_ref, dx3_ref,
    layer_ref, xgrad_ref, agrad_ref, normed_ref, attu_ref, s0_ref, s1_ref, s2_ref, s3_ref, sums_ref, upb_ref,
    act_out, hid_out,
    y_ref, back_ref, up_buf, dn_buf, act_ref, hid_ref, load_sems, store_sems,
):
    ats = (at0_ref, at1_ref, at2_ref, at3_ref)
    wos = (wo0_ref, wo1_ref, wo2_ref, wo3_ref)
    upper = up0_ref.shape[0]
    ups = (up0_ref, up1_ref, ff2_ref.at[0:upper], ff3_ref.at[0:upper])
    dn2_ref, dn3_ref = ff2_ref.at[upper:], ff3_ref.at[upper:]
    sends = (s0_ref, s1_ref, s2_ref, s3_ref)
    rows, wide = tok_ref.shape
    hidden = act_ref.shape[2]
    half = hidden // 2
    side = side_ref[0]
    mine = pl.ds(pl.multiple_of(side * half, half), half)
    other = pl.ds(pl.multiple_of((1 - side) * half, half), half)
    loads = [[pltpu.make_async_copy(ups[i], up_buf.at[i], load_sems.at[i])] for i in range(4)]
    for index, ref, target, sem in (
        (0, dn0_ref, dn_buf.at[0], 4),
        (1, dn1_ref, dn_buf.at[1], 5),
        (2, dn2_ref, dn_buf.at[2, mine], 6),
        (2, dx2_ref, dn_buf.at[2, other], 7),
        (3, dn3_ref, dn_buf.at[3, mine], 8),
        (3, dx3_ref, dn_buf.at[3, other], 9),
    ):
        loads[index].append(pltpu.make_async_copy(ref, target, load_sems.at[sem]))
    for load in sum(loads, []):
        load.start()
    gain = row_of(gain_ref)
    values, _ = rows_with_lead(tok_ref, frame_ref, lead_ref, table_ref)
    perm = perm_ref[...]
    x_one = values + row_of(out_bias_ref)
    for index in range(4):
        mine = dot(perm, ats[index][...], TN).astype(bf16)
        attu_ref[index] = mine
        x_one = x_one + dot(mine, wos[index][...], NN)
    unit, inverse = norm_stats(x_one)
    normed_ref[...] = (unit * gain + row_of(shift_ref)).astype(bf16)
    y_ref[...] = x_one + row_of(down_bias_ref)
    back_ref[...] = jnp.zeros(back_ref.shape, f32)
    stores = []
    for index in range(4):
        for load in loads[index]:
            load.wait()
        up = up_buf[index, 0:wide, :]
        down = dn_buf[index]
        h = dot(normed_ref[...], up, NN) + up_buf[index, wide : wide + PAD, :][0:1].astype(f32)
        g = dot(og_ref[...], down, NT)
        c = math.sqrt(2.0 / math.pi)
        h2 = h * h
        t = jnp.tanh(h * (c + (c * 0.044715) * h2))
        half = 0.5 + 0.5 * t
        act = h * half
        slope = half + act * (1.0 - t) * (c + (3 * c * 0.044715) * h2)
        hid = (slope * g).astype(bf16)
        actb = act.astype(bf16)
        act_ref[index] = actb
        hid_ref[index] = hid
        upb_ref[index] = jnp.broadcast_to(jnp.sum(hid.astype(f32), axis=0, keepdims=True), (8, hidden))
        y_ref[...] += dot(actb, down, NN)
        back_ref[...] += dot(hid, up, NT)
        for source, target, sem in ((act_ref, act_out, 0), (hid_ref, hid_out, 4)):
            store = pltpu.make_async_copy(source.at[index], target.at[index], store_sems.at[sem + index])
            store.start()
            stores.append(store)
    layer_ref[...] = y_ref[...].astype(bf16)
    grad = back_ref[...]
    e = grad * gain
    spread_mean = jnp.mean(e, axis=-1, keepdims=True)
    along = jnp.mean(e * unit, axis=-1, keepdims=True)
    og = og_ref[...].astype(f32)
    xgrad = og + inverse * (e - spread_mean - unit * along)
    xgrad_ref[...] = xgrad
    agrad = xgrad.astype(bf16)
    agrad_ref[...] = agrad
    for index in range(4):
        back = dot(agrad, wos[index][...], NT).astype(bf16)
        sends[index][...] = dot(perm, back, NN).astype(bf16)
    sums_ref[...] = jnp.concatenate(
        [
            jnp.sum(grad * unit, axis=0, keepdims=True),
            jnp.sum(grad, axis=0, keepdims=True),
            jnp.sum(agrad.astype(f32), axis=0, keepdims=True),
            jnp.sum(og, axis=0, keepdims=True),
            jnp.zeros((4, og.shape[1]), f32),
        ],
        axis=0,
    )
    for store in stores:
        store.wait()


def weight_grad_kernel(normed_ref, og_ref, agrad_ref, act_ref, hid_ref, attu_ref, send_ref, keep_ref):
    up = dot(normed_ref[...], hid_ref[0], TN).astype(bf16)
    out = dot(attu_ref[0], agrad_ref[...], TN).astype(bf16)
    down = dot(act_ref[0], og_ref[...], TN).astype(bf16)
    rows, more = up.shape[0], out.shape[0]
    step = pl.program_id(0)
    for chosen, ref in ((step < 2, send_ref), (step >= 2, keep_ref)):

        @pl.when(chosen)
        def _(ref=ref):
            ref[0, 0:rows, :] = up
            ref[0, rows : rows + more, :] = out
            ref[0, rows + more :, :] = down


def gather_grad_kernel(counts_ref, b0_ref, b1_ref, b2_ref, b3_ref, att_ref, out_ref, inner_ref, sorted_ref):
    blocks = (b0_ref, b1_ref, b2_ref, b3_ref)
    rows, width = b0_ref.shape
    group = 4 * rows
    heads = width // HEAD
    counts = [counts_ref[i] for i in range(4)]
    sorted_ref[...] = jnp.zeros(sorted_ref.shape, sorted_ref.dtype)
    for index, ref in enumerate(blocks):

        def place(tile, _, index=index, ref=ref):
            to_group(ref[aligned(tile, TILE), :], sorted_ref, tile_moves(counts, rows, index, tile))
            return 0

        lax.fori_loop(0, rows // TILE, place, 0)
    lane = iota((group, 128), 1)
    pick_row, pick_lane = iota((8, 128), 0), iota((8, 128), 1)
    inner_ref[...] = jnp.zeros(inner_ref.shape, f32)
    for pair in range((heads + 1) // 2):
        columns = slice(pair * 128, (pair + 1) * 128)
        grad = sorted_ref[:, columns].astype(f32)
        product = grad * att_ref[:, columns].astype(f32)
        high = product.astype(bf16)
        low = (product - high.astype(f32)).astype(bf16)
        pick = (pick_row == 2 * pair + pick_lane // HEAD).astype(bf16)
        inner_ref[...] += dot(pick, high, NT) + dot(pick, low, NT)
        out_ref[2 * pair] = jnp.where(lane < HEAD, grad, 0.0).astype(bf16)
        if 2 * pair + 1 < heads:
            out_ref[2 * pair + 1] = jnp.where(lane < HEAD, pltpu.roll(grad, HEAD, 1), 0.0).astype(bf16)


def attend_back_kernel(first_head, lse_ref, inner_ref, q_ref, k_ref, v_ref, g_ref, out_ref, dq_ref):
    group = q_ref.shape[1]
    long = 2 * group // 3
    block = 1024
    lane = iota((block, 128), 1)
    head = first_head + pl.program_id(0)
    lse = jnp.sum(jnp.where(iota(lse_ref.shape, 0) == head, lse_ref[...], 0.0), axis=0, keepdims=True)
    inner = jnp.sum(jnp.where(iota(inner_ref.shape, 0) == head, inner_ref[...], 0.0), axis=0, keepdims=True)
    done = set()
    for low, high in ((0, long), (long, group)):
        for keys in range(low, high, block):
            key = k_ref[0, keys : keys + block, :]
            value = v_ref[0, keys : keys + block, :]
            key_grad, value_grad = None, None
            for queries in range(low, high, block):
                query = q_ref[0, queries : queries + block, :]
                grad = g_ref[0, queries : queries + block, :]
                probs = jnp.exp2(dot(key, query, NT) - lse[:, queries : queries + block])
                inside = dot(value, grad, NT) - inner[:, queries : queries + block]
                score_grad = (probs * inside).astype(bf16)
                value_part = dot(probs.astype(bf16), grad, NN)
                key_part = dot(score_grad, query, NN)
                query_part = dot(key, score_grad, TN)
                value_grad = value_part if value_grad is None else value_grad + value_part
                key_grad = key_part if key_grad is None else key_grad + key_part
                place = (slice(None), slice(queries, queries + block))
                dq_ref[place] = query_part if queries not in done else dq_ref[place] + query_part
                done.add(queries)
            out_ref[0, keys : keys + block, 0:128] = pltpu.roll(key_grad * LN2, HEAD, 1).astype(bf16)
            out_ref[0, keys : keys + block, 128:256] = value_grad.astype(bf16)
    wide = iota((group, 128), 1)
    query_grad = dq_ref[...].T * (1.0 / math.sqrt(HEAD))
    pair = jnp.where(wide < HEAD, query_grad, out_ref[0, :, 0:128].astype(f32))
    out_ref[0, :, 0:128] = pair.astype(bf16)


def project_back_kernel(
    counts_ref, h01_ref, h2_ref, weight_ref, local_ref, b0_ref, b1_ref, b2_ref, b3_ref, *acc_refs
):
    refs = [h01_ref.at[i] for i in range(h01_ref.shape[0])] + [h2_ref.at[i] for i in range(h2_ref.shape[0])]
    backs = (b0_ref, b1_ref, b2_ref, b3_ref)
    rows = local_ref.shape[1]
    counts = [counts_ref[i] for i in range(4)]
    pairs = len(refs) * 128
    lane = iota((TILE, 128), 1)
    for index in (3, 1, 2, 0):

        def step(tile, _, index=index):
            here = aligned(tile, TILE)
            from_group(refs, acc_refs, tile_moves(counts, rows, index, tile))
            for head, ref in enumerate(acc_refs):
                local_ref[index, here, head * 128 : (head + 1) * 128] = ref[:, 0:128]
            for pair in range((len(refs) + 1) // 2):
                value = acc_refs[2 * pair][:, 128:256]
                if 2 * pair + 1 < len(refs):
                    other = acc_refs[2 * pair + 1][:, 128:256].astype(f32)
                    value = jnp.where(lane < HEAD, value.astype(f32), pltpu.roll(other, HEAD, 1)).astype(bf16)
                first = pairs + pair * 128
                local_ref[index, here, first : first + 128] = value
            return 0

        lax.fori_loop(0, rows // TILE, step, 0)
        backs[index][...] = dot(local_ref[index], weight_ref[...], NT).astype(bf16)


def project_grad_kernel(first, x0_ref, x1_ref, x2_ref, x3_ref, local_ref, out_ref, sums_ref):
    rows = local_ref.shape[1]
    columns = slice(first, first + out_ref.shape[1])
    total, sums = None, None
    for index, ref in enumerate((x0_ref, x1_ref, x2_ref, x3_ref)):
        value = local_ref[index, :, columns]
        part = dot(ref[0:rows, :], value, TN)
        total = part if total is None else total + part
        one = jnp.sum(value.astype(f32), axis=0, keepdims=True)
        sums = one if sums is None else sums + one
    out_ref[...] = total.astype(bf16)
    sums_ref[...] = jnp.broadcast_to(sums, sums_ref.shape)


def last_kernel(
    tok_ref, frame_ref, lead_ref, table_ref, gain_ref, perm_ref, mine_ref, one_ref, more_ref, rest_ref, xgrad_ref,
    two_ref, upb_ref, qk_ref, v_ref, me_ref, out_ref, sums_ref,
):
    values, hot = rows_with_lead(tok_ref, frame_ref, lead_ref, table_ref)
    unit, inverse = norm_stats(values)
    other = jnp.concatenate([one_ref[...], more_ref[...], rest_ref[...]], axis=0)
    local = (mine_ref[...].astype(f32) + other.astype(f32)).astype(bf16)
    grad = dot(perm_ref[...], local, TN)
    e = grad * row_of(gain_ref)
    mean_e = jnp.mean(e, axis=-1, keepdims=True)
    along = jnp.mean(e * unit, axis=-1, keepdims=True)
    out = xgrad_ref[...] + inverse * (e - mean_e - unit * along)
    out_ref[...] = out
    leads = table_ref.shape[0]
    one = out.astype(bf16)
    rest = out - one.astype(f32)
    two = rest.astype(bf16)
    three = (rest - two.astype(f32)).astype(bf16)
    sums_ref[0:leads, :] = dot(hot, one, NN) + dot(hot, two, NN) + dot(hot, three, NN)
    row = iota((16, grad.shape[1]), 0)
    me = me_ref[0]
    small = jnp.zeros((16, grad.shape[1]), f32)
    small = jnp.where(row == 0, jnp.sum(grad * unit, axis=0, keepdims=True), small)
    small = jnp.where(row == 1, jnp.sum(grad, axis=0, keepdims=True), small)
    for i in range(4):
        small = jnp.where(row == 2 + i, two_ref[i : i + 1, :], small)
        small = jnp.where(row == 6 + (me ^ i), upb_ref[i, 0:1, :], small)
    heads = qk_ref.shape[1] // 128
    bias = [qk_ref[0:1, head * 128 : head * 128 + HEAD] for head in range(heads)]
    bias.append(v_ref[0:1, 0 : heads * HEAD])
    bias.append(jnp.zeros((1, grad.shape[1] - 2 * heads * HEAD), f32))
    small = jnp.where(row == 10 + me, jnp.concatenate(bias, axis=1), small)
    sums_ref[leads : leads + 16, :] = small


def finish_kernel(left_ref, right_ref, me_ref, lead_ref, g1_ref, b1_ref, g2_ref, b2_ref, ob_ref, db_ref, ub_ref, qv_ref):
    total = left_ref[...] + right_ref[...]
    leads = lead_ref.shape[0]
    lead_ref[...] = total[0:leads]
    for place, ref in enumerate((g1_ref, b1_ref, g2_ref, b2_ref, ob_ref, db_ref)):
        ref[...] = total[leads + place].reshape(ref.shape)
    me = me_ref[0]
    up, qv = total[leads + 6 : leads + 7], total[leads + 10 : leads + 11]
    for i in range(1, 4):
        up = jnp.where(me == i, total[leads + 6 + i : leads + 7 + i], up)
        qv = jnp.where(me == i, total[leads + 10 + i : leads + 11 + i], qv)
    ub_ref[...] = up.reshape(ub_ref.shape)
    width = qv_ref.shape[1]
    qv_ref[...] = jnp.concatenate([qv[:, 0:width], qv[:, width : 2 * width]], axis=0)


def bits_of(size):
    bits = []
    step = 1
    while step < size:
        bits.append(step)
        step *= 2
    return bits


def after(value, *others):
    return lax.optimization_barrier((value, *others))[0]


def swap(value, size, bit):
    return lax.ppermute(value, "rows", [(i, i ^ bit) for i in range(size)])


def add_low(left, right):
    return (left.astype(f32) + right.astype(f32)).astype(bf16)


def halves(value, bit, axis=0):
    half = value.shape[axis] // 2
    high = (lax.axis_index("rows") // bit) % 2
    return (
        lax.dynamic_slice_in_dim(value, high * half, half, axis),
        lax.dynamic_slice_in_dim(value, (1 - high) * half, half, axis),
    )


def joined(mine, other, bit, axis=0):
    high = (lax.axis_index("rows") // bit) % 2
    low_part, high_part = jnp.where(high == 1, other, mine), jnp.where(high == 1, mine, other)
    return jnp.concatenate([low_part, high_part], axis)


def on_device(
    rows_size,
    tokens, frame_id, lead_index, lead_embed, ln1_gain, ln1_bias, qkv_weight, qv_bias,
    out_weight, out_bias, ln2_gain, ln2_bias, up_weight, up_bias, down_weight, down_bias, out_grad,
):
    rows, width_all = tokens.shape
    width = qkv_weight.shape[2]
    heads = width // HEAD
    hidden = up_weight.shape[1]
    leads = lead_embed.shape[0]
    group = 4 * rows
    wide = (heads + 1) // 2 * 128
    bits = bits_of(rows_size)
    me = lax.axis_index("tp").reshape(1)
    side = (lax.axis_index("rows") % 2).reshape(1)

    def over(value, ring):
        return lax.ppermute(value, "tp", ring)

    up_rows = jnp.concatenate([up_weight, jnp.broadcast_to(up_bias.reshape(1, hidden), (PAD, hidden))], axis=0)
    out_far = over(out_weight, NEXT)
    mine, perm = call(
        pre_kernel,
        (shape_of((rows + PAD, width_all), bf16), shape_of((rows, rows), bf16)),
        [VMEM, VMEM, SMEM, VMEM, VMEM, VMEM], (VMEM, VMEM), "pre", 5,
    )(tokens, frame_id, lead_index, lead_embed, ln1_gain, ln1_bias)
    mine = after(mine, out_far)
    near = over(mine, CORE)
    far = over(mine, NEXT)

    out_near = over(out_weight, CORE)
    up_near = over(up_rows, CORE)
    down_near = over(down_weight, CORE)
    out_across = over(out_far, CORE)
    ff_rows = jnp.concatenate([up_rows, halves(down_weight, 1)[0]], axis=0)
    weight_qkv = jnp.concatenate([qkv_weight[0], qkv_weight[1], qkv_weight[2]], axis=1)
    zero = jnp.zeros((width,), f32)
    bias_qkv = jnp.concatenate([qv_bias[0].astype(f32), zero, qv_bias[1].astype(f32)]).reshape(1, 3 * width)
    scale_qkv = jnp.concatenate(
        [jnp.full((width,), LOG2E / math.sqrt(HEAD), f32), jnp.ones((2 * width,), f32)]
    ).reshape(1, 3 * width)
    pair_weight = qkv_weight[0:2].reshape(2, width_all, heads, HEAD).transpose(1, 2, 0, 3)
    weight_heads = jnp.concatenate(
        [
            pair_weight.reshape(width_all, heads * 128),
            jnp.pad(qkv_weight[2], ((0, 0), (0, wide - width))),
        ],
        axis=1,
    )
    far, weight_qkv, weight_heads, bias_qkv, scale_qkv, ff_rows, *_ = lax.optimization_barrier(
        (
            far, weight_qkv, weight_heads, bias_qkv, scale_qkv, ff_rows,
            out_near, out_across, up_near, down_near,
        )
    )
    across = over(far, CORE)
    parts = (mine, near, far, across)

    ff_far = over(ff_rows, NEXT)

    att, lse, counts, a0, a1, a2, a3, q_all, k_all, v_all = call(
        attend_kernel,
        (
            shape_of((group, wide), bf16),
            shape_of((8, group), f32),
            shape_of((8,), i32),
        )
        + (shape_of((rows, width), bf16),) * 4
        + (shape_of((heads, group, 128), bf16),) * 3,
        whole_specs(3) + [HBM] * 4, (VMEM, VMEM, SMEM) + (VMEM,) * 4 + (HBM,) * 3, "attend", 40,
        scratch=[
            pltpu.VMEM((4, rows + PAD, width_all), bf16),
            pltpu.VMEM((group, 3 * width), bf16),
            pltpu.VMEM((heads, group, 128), bf16),
            pltpu.VMEM((heads, group, 128), bf16),
            pltpu.VMEM((heads, group, 128), bf16),
            pltpu.VMEM((2, 2 * group // 3, 512), f32),
            pltpu.SemaphoreType.DMA((4,)),
            pltpu.SemaphoreType.DMA((3,)),
        ],
    )(weight_qkv, bias_qkv, scale_qkv, *parts)

    got = [a0, over(a1, CORE), over(a2, NEXT), over(a3, DIAG)]
    ff_far = after(ff_far, counts)
    down_side = swap(ff_far[up_rows.shape[0] :], rows_size, 1)
    ff_across = over(after(ff_far, got[1]), CORE)
    down_side, *got[2:] = lax.optimization_barrier((down_side, *got[2:]))
    down_side_across = over(down_side, CORE)

    layer_out, xgrad, agrad, normed_two, attu, s0, s1, s2, s3, sums_two, up_b, act, hid = call(
        middle_kernel,
        (
            shape_of((rows, width_all), bf16),
            shape_of((rows, width_all), f32),
            shape_of((rows, width_all), bf16),
            shape_of((rows, width_all), bf16),
            shape_of((4, rows, width), bf16),
        )
        + (shape_of((rows, width), bf16),) * 4
        + (
            shape_of((8, width_all), f32),
            shape_of((4, 8, hidden), f32),
            shape_of((4, rows, hidden), bf16),
            shape_of((4, rows, hidden), bf16),
        ),
        [VMEM, VMEM, SMEM] + whole_specs(15) + [SMEM] + [HBM] * 8, (VMEM,) * 11 + (HBM,) * 2, "middle", 32,
        scratch=[
            pltpu.VMEM((rows, width_all), f32),
            pltpu.VMEM((rows, width_all), f32),
            pltpu.VMEM((4, width_all + PAD, hidden), bf16),
            pltpu.VMEM((4, hidden, width_all), bf16),
            pltpu.VMEM((4, rows, hidden), bf16),
            pltpu.VMEM((4, rows, hidden), bf16),
            pltpu.SemaphoreType.DMA((10,)),
            pltpu.SemaphoreType.DMA((8,)),
        ],
    )(
        tokens, frame_id, lead_index, lead_embed, perm, *got, out_weight, out_near, out_far, out_across,
        ln2_gain, ln2_bias, out_bias, down_bias, out_grad, side,
        up_rows, up_near, ff_far, ff_across, down_weight, down_near, down_side, down_side_across,
    )

    got_grad = [s0, over(s1, CORE), over(s2, NEXT), over(s3, DIAG)]

    def block_of(step):
        return jnp.where(step < 2, 2 * step + 1, 2 * step - 4)

    def full(shape):
        return pl.BlockSpec(shape, lambda s: (0,) * len(shape))

    def picked(shape):
        return pl.BlockSpec((1,) + shape, lambda s: (block_of(s), 0, 0))

    tall = width_all + width + hidden
    send, keep = call(
        weight_grad_kernel,
        (shape_of((2, tall, width_all), bf16),) * 2,
        [full((rows, width_all))] * 3 + [picked((rows, hidden))] * 2 + [picked((rows, width))],
        (
            pl.BlockSpec((1, tall, width_all), lambda s: (jnp.minimum(s, 1), 0, 0)),
            pl.BlockSpec((1, tall, width_all), lambda s: (jnp.maximum(s - 2, 0), 0, 0)),
        ),
        "weight_grad", 18, grid=(4,),
    )(normed_two, out_grad, agrad, act, hid, attu)
    *got_grad[1:], send, keep = lax.optimization_barrier((*got_grad[1:], send, keep))

    from_core = over(send, CORE)
    grad_all, inner = call(
        gather_grad_kernel,
        (shape_of((heads, group, 128), bf16), shape_of((8, group), f32)),
        [SMEM] + whole_specs(5), (VMEM, VMEM), "gather_grad", 6,
        scratch=[pltpu.VMEM((group, wide), bf16)],
    )(after(counts, send), *got_grad, att)

    cut = width_all + width
    from_core = after(from_core, inner)
    down_mine = add_low(keep[0, cut:], from_core[0, cut:])
    down_other = add_low(keep[1, cut:], from_core[1, cut:])
    up_keep, up_give = halves(keep[:, :cut], 1, 1)
    up_keep_two, up_give_two = halves(from_core[:, :cut], 1, 1)
    up_mine, up_away = add_low(up_keep, up_keep_two), add_low(up_give, up_give_two)
    down_y = over(down_other, NEXT)
    up_x = swap(up_away, rows_size, 1)

    def attend_back(first, count, grads):
        spec = pl.BlockSpec((1, group, 128), lambda s: (first + s, 0, 0))
        return call(
            functools.partial(attend_back_kernel, first),
            shape_of((count, group, 256), bf16),
            [full((8, group))] * 2 + [spec] * 4,
            pl.BlockSpec((1, group, 256), lambda s: (s, 0, 0)), "attend_back", 15 * count,
            scratch=[pltpu.VMEM((128, group), f32)], grid=(count,),
        )(lse, inner, q_all, k_all, v_all, grads)

    back_01 = attend_back(0, heads - 1, after(grad_all, down_other, up_away, down_mine, up_mine))
    down_y, up_x = after(down_y, back_01), after(up_x, back_01)
    (down_keep, down_give), (down_keep_two, down_give_two) = halves(down_mine, 1), halves(down_y, 1)
    down_half_sum, down_away = add_low(down_keep, down_keep_two), add_low(down_give, down_give_two)
    up_half_sum = add_low(up_mine[0], up_x[0])
    up_other = add_low(up_mine[1], up_x[1])
    down_x = swap(down_away, rows_size, 1)
    up_y = over(up_other, NEXT)
    back_2 = attend_back(heads - 1, 1, after(grad_all, back_01, down_away, up_other, up_half_sum, down_half_sum))
    steps = bits[1:]
    down_x, up_y = after(down_x, back_2), after(up_y, back_2)

    def both(pick):
        return jnp.concatenate(
            [
                add_low(halves(down_half_sum, steps[0])[pick], halves(down_x, steps[0])[pick]),
                add_low(halves(up_half_sum, steps[0])[pick], halves(up_y, steps[0])[pick]),
            ],
            axis=0,
        )

    mixed, away = both(0), both(1)
    arrived = swap(away, rows_size, steps[0])

    local, b0, b1, b2, b3 = call(
        project_back_kernel,
        (shape_of((4, rows, heads * 128 + wide), bf16),) + (shape_of((rows, width_all), bf16),) * 4,
        [SMEM] + whole_specs(3), (VMEM,) * 5, "project_back", 12,
        scratch=[pltpu.VMEM((TILE, 256), bf16)] * heads,
    )(after(counts, away, mixed), back_01, back_2, weight_heads)

    arrived, b3, b1 = lax.optimization_barrier((arrived, b3, b1))
    over_far = over(b3, CORE)
    over_near = over(b1, CORE)
    back_far = add_low(b2, over_far)
    here = add_low(b0, over_near)
    (keep_z, give_z), (keep_z_two, give_z_two) = halves(mixed, steps[1]), halves(arrived, steps[1])
    mixed, away = add_low(keep_z, keep_z_two), add_low(give_z, give_z_two)
    arrived = swap(away, rows_size, steps[1])
    third = rows // 3
    far_one = over(back_far[:third], NEXT)

    def project_grad(first, count, local):
        return call(
            functools.partial(project_grad_kernel, first),
            (shape_of((width_all, count), bf16), shape_of((8, count), f32)),
            whole_specs(5), (VMEM, VMEM), "project_grad", 4,
        )(*parts, local)

    qk_grad, qk_sums = project_grad(0, heads * 128, after(local, back_far, away, mixed, here))
    far_one, arrived = after(far_one, qk_grad), after(arrived, qk_grad)
    far_two = over(after(back_far[third : 2 * third], far_one), NEXT)
    mixed = add_low(mixed, arrived)
    for bit in steps[2:]:
        mixed, away = halves(mixed, bit)
        mixed = add_low(mixed, swap(away, rows_size, bit))
    for bit in reversed(steps[2:]):
        mixed = joined(mixed, swap(mixed, rows_size, bit), bit)
    arrived = swap(mixed, rows_size, steps[1])
    v_grad, v_sums = project_grad(heads * 128, wide, after(local, mixed, far_one))
    far_two, arrived = after(far_two, v_grad), after(arrived, v_grad)
    far_three = over(after(back_far[2 * third :], far_two), NEXT)
    mixed = joined(mixed, arrived, steps[1])
    split = down_half_sum.shape[0] // 2
    down_part, up_part = mixed[0:split], mixed[split:]
    down_got, up_got = swap(down_part, rows_size, steps[0]), swap(up_part, rows_size, 1)
    keep_q, away_q = halves(jnp.concatenate([qk_grad, v_grad], axis=1), bits[0])
    arrived_q = swap(after(away_q, far_two), rows_size, bits[0])
    far_three, arrived_q = lax.optimization_barrier((far_three, arrived_q))
    qkv_sum = add_low(keep_q, arrived_q)

    tokens_grad, small = call(
        last_kernel,
        (shape_of((rows, width_all), f32), shape_of((leads + 16, width_all), f32)),
        [VMEM, VMEM, SMEM] + whole_specs(12) + [SMEM], (VMEM, VMEM), "last", 7,
    )(
        tokens, frame_id, lead_index, lead_embed, ln1_gain, perm, here, far_one, far_two, far_three, xgrad,
        sums_two, up_b, qk_sums, v_sums, me,
    )

    down_got, up_got = after(down_got, small), after(up_got, small)
    down_part = joined(down_part, down_got, steps[0])
    up_part = joined(up_part[None], up_got[None], 1)
    down_sum = joined(down_part, swap(down_part, rows_size, 1), 1).astype(f32)
    up_sum = joined(up_part, swap(up_part, rows_size, steps[0]), steps[0], 1).astype(f32)
    up_sum = up_sum.reshape(cut, width_all)

    for bit in bits[1:]:
        (keep_q, away) = halves(qkv_sum, bit)
        qkv_sum = add_low(keep_q, swap(away, rows_size, bit))
    for bit in reversed(bits):
        qkv_sum = joined(qkv_sum, swap(qkv_sum, rows_size, bit), bit)

    for pairs in (CORE, NEXT):
        small = small + over(small, pairs)
    for bit in bits[:-1]:
        small = small + swap(small, rows_size, bit)
    vector = shape_of((width_all,), f32)
    lead_sum, g1, b1, g2, b2, out_b, down_b, up_b_sum, qv_sum = call(
        finish_kernel,
        (shape_of((leads, width_all), f32),) + (vector,) * 6 + (shape_of((hidden,), f32), shape_of((2, width), f32)),
        [VMEM, VMEM, SMEM], (VMEM,) * 9, "finish", 1,
    )(small, swap(small, rows_size, bits[-1]), me)

    pairs_sum = qkv_sum[:, 0 : heads * 128].reshape(width_all, heads, 2, HEAD).transpose(2, 0, 1, 3)
    qkv_out = jnp.concatenate(
        [
            pairs_sum.reshape(2, width_all, width),
            qkv_sum[:, heads * 128 : heads * 128 + width].reshape(1, width_all, width),
        ],
        axis=0,
    ).astype(f32)
    return (
        layer_out, tokens_grad, lead_sum, g1, b1, qkv_out, qv_sum, up_sum[width_all:], out_b, g2, b2,
        up_sum[0:width_all], up_b_sum, down_sum, down_b,
    )


def solution(mesh):
    rows_size = mesh.shape["rows"]
    split = P(("rows", "tp"), None)
    placed = (
        split, P(("rows", "tp")), P("rows"), P(), P(), P(), P(None, None, "tp"), P(None, "tp"),
        P("tp", None), P(), P(), P(), P(None, "tp"), P("tp"), P("tp", None), P(), split,
    )
    return jax.shard_map(
        functools.partial(on_device, rows_size),
        mesh=mesh,
        in_specs=placed,
        out_specs=(
            split, split, P(), P(), P(), P(None, None, "tp"), P(None, "tp"), P("tp", None), P(), P(), P(),
            P(None, "tp"), P("tp"), P("tp", None), P(),
        ),
        check_vma=False,
    )
```

time: 595 us -> 384 us (0.65)
  waiting for transfers between devices: 248 us -> 102 us
  Pallas kernels: 237 us -> 189 us
  starting transfers between devices: 53.4 us -> 38.5 us
    ppermute x56 -> x46, waiting for transfers between devices: 248 us -> 102 us  [the longest x27 53.7 us: over(): return lax.ppermute(value, 'tp', ring)]
    pallas_call x10, Pallas kernels: 195 us -> 152 us  [the longest x2 45 us: attend_back(): call(functools.partial(attend_back_kernel, first), shape_of((count, group...]
    ppermute x56 -> x46, starting transfers between devices: 53.4 us -> 38.5 us  [the longest x19 20 us: swap(): return lax.ppermute(value, 'rows', [(i, i ^ bit) for i in range(size)])]
    squeeze x3 -> x0, local copies, waits for them, and re-layouts: 6.34 us -> none  [the longest x1 2.21 us: on_device(): attended[i]]
    convert_element_type x14 -> x13, other arithmetic: 11.1 us -> 15.5 us  [add_low(): return (left.astype(f32) + right.astype(f32)).astype(bf16)]
  transfers between devices with their start and end apart: 56 -> 46, of which waited for: 30 -> 21; matrix products, arithmetic and copies ran while one was open for 7% -> 8% of each run, Pallas kernels for 32% -> 42%
where the time goes in v2:
time: 384 us; the launch traced here: 377 us
  Pallas kernels  189 us (49%)
  waiting for transfers between devices  102 us (27%)
  starting transfers between devices  38.5 us (10%)
  other arithmetic  26.2 us (7%)
  local copies, waits for them, and re-layouts  20.4 us (5%)
    ppermute x27, waiting for transfers between devices, over(): return lax.ppermute(value, 'tp', ring)  53.7 us
    ppermute x19, waiting for transfers between devices, swap(): return lax.ppermute(value, 'rows', [(i, i ^ bit) for i in range(size)])  48.2 us
    pallas_call x2, Pallas kernels, attend_back(): call(functools.partial(attend_back_kernel, first), shape_of((count, group...  45 us
    pallas_call x1, Pallas kernels, on_device(): call(attend_kernel, (shape_of((group, wide), bf16), shape_of((8, group),...  43 us
    pallas_call x1, Pallas kernels, on_device(): call(middle_kernel, (shape_of((rows, width_all), bf16), shape_of((rows, w...  32 us
    ppermute x19, starting transfers between devices, swap(): return lax.ppermute(value, 'rows', [(i, i ^ bit) for i in range(size)])  20 us
    ppermute x27, starting transfers between devices, over(): return lax.ppermute(value, 'tp', ring)  18.5 us
    pallas_call x1, Pallas kernels, on_device(): call(project_back_kernel, (shape_of((4, rows, heads * 128 + wide), bf16),...  16.7 us
  transfers between devices with their start and end apart: 46, of which 21 were waited for; matrix products, arithmetic and copies ran while one was open for 8% of the time, Pallas kernels for 42%

profile of v2, /device:TPU:0, one launch (start us, length us, event | category | flops | bytes accessed | tf_op | source)
XLA Modules:
  0.0 377.0 jit_solution(17946892087147628082)
XLA Ops:
  0.7 3.0 collective-permute-start
  4.4 2.4 pad_maximum_fusion.2.up0_ref
  7.4 5.1 %pre.1 = (bf16[784,768]{1,0:T(8,128)(2,1)}, bf16[768,768]{1,0:T(8,128)(2,1)}) custom-call(bf16[768,768]{1,0:T(8,128)(2,1)} %tok_ref.5, s32[768]{0:T(1024)} %frame_ref.5, s32[2]{0:T(128)} %lead_ref.5, bf16[32,768]{1,0:T(8,128)(2,1)} %table_ref.5, bf16[768]{0:T(1024)(128)(2,1)} %gain_ref.5, bf16[768]{0:T(1024)(128)(2,1)} %shift_ref.2), custom_call_target="tpu_custom_call" | custom-call | flops 5750000128 | bytes 1024 | tf_op jit(solution)/shard_map/pre/pallas_call | solution.py:616
  15.3 1.1 fusion.4.weight_ref
  16.4 1.3 pad_maximum_fusion.3.weight_ref
  19.5 22.2 %collective-permute-done.1.x2_ref = bf16[784,768]{1,0:T(8,128)(2,1)} collective-permute-done((bf16[784,768]{1,0:T(8,128)(2,1)}, bf16[784,768]{1,0:T(8,128)(2,1)}, u32[]{:S(2)}, u32[]{:S(2)}) %collective-permute-start.1) | collective-permute-done | bytes 1204256 | tf_op jit(solution)/shard_map/ppermute | solution.py:612
  42.0 1.0 copy-done.15
  43.0 1.9 collective-permute-done.7.x3_ref
  44.9 43.0 %attend.1 = (bf16[3072,256]{1,0:T(8,128)(2,1)}, f32[8,3072]{1,0:T(8,128)}, s32[8]{0:T(128)}, bf16[768,192]{1,0:T(8,128)(2,1)}, bf16[768,192]{1,0:T(8,128)(2,1)},...) custom-call(bf16[768,576]{1,0:T(8,128)(2,1)} %pad_maximum_fusion.3.w, ...), custom_call_target="tpu_custom_call" | custom-call | flops 46000001024 | bytes 1024 | tf_op jit(solution)/shard_map/attend/pallas_call | solution.py:655
  88.1 1.8 collective-permute-done.8.at1_ref
  90.1 1.6 collective-permute-start.10
  93.1 10.8 %collective-permute-done.11.at2_ref = bf16[768,192]{1,0:T(8,128)(2,1)S(1)} collective-permute-done((bf16[768,192]{1,0:T(8,128)(2,1)}, bf16[768,192]{1,0:T(8,128)(2,1)S(1)}, u32[]{:S(2)}, u32[]{:S(2)}) %collective-permute-start.11) | collective-permute-done | bytes 294944 | tf_op jit(solution)/shard_map/ppermute | solution.py:612
  103.8 6.7 %collective-permute-done.12.at3_ref = bf16[768,192]{1,0:T(8,128)(2,1)S(1)} collective-permute-done((bf16[768,192]{1,0:T(8,128)(2,1)}, bf16[768,192]{1,0:T(8,128)(2,1)S(1)}, u32[]{:S(2)}, u32[]{:S(2)}) %collective-permute-start.12) | collective-permute-done | bytes 294944 | tf_op jit(solution)/shard_map/ppermute | solution.py:612
  112.0 1.6 collective-permute-done.14.dx3_ref
  115.1 32.0 %middle.1 = (bf16[768,768]{1,0:T(8,128)(2,1)}, f32[768,768]{1,0:T(8,128)}, bf16[768,768]{1,0:T(8,128)(2,1)}, bf16[768,768]{1,0:T(8,128)(2,1)}, bf16[4,768,192]{2...) custom-call(bf16[768,768]{1,0:T(8,128)(2,1)} %tok_ref.5, ...), custom_call_target="tpu_custom_call" | custom-call | flops 36800000000 | bytes 1024 | tf_op jit(solution)/shard_map/middle/pallas_call | solution.py:684
  149.1 16.2 %weight_grad.1 = (bf16[2,1728,768]{2,1,0:T(8,128)(2,1)}, bf16[2,1728,768]{2,1,0:T(8,128)(2,1)}) custom-call(bf16[768,768]{1,0:T(8,128)(2,1)} %get-tuple-element.128.normed_ref, bf16[768,768]{1,0:T(8,128)(2,1)} %og_ref.3, bf16[768,768]{1,0:T(8,128)(2,1)} %get-tuple-element.129.agrad_ref, bf16[4,768,768]{2,1,0:T(8,128)(2,1)} %get-tuple-element.130.act_ref, ...), custom_call_target="tpu_custom_call" | custom-call | flops 20700000256 | bytes 1024 | tf_op jit(solution)/shard_map/weight_grad/pallas_call | solution.py:729
  165.3 1.2 collective-permute-done.17.b3_ref
  167.2 2.0 slice.90
  169.3 8.5 %gather_grad.1 = (bf16[3,3072,128]{2,1,0:T(8,128)(2,1)}, f32[8,3072]{1,0:T(8,128)}) custom-call(s32[8]{0:T(128)} %get-tuple-element.156.counts_ref, bf16[768,192]{1,0:T(8,128)(2,1)} %get-tuple-element.138.b0_ref, bf16[768,192]{1,0:T(8,128)(2,1)} %copy-done.18, bf16[768,192]{1,0:T(8,128)(2,1)} %copy-done.19, bf16[768,192]{1,0:T(8,128)(2,1)} %copy-done.20, ...), custom_call_target="tpu_custom_call" | custom-call | flops 6899999744 | bytes 1024 | tf_op jit(solution)/shard_map/gather_grad/pallas_call | solution.py:742
  177.8 3.9 %add_convert_fusion.5 = (bf16[1,768,768]{2,1,0:T(8,128)(2,1)S(1)}, bf16[768,768]{1,0:T(8,128)(2,1)}) fusion(bf16[2,1728,768]{2,1,0:T(8,128)(2,1)} %collective-permute-done.18, bf16[2,1728,768]{2,1,0:T(8,128)(2,1)} %get-tuple-element.135), kind=kLoop, calls=%fused_computation.5 | loop fusion | flops 4718592 | bytes 7077888 | tf_op jit(solution)/shard_map/convert_element_type | solution.py:577
  181.7 2.0 slice.91
  184.3 2.4 add_convert_fusion.1
  187.1 29.2 %attend_back.2.h01_ref = bf16[2,3072,256]{2,1,0:T(8,128)(2,1)} custom-call(f32[8,3072]{1,0:T(8,128)} %get-tuple-element.145.lse_ref, f32[8,3072]{1,0:T(8,128)} %get-tuple-element.143.inner_ref, bf16[3,3072,128]{2,1,0:T(8,128)(2,1)} %get-tuple-element.146.q_ref, bf16[3,3072,128]{2,1,0:T(8,128)(2,1)} %get-tuple-element.147.k_ref, ...), custom_call_target="tpu_custom_call" | custom-call | flops 34500001792 | bytes 1024 | tf_op jit(solution)/shard_map/attend_back/pallas_call | solution.py:761
  216.4 2.5 fusion.3
  218.8 1.7 collective-permute-start.20
  221.0 1.3 add_convert_fusion.6
  222.2 1.5 collective-permute-start.22
  223.8 15.7 %attend_back.3.h2_ref = bf16[1,3072,256]{2,1,0:T(8,128)(2,1)} custom-call(f32[8,3072]{1,0:T(8,128)} %get-tuple-element.145.lse_ref, f32[8,3072]{1,0:T(8,128)} %get-tuple-element.143.inner_ref, bf16[3,3072,128]{2,1,0:T(8,128)(2,1)} %get-tuple-element.146.q_ref, bf16[3,3072,128]{2,1,0:T(8,128)(2,1)} %get-tuple-element.147.k_ref, ...), custom_call_target="tpu_custom_call" | custom-call | flops 17250000896 | bytes 1024 | tf_op jit(solution)/shard_map/attend_back/pallas_call | solution.py:761
  240.1 1.6 collective-permute-start.23
  241.7 16.7 %project_back.1 = (bf16[4,768,640]{2,1,0:T(8,128)(2,1)}, bf16[768,768]{1,0:T(8,128)(2,1)}, bf16[768,768]{1,0:T(8,128)(2,1)}, bf16[768,768]{1,0:T(8,128)(2,1)}, bf16[768,768]{1,0:T(8,128)(2,1)}) custom-call(s32[8]{0:T(128)} %get-tuple-element.156.counts_ref, bf16[2,3072,256]{2,1,0:T(8,128)(2,1)} %attend_back.2.h01_ref, ...), custom_call_target="tpu_custom_call" | custom-call | flops 13799999488 | bytes 1024 | tf_op jit(solution)/shard_map/project_back/pallas_call | solution.py:793
  259.8 1.9 add_convert_fusion.10
  261.7 2.9 collective-permute-start.28
  264.6 1.6 add_convert_fusion.2
  267.6 1.4 add_convert_fusion.3.mine_ref
  269.0 1.5 collective-permute-start.26
  270.4 7.0 %project_grad.2 = (bf16[768,384]{1,0:T(8,128)(2,1)}, f32[8,384]{1,0:T(8,128)}) custom-call(bf16[784,768]{1,0:T(8,128)(2,1)} %get-tuple-element.108.x0_ref, bf16[784,768]{1,0:T(8,128)(2,1)} %copy-done.15, bf16[784,768]{1,0:T(8,128)(2,1)} %collective-permute-done.1.x2_ref, bf16[784,768]{1,0:T(8,128)(2,1)} %collective-permute-done.7.x3_ref, ...), custom_call_target="tpu_custom_call" | custom-call | flops 4600000000 | bytes 1024 | tf_op jit(solution)/shard_map/project_grad/pallas_call | solution.py:812
  277.5 2.0 collective-permute-done.28
  280.0 1.1 constant_dynamic-update-slice_fusion.1
  281.2 1.2 collective-permute-start.27
  282.4 5.8 %project_grad.3 = (bf16[768,256]{1,0:T(8,128)(2,1)}, f32[8,256]{1,0:T(8,128)}) custom-call(bf16[784,768]{1,0:T(8,128)(2,1)} %get-tuple-element.108.x0_ref, bf16[784,768]{1,0:T(8,128)(2,1)} %copy-done.15, bf16[784,768]{1,0:T(8,128)(2,1)} %collective-permute-done.1.x2_ref, bf16[784,768]{1,0:T(8,128)(2,1)} %collective-permute-done.7.x3_ref, ...), custom_call_target="tpu_custom_call" | custom-call | flops 4600000000 | bytes 1024 | tf_op jit(solution)/shard_map/project_grad/pallas_call | solution.py:812
  288.2 1.0 constant_dynamic-update-slice_fusion
  289.3 2.9 collective-permute-done.27.more_ref
  292.9 1.5 collective-permute-start.29
  294.4 2.1 collective-permute-done.41
  297.3 1.3 collective-permute-start.42
  298.6 4.4 %collective-permute-done.29.rest_ref = bf16[256,768]{1,0:T(8,128)(2,1)} collective-permute-done((bf16[256,768]{1,0:T(8,128)(2,1)S(1)}, bf16[256,768]{1,0:T(8,128)(2,1)}, u32[]{:S(2)}, u32[]{:S(2)}) %collective-permute-start.29) | collective-permute-done | bytes 393248 | tf_op jit(solution)/shard_map/ppermute | solution.py:612
  303.0 3.3 collective-permute-done.30
  306.3 7.7 %last.1 = (f32[768,768]{1,0:T(8,128)}, f32[48,768]{1,0:T(8,128)}) custom-call(bf16[768,768]{1,0:T(8,128)(2,1)} %tok_ref.5, s32[768]{0:T(1024)} %frame_ref.5, s32[2]{0:T(128)} %lead_ref.5, bf16[32,768]{1,0:T(8,128)(2,1)} %table_ref.5, bf16[768]{0:T(1024)(128)(2,1)} %gain_ref.5, bf16[768,768]{1,0:T(8,128)(2,1)} %get-tuple-element.106.perm_ref, ...), custom_call_target="tpu_custom_call" | custom-call | flops 8049999872 | bytes 1024 | tf_op jit(solution)/shard_map/last/pallas_call | solution.py:840
  314.2 2.1 collective-permute-start.36
  316.3 1.0 broadcast_select_fusion.9
  318.0 1.6 collective-permute-start.32
  319.6 3.3 collective-permute-done.36
  323.0 2.4 collective-permute-start.37
  326.1 5.7 %collective-permute-done.37 = bf16[96,640]{1,0:T(8,128)(2,1)S(1)} collective-permute-done((bf16[96,640]{1,0:T(8,128)(2,1)S(1)}, bf16[96,640]{1,0:T(8,128)(2,1)S(1)}, u32[]{:S(2)}, u32[]{:S(2)}) %collective-permute-start.37) | collective-permute-done | bytes 122912 | tf_op jit(solution)/shard_map/ppermute | solution.py:573
  331.9 2.7 collective-permute-start.43
  334.6 1.4 collective-permute-done.33
  336.4 2.8 collective-permute-done.38
  339.8 1.6 maximum_convert_fusion
  341.3 16.0 %collective-permute-done.34 = f32[48,768]{1,0:T(8,128)S(1)} collective-permute-done((f32[48,768]{1,0:T(8,128)S(1)}, f32[48,768]{1,0:T(8,128)S(1)}, u32[]{:S(2)}, u32[]{:S(2)}) %collective-permute-start.34) | collective-permute-done | bytes 147488 | tf_op jit(solution)/shard_map/ppermute | solution.py:573
  357.6 5.4 %collective-permute-done.39 = bf16[192,640]{1,0:T(8,128)(2,1)S(1)} collective-permute-done((bf16[192,640]{1,0:T(8,128)(2,1)S(1)}, bf16[192,640]{1,0:T(8,128)(2,1)S(1)}, u32[]{:S(2)}, u32[]{:S(2)}) %collective-permute-start.39) | collective-permute-done | bytes 245792 | tf_op jit(solution)/shard_map/ppermute | solution.py:573
  364.2 1.6 slice.113
  367.3 1.7 finish.1
  369.0 5.7 %collective-permute-done.40 = bf16[384,640]{1,0:T(8,128)(2,1)S(1)} collective-permute-done((bf16[384,640]{1,0:T(8,128)(2,1)S(1)}, bf16[384,640]{1,0:T(8,128)(2,1)S(1)}, u32[]{:S(2)}, u32[]{:S(2)}) %collective-permute-start.40) | collective-permute-done | bytes 491552 | tf_op jit(solution)/shard_map/ppermute | solution.py:573
  375.5 1.3 maximum_convert_fusion.1
  (170 shorter events, 27.0 us)
Async XLA Ops:
  0.6 6.7 %copy-start.6 = (bf16[768,768]{1,0:T(8,128)(2,1)S(1)}, bf16[768,768]{1,0:T(8,128)(2,1)}, u32[]{:S(2)}) copy-start(bf16[768,768]{1,0:T(8,128)(2,1)} %dn0_ref.1) | copy-start | bytes 3538948
  0.7 11.8 %collective-permute-start = (bf16[192,768]{1,0:T(8,128)(2,1)}, bf16[192,768]{1,0:T(8,128)(2,1)S(1)}, u32[]{:S(2)}, u32[]{:S(2)}) collective-permute-start(bf16[192,768]{1,0:T(8,128)(2,1)} %wo0_ref.1), channel_id=1, source_target_pairs={{0,2},{2,0},{1,3},{3,1},{4,6},{6,4},{5,7},{7,5},{8,10},{10,8},{9,1... | collective-permute-start | bytes 884744 | tf_op jit(solution)/shard_map/ppermute | solution.py:612
  3.7 14.6 %collective-permute-start.2 = (bf16[192,768]{1,0:T(8,128)(2,1)}, bf16[192,768]{1,0:T(8,128)(2,1)}, u32[]{:S(2)}, u32[]{:S(2)}) collective-permute-start(bf16[192,768]{1,0:T(8,128)(2,1)} %wo0_ref.1), channel_id=1, source_target_pairs={{0,1},{1,0},{2,3},{3,2},{4,5},{5,4},{6,7},{7,6},{8,9},{9,8},{10,11... | collective-permute-start | bytes 884744 | tf_op jit(solution)/shard_map/ppermute | solution.py:612
  4.4 2.4 copy-start.7
  6.8 12.7 %collective-permute-start.4 = (bf16[784,768]{1,0:T(8,128)(2,1)}, bf16[784,768]{1,0:T(8,128)(2,1)}, u32[]{:S(2)}, u32[]{:S(2)}) collective-permute-start(bf16[784,768]{1,0:T(8,128)(2,1)} %pad_maximum_fusion.2.up0_ref), channel_id=1, source_target_pairs={{0,1},{1,0},{2,3},{3,2},{4,5},{5,4},{6,7},{7,6},{8,9},{9,8},{10,11... | collective-permute-start | bytes 3612680 | tf_op jit(solution)/shard_map/ppermute | solution.py:612
  7.3 12.2 %collective-permute-start.5 = (bf16[768,768]{1,0:T(8,128)(2,1)S(1)}, bf16[768,768]{1,0:T(8,128)(2,1)}, u32[]{:S(2)}, u32[]{:S(2)}) collective-permute-start(bf16[768,768]{1,0:T(8,128)(2,1)S(1)} %copy-done.6), channel_id=1, source_target_pairs={{0,1},{1,0},{2,3},{3,2},{4,5},{5,4},{6,7},{7,6},{8,9},{9,8},{10,11... | collective-permute-start | bytes 3538952 | tf_op jit(solution)/shard_map/ppermute | solution.py:612
  7.4 5.3 %copy-start.2 = (bf16[3,768,192]{1,2,0:T(8,128)(2,1)S(1)}, bf16[3,768,192]{1,2,0:T(8,128)(2,1)}, u32[]{:S(2)}) copy-start(bf16[3,768,192]{1,2,0:T(8,128)(2,1)} %param.23) | copy-start | bytes 2654212
  12.5 29.2 %collective-permute-start.1 = (bf16[784,768]{1,0:T(8,128)(2,1)}, bf16[784,768]{1,0:T(8,128)(2,1)}, u32[]{:S(2)}, u32[]{:S(2)}) collective-permute-start(bf16[784,768]{1,0:T(8,128)(2,1)} %get-tuple-element.108.x0_ref), channel_id=1, source_target_pairs={{0,2},{2,0},{1,3},{3,1},{4,6},{6,4},{5,7},{7,5},{8,10},{10,8},{9,1... | collective-permute-start | bytes 3612680 | tf_op jit(solution)/shard_map/ppermute | solution.py:612
  16.4 1.7 copy-start.1
  16.4 1.7 copy-start.8
  17.7 1.8 collective-permute-start.3
  19.0 22.9 %collective-permute-start.6 = (bf16[784,768]{1,0:T(8,128)(2,1)S(1)}, bf16[784,768]{1,0:T(8,128)(2,1)S(1)}, u32[]{:S(2)}, u32[]{:S(2)}) collective-permute-start(bf16[784,768]{1,0:T(8,128)(2,1)S(1)} %copy-done.14), channel_id=1, source_target_pairs={{0,1},{1,0},{2,3},{3,2},{4,5},{5,4},{6,7},{7,6},{8,9},{9,8},{10,11... | collective-permute-start | bytes 3612680 | tf_op jit(solution)/shard_map/ppermute | solution.py:612
  19.5 22.2 %copy-start.28 = (bf16[192,768]{1,0:T(8,128)(2,1)}, bf16[192,768]{1,0:T(8,128)(2,1)S(1)}, u32[]{:S(2)}) copy-start(bf16[192,768]{1,0:T(8,128)(2,1)S(1)} %collective-permute-done.3.wo3_ref) | copy-start | bytes 884740
  41.7 3.2 collective-permute-start.7
  41.7 46.4 %collective-permute-start.9 = (bf16[1168,768]{1,0:T(8,128)(2,1)S(1)}, bf16[1168,768]{1,0:T(8,128)(2,1)S(1)}, u32[]{:S(2)}, u32[]{:S(2)}) collective-permute-start(bf16[1168,768]{1,0:T(8,128)(2,1)S(1)} %pad_maximum_fusion), channel_id=1, source_target_pairs={{0,2},{2,0},{1,3},{3,1},{4,6},{6,4},{5,7},{7,5},{8,10},{10,8},{9,1... | collective-permute-start | bytes 5382152 | tf_op jit(solution)/shard_map/ppermute | solution.py:612
  87.9 2.0 collective-permute-start.8
  88.1 26.4 %copy-start.9 = (bf16[1168,768]{1,0:T(8,128)(2,1)}, bf16[1168,768]{1,0:T(8,128)(2,1)S(1)}, u32[]{:S(2)}) copy-start(bf16[1168,768]{1,0:T(8,128)(2,1)S(1)} %collective-permute-done.9.ff2_ref) | copy-start | bytes 5382148
  89.9 24.6 %copy-start.23 = (bf16[768,192]{1,0:T(8,128)(2,1)}, bf16[768,192]{1,0:T(8,128)(2,1)S(1)}, u32[]{:S(2)}) copy-start(bf16[768,192]{1,0:T(8,128)(2,1)S(1)} %collective-permute-done.8.at1_ref) | copy-start | bytes 884740
  89.9 23.7 %collective-permute-start.13 = (bf16[1168,768]{1,0:T(8,128)(2,1)S(1)}, bf16[1168,768]{1,0:T(8,128)(2,1)S(1)}, u32[]{:S(2)}, u32[]{:S(2)}) collective-permute-start(bf16[1168,768]{1,0:T(8,128)(2,1)S(1)} %collective-permute-done.9.ff2_ref), channel_id=1, source_target_pairs={{0,1},{1,0},{2,3},{3,2},{4,5},{5,4},{6,7},{7,6},{8,9},{9,8},{10,11... | collective-permute-start | bytes 5382152 | tf_op jit(solution)/shard_map/ppermute | solution.py:612
  90.1 21.2 %collective-permute-start.10 = (bf16[384,768]{1,0:T(8,128)(2,1)S(1)}, bf16[384,768]{1,0:T(8,128)(2,1)S(1)}, u32[]{:S(2)}, u32[]{:S(2)}) collective-permute-start(bf16[384,768]{1,0:T(8,128)(2,1)S(1)} %slice.85), channel_id=1, source_target_pairs={{0,4},{4,0},{8,12},{12,8},{16,20},{20,16},{24,28},{28,24},{1,5},{5... | collective-permute-start | bytes 1769480 | tf_op jit(solution)/shard_map/ppermute | solution.py:573
  91.7 12.2 %collective-permute-start.11 = (bf16[768,192]{1,0:T(8,128)(2,1)}, bf16[768,192]{1,0:T(8,128)(2,1)S(1)}, u32[]{:S(2)}, u32[]{:S(2)}) collective-permute-start(bf16[768,192]{1,0:T(8,128)(2,1)} %get-tuple-element.118), channel_id=1, source_target_pairs={{0,2},{2,0},{1,3},{3,1},{4,6},{6,4},{5,7},{7,5},{8,10},{10,8},{9,1... | collective-permute-start | bytes 884744 | tf_op jit(solution)/shard_map/ppermute | solution.py:612
  92.2 18.3 %collective-permute-start.12 = (bf16[768,192]{1,0:T(8,128)(2,1)}, bf16[768,192]{1,0:T(8,128)(2,1)S(1)}, u32[]{:S(2)}, u32[]{:S(2)}) collective-permute-start(bf16[768,192]{1,0:T(8,128)(2,1)} %get-tuple-element.119), channel_id=1, source_target_pairs={{0,3},{3,0},{1,2},{2,1},{4,7},{7,4},{5,6},{6,5},{8,11},{11,8},{9,1... | collective-permute-start | bytes 884744 | tf_op jit(solution)/shard_map/ppermute | solution.py:612
  103.8 6.7 %copy-start.24 = (bf16[768,192]{1,0:T(8,128)(2,1)}, bf16[768,192]{1,0:T(8,128)(2,1)S(1)}, u32[]{:S(2)}) copy-start(bf16[768,192]{1,0:T(8,128)(2,1)S(1)} %collective-permute-done.11.at2_ref) | copy-start | bytes 884740
  111.3 2.3 copy-start.16
  111.3 2.3 collective-permute-start.14
  147.2 18.2 %collective-permute-start.15 = (bf16[768,192]{1,0:T(8,128)(2,1)}, bf16[768,192]{1,0:T(8,128)(2,1)S(1)}, u32[]{:S(2)}, u32[]{:S(2)}) collective-permute-start(bf16[768,192]{1,0:T(8,128)(2,1)} %get-tuple-element.125), channel_id=1, source_target_pairs={{0,1},{1,0},{2,3},{3,2},{4,5},{5,4},{6,7},{7,6},{8,9},{9,8},{10,11... | collective-permute-start | bytes 884744 | tf_op jit(solution)/shard_map/ppermute | solution.py:612
  147.6 17.7 %collective-permute-start.16 = (bf16[768,192]{1,0:T(8,128)(2,1)}, bf16[768,192]{1,0:T(8,128)(2,1)S(1)}, u32[]{:S(2)}, u32[]{:S(2)}) collective-permute-start(bf16[768,192]{1,0:T(8,128)(2,1)} %get-tuple-element.126), channel_id=1, source_target_pairs={{0,2},{2,0},{1,3},{3,1},{4,6},{6,4},{5,7},{7,5},{8,10},{10,8},{9,1... | collective-permute-start | bytes 884744 | tf_op jit(solution)/shard_map/ppermute | solution.py:612
  148.1 18.5 %collective-permute-start.17 = (bf16[768,192]{1,0:T(8,128)(2,1)}, bf16[768,192]{1,0:T(8,128)(2,1)S(1)}, u32[]{:S(2)}, u32[]{:S(2)}) collective-permute-start(bf16[768,192]{1,0:T(8,128)(2,1)} %get-tuple-element.127), channel_id=1, source_target_pairs={{0,3},{3,0},{1,2},{2,1},{4,7},{7,4},{5,6},{6,5},{8,11},{11,8},{9,1... | collective-permute-start | bytes 884744 | tf_op jit(solution)/shard_map/ppermute | solution.py:612
  165.3 3.9 %copy-start.18 = (bf16[768,192]{1,0:T(8,128)(2,1)}, bf16[768,192]{1,0:T(8,128)(2,1)S(1)}, u32[]{:S(2)}) copy-start(bf16[768,192]{1,0:T(8,128)(2,1)S(1)} %collective-permute-done.15.b1_ref) | copy-start | bytes 884740
  165.3 3.9 %copy-start.19 = (bf16[768,192]{1,0:T(8,128)(2,1)}, bf16[768,192]{1,0:T(8,128)(2,1)S(1)}, u32[]{:S(2)}) copy-start(bf16[768,192]{1,0:T(8,128)(2,1)S(1)} %collective-permute-done.16.b2_ref) | copy-start | bytes 884740
  166.6 2.7 copy-start.20
  166.6 11.2 %collective-permute-start.18 = (bf16[2,1728,768]{2,1,0:T(8,128)(2,1)}, bf16[2,1728,768]{2,1,0:T(8,128)(2,1)}, u32[]{:S(2)}, u32[]{:S(2)}) collective-permute-start(bf16[2,1728,768]{2,1,0:T(8,128)(2,1)} %get-tuple-element.136), channel_id=1, source_target_pairs={{0,1},{1,0},{2,3},{3,2},{4,5},{5,4},{6,7},{7,6},{8,9},{9,8},{10,11... | collective-permute-start | bytes 15925256 | tf_op jit(solution)/shard_map/ppermute | solution.py:612
  183.8 32.6 %collective-permute-start.19 = (bf16[768,768]{1,0:T(8,128)(2,1)}, bf16[768,768]{1,0:T(8,128)(2,1)}, u32[]{:S(2)}, u32[]{:S(2)}) collective-permute-start(bf16[768,768]{1,0:T(8,128)(2,1)} %get-tuple-element.198), channel_id=1, source_target_pairs={{0,2},{2,0},{1,3},{3,1},{4,6},{6,4},{5,7},{7,5},{8,10},{10,8},{9,1... | collective-permute-start | bytes 3538952 | tf_op jit(solution)/shard_map/ppermute | solution.py:612
  186.7 34.3 %collective-permute-start.21 = (bf16[2,480,768]{2,1,0:T(8,128)(2,1)}, bf16[2,480,768]{2,1,0:T(8,128)(2,1)S(1)}, u32[]{:S(2)}, u32[]{:S(2)}) collective-permute-start(bf16[2,480,768]{2,1,0:T(8,128)(2,1)} %get-tuple-element.199), channel_id=1, source_target_pairs={{0,4},{4,0},{8,12},{12,8},{16,20},{20,16},{24,28},{28,24},{1,5},{5... | collective-permute-start | bytes 4423688 | tf_op jit(solution)/shard_map/ppermute | solution.py:573
  216.3 4.6 %copy-start = (bf16[2,480,768]{2,1,0:T(8,128)(2,1)S(1)}, bf16[2,480,768]{2,1,0:T(8,128)(2,1)}, u32[]{:S(2)}) copy-start(bf16[2,480,768]{2,1,0:T(8,128)(2,1)} %get-tuple-element.200) | copy-start | bytes 4423684
  218.8 20.7 %collective-permute-start.20 = (bf16[384,768]{1,0:T(8,128)(2,1)}, bf16[384,768]{1,0:T(8,128)(2,1)S(1)}, u32[]{:S(2)}, u32[]{:S(2)}) collective-permute-start(bf16[384,768]{1,0:T(8,128)(2,1)} %get-tuple-element.204), channel_id=1, source_target_pairs={{0,4},{4,0},{8,12},{12,8},{16,20},{20,16},{24,28},{28,24},{1,5},{5... | collective-permute-start | bytes 1769480 | tf_op jit(solution)/shard_map/ppermute | solution.py:573
  222.2 17.6 %collective-permute-start.22 = (bf16[480,768]{1,0:T(8,128)(2,1)}, bf16[480,768]{1,0:T(8,128)(2,1)S(1)}, u32[]{:S(2)}, u32[]{:S(2)}) collective-permute-start(bf16[480,768]{1,0:T(8,128)(2,1)} %get-tuple-element.202), channel_id=1, source_target_pairs={{0,2},{2,0},{1,3},{3,1},{4,6},{6,4},{5,7},{7,5},{8,10},{10,8},{9,1... | collective-permute-start | bytes 2211848 | tf_op jit(solution)/shard_map/ppermute | solution.py:612
  240.1 18.3 %collective-permute-start.23 = (bf16[432,768]{1,0:T(8,128)(2,1)S(1)}, bf16[432,768]{1,0:T(8,128)(2,1)S(1)}, u32[]{:S(2)}, u32[]{:S(2)}) collective-permute-start(bf16[432,768]{1,0:T(8,128)(2,1)S(1)} %pad_maximum_fusion.6), channel_id=1, source_target_pairs={{0,8},{4,12},{8,0},{12,4},{16,24},{20,28},{24,16},{28,20},{1,9},{5... | collective-permute-start | bytes 1990664 | tf_op jit(solution)/shard_map/ppermute | solution.py:573
  258.4 6.1 %copy-start.4 = (bf16[768,768]{1,0:T(8,128)(2,1)S(1)}, bf16[768,768]{1,0:T(8,128)(2,1)}, u32[]{:S(2)}) copy-start(bf16[768,768]{1,0:T(8,128)(2,1)} %get-tuple-element.162) | copy-start | bytes 3538948
  259.3 5.3 %collective-permute-start.25 = (bf16[768,768]{1,0:T(8,128)(2,1)}, bf16[768,768]{1,0:T(8,128)(2,1)}, u32[]{:S(2)}, u32[]{:S(2)}) collective-permute-start(bf16[768,768]{1,0:T(8,128)(2,1)} %get-tuple-element.163), channel_id=1, source_target_pairs={{0,1},{1,0},{2,3},{3,2},{4,5},{5,4},{6,7},{7,6},{8,9},{9,8},{10,11... | collective-permute-start | bytes 3538952 | tf_op jit(solution)/shard_map/ppermute | solution.py:612
  259.3 7.7 %collective-permute-start.24 = (bf16[768,768]{1,0:T(8,128)(2,1)}, bf16[768,768]{1,0:T(8,128)(2,1)S(1)}, u32[]{:S(2)}, u32[]{:S(2)}) collective-permute-start(bf16[768,768]{1,0:T(8,128)(2,1)} %get-tuple-element.161), channel_id=1, source_target_pairs={{0,1},{1,0},{2,3},{3,2},{4,5},{5,4},{6,7},{7,6},{8,9},{9,8},{10,11... | collective-permute-start | bytes 3538952 | tf_op jit(solution)/shard_map/ppermute | solution.py:612
  261.7 17.9 %collective-permute-start.28 = (bf16[216,768]{1,0:T(8,128)(2,1)S(1)}, bf16[216,768]{1,0:T(8,128)(2,1)S(1)}, u32[]{:S(2)}, u32[]{:S(2)}) collective-permute-start(bf16[216,768]{1,0:T(8,128)(2,1)S(1)} %get-tuple-element.210), channel_id=1, source_target_pairs={{0,16},{4,20},{8,24},{12,28},{16,0},{20,4},{24,8},{28,12},{1,17},{... | collective-permute-start | bytes 995336 | tf_op jit(solution)/shard_map/ppermute | solution.py:573
  269.0 12.2 %collective-permute-start.26 = (bf16[256,768]{1,0:T(8,128)(2,1)S(1)}, bf16[256,768]{1,0:T(8,128)(2,1)S(1)}, u32[]{:S(2)}, u32[]{:S(2)}) collective-permute-start(bf16[256,768]{1,0:T(8,128)(2,1)S(1)} %get-tuple-element.215), channel_id=1, source_target_pairs={{0,2},{2,0},{1,3},{3,1},{4,6},{6,4},{5,7},{7,5},{8,10},{10,8},{9,1... | collective-permute-start | bytes 1179656 | tf_op jit(solution)/shard_map/ppermute | solution.py:612
  279.6 16.9 %collective-permute-start.41 = (bf16[216,768]{1,0:T(8,128)(2,1)S(1)}, bf16[216,768]{1,0:T(8,128)(2,1)S(1)}, u32[]{:S(2)}, u32[]{:S(2)}) collective-permute-start(bf16[216,768]{1,0:T(8,128)(2,1)S(1)} %add_convert_fusion.9), channel_id=1, source_target_pairs={{0,16},{4,20},{8,24},{12,28},{16,0},{20,4},{24,8},{28,12},{1,17},{... | collective-permute-start | bytes 995336 | tf_op jit(solution)/shard_map/ppermute | solution.py:573
  281.2 7.0 %copy-start.21 = (bf16[256,768]{1,0:T(8,128)(2,1)}, bf16[256,768]{1,0:T(8,128)(2,1)S(1)}, u32[]{:S(2)}) copy-start(bf16[256,768]{1,0:T(8,128)(2,1)S(1)} %collective-permute-done.26.one_ref) | copy-start | bytes 1179652
  281.2 11.0 %collective-permute-start.27 = (bf16[256,768]{1,0:T(8,128)(2,1)}, bf16[256,768]{1,0:T(8,128)(2,1)S(1)}, u32[]{:S(2)}, u32[]{:S(2)}) collective-permute-start(bf16[256,768]{1,0:T(8,128)(2,1)} %get-tuple-element.169), channel_id=1, source_target_pairs={{0,2},{2,0},{1,3},{3,1},{4,6},{6,4},{5,7},{7,5},{8,10},{10,8},{9,1... | collective-permute-start | bytes 1179656 | tf_op jit(solution)/shard_map/ppermute | solution.py:612
  292.2 14.2 %collective-permute-start.30 = (bf16[384,640]{1,0:T(8,128)(2,1)S(1)}, bf16[384,640]{1,0:T(8,128)(2,1)S(1)}, u32[]{:S(2)}, u32[]{:S(2)}) collective-permute-start(bf16[384,640]{1,0:T(8,128)(2,1)S(1)} %constant_dynamic-slice_fusion), channel_id=1, source_target_pairs={{0,4},{4,0},{8,12},{12,8},{16,20},{20,16},{24,28},{28,24},{1,5},{5... | collective-permute-start | bytes 1474568 | tf_op jit(solution)/shard_map/ppermute | solution.py:573
  292.9 10.1 %collective-permute-start.29 = (bf16[256,768]{1,0:T(8,128)(2,1)S(1)}, bf16[256,768]{1,0:T(8,128)(2,1)}, u32[]{:S(2)}, u32[]{:S(2)}) collective-permute-start(bf16[256,768]{1,0:T(8,128)(2,1)S(1)} %get-tuple-element.174), channel_id=1, source_target_pairs={{0,2},{2,0},{1,3},{3,1},{4,6},{6,4},{5,7},{7,5},{8,10},{10,8},{9,1... | collective-permute-start | bytes 1179656 | tf_op jit(solution)/shard_map/ppermute | solution.py:612
  297.3 16.7 %collective-permute-start.44 = (bf16[192,768]{1,0:T(8,128)(2,1)}, bf16[192,768]{1,0:T(8,128)(2,1)}, u32[]{:S(2)}, u32[]{:S(2)}) collective-permute-start(bf16[192,768]{1,0:T(8,128)(2,1)} %slice.114), channel_id=1, source_target_pairs={{0,8},{4,12},{8,0},{12,4},{16,24},{20,28},{24,16},{28,20},{1,9},{5... | collective-permute-start | bytes 884744 | tf_op jit(solution)/shard_map/ppermute | solution.py:573
  297.3 20.6 %collective-permute-start.42 = (bf16[240,768]{1,0:T(8,128)(2,1)S(1)}, bf16[240,768]{1,0:T(8,128)(2,1)S(1)}, u32[]{:S(2)}, u32[]{:S(2)}) collective-permute-start(bf16[240,768]{1,0:T(8,128)(2,1)S(1)} %pad_maximum_fusion.10), channel_id=1, source_target_pairs={{0,4},{4,0},{8,12},{12,8},{16,20},{20,16},{24,28},{28,24},{1,5},{5... | collective-permute-start | bytes 1105928 | tf_op jit(solution)/shard_map/ppermute | solution.py:573
  314.0 3.9 %collective-permute-start.31 = (f32[48,768]{1,0:T(8,128)}, f32[48,768]{1,0:T(8,128)S(1)}, u32[]{:S(2)}, u32[]{:S(2)}) collective-permute-start(f32[48,768]{1,0:T(8,128)} %get-tuple-element.183), channel_id=1, source_target_pairs={{0,1},{1,0},{2,3},{3,2},{4,5},{5,4},{6,7},{7,6},{8,9},{9,8},{10,11... | collective-permute-start | bytes 442376 | tf_op jit(solution)/shard_map/ppermute | solution.py:612
  314.2 3.8 %copy-start.11 = (f32[48,768]{1,0:T(8,128)S(1)}, f32[48,768]{1,0:T(8,128)}, u32[]{:S(2)}) copy-start(f32[48,768]{1,0:T(8,128)} %get-tuple-element.183) | copy-start | bytes 442372
  314.2 8.7 %collective-permute-start.36 = (bf16[192,640]{1,0:T(8,128)(2,1)S(1)}, bf16[192,640]{1,0:T(8,128)(2,1)S(1)}, u32[]{:S(2)}, u32[]{:S(2)}) collective-permute-start(bf16[192,640]{1,0:T(8,128)(2,1)S(1)} %constant_dynamic-slice_fusion.2), channel_id=1, source_target_pairs={{0,8},{4,12},{8,0},{12,4},{16,24},{20,28},{24,16},{28,20},{1,9},{5... | collective-permute-start | bytes 737288 | tf_op jit(solution)/shard_map/ppermute | solution.py:573
  317.3 22.2 %collective-permute-start.45 = (bf16[384,768]{1,0:T(8,128)(2,1)S(1)}, bf16[384,768]{1,0:T(8,128)(2,1)S(1)}, u32[]{:S(2)}, u32[]{:S(2)}) collective-permute-start(bf16[384,768]{1,0:T(8,128)(2,1)S(1)} %pad_maximum_fusion.7), channel_id=1, source_target_pairs={{0,4},{4,0},{8,12},{12,8},{16,20},{20,16},{24,28},{28,24},{1,5},{5... | collective-permute-start | bytes 1769480 | tf_op jit(solution)/shard_map/ppermute | solution.py:573
  318.0 7.5 %collective-permute-start.32 = (f32[48,768]{1,0:T(8,128)S(1)}, f32[48,768]{1,0:T(8,128)S(1)}, u32[]{:S(2)}, u32[]{:S(2)}) collective-permute-start(f32[48,768]{1,0:T(8,128)S(1)} %add.196), channel_id=1, source_target_pairs={{0,2},{2,0},{1,3},{3,1},{4,6},{6,4},{5,7},{7,5},{8,10},{10,8},{9,1... | collective-permute-start | bytes 442376 | tf_op jit(solution)/shard_map/ppermute | solution.py:612
  323.0 8.7 %collective-permute-start.37 = (bf16[96,640]{1,0:T(8,128)(2,1)S(1)}, bf16[96,640]{1,0:T(8,128)(2,1)S(1)}, u32[]{:S(2)}, u32[]{:S(2)}) collective-permute-start(bf16[96,640]{1,0:T(8,128)(2,1)S(1)} %constant_dynamic-slice_fusion.1), channel_id=1, source_target_pairs={{0,16},{4,20},{8,24},{12,28},{16,0},{20,4},{24,8},{28,12},{1,17},{... | collective-permute-start | bytes 368648 | tf_op jit(solution)/shard_map/ppermute | solution.py:573
  325.5 10.5 %collective-permute-start.33 = (f32[48,768]{1,0:T(8,128)S(1)}, f32[48,768]{1,0:T(8,128)S(1)}, u32[]{:S(2)}, u32[]{:S(2)}) collective-permute-start(f32[48,768]{1,0:T(8,128)S(1)} %add.197), channel_id=1, source_target_pairs={{0,4},{4,0},{8,12},{12,8},{16,20},{20,16},{24,28},{28,24},{1,5},{5... | collective-permute-start | bytes 442376 | tf_op jit(solution)/shard_map/ppermute | solution.py:573
  331.8 7.4 %collective-permute-start.38 = (bf16[96,640]{1,0:T(8,128)(2,1)S(1)}, bf16[96,640]{1,0:T(8,128)(2,1)S(1)}, u32[]{:S(2)}, u32[]{:S(2)}) collective-permute-start(bf16[96,640]{1,0:T(8,128)(2,1)S(1)} %add_convert_fusion.15), channel_id=1, source_target_pairs={{0,16},{4,20},{8,24},{12,28},{16,0},{20,4},{24,8},{28,12},{1,17},{... | collective-permute-start | bytes 368648 | tf_op jit(solution)/shard_map/ppermute | solution.py:573
  331.9 31.8 %collective-permute-start.43 = (bf16[2,240,768]{2,1,0:T(8,128)(2,1)S(1)}, bf16[2,240,768]{2,1,0:T(8,128)(2,1)S(1)}, u32[]{:S(2)}, u32[]{:S(2)}) collective-permute-start(bf16[2,240,768]{2,1,0:T(8,128)(2,1)S(1)} %pad_maximum_fusion.5), channel_id=1, source_target_pairs={{0,8},{4,12},{8,0},{12,4},{16,24},{20,28},{24,16},{28,20},{1,9},{5... | collective-permute-start | bytes 2211848 | tf_op jit(solution)/shard_map/ppermute | solution.py:573
  336.0 21.3 %collective-permute-start.34 = (f32[48,768]{1,0:T(8,128)S(1)}, f32[48,768]{1,0:T(8,128)S(1)}, u32[]{:S(2)}, u32[]{:S(2)}) collective-permute-start(f32[48,768]{1,0:T(8,128)S(1)} %add.198), channel_id=1, source_target_pairs={{0,8},{4,12},{8,0},{12,4},{16,24},{20,28},{24,16},{28,20},{1,9},{5... | collective-permute-start | bytes 442376 | tf_op jit(solution)/shard_map/ppermute | solution.py:573
  339.5 23.5 %collective-permute-start.39 = (bf16[192,640]{1,0:T(8,128)(2,1)S(1)}, bf16[192,640]{1,0:T(8,128)(2,1)S(1)}, u32[]{:S(2)}, u32[]{:S(2)}) collective-permute-start(bf16[192,640]{1,0:T(8,128)(2,1)S(1)} %pad_maximum_fusion.11), channel_id=1, source_target_pairs={{0,8},{4,12},{8,0},{12,4},{16,24},{20,28},{24,16},{28,20},{1,9},{5... | collective-permute-start | bytes 737288 | tf_op jit(solution)/shard_map/ppermute | solution.py:573
  357.3 6.5 %copy-start.10 = (f32[48,768]{1,0:T(8,128)}, f32[48,768]{1,0:T(8,128)S(1)}, u32[]{:S(2)}) copy-start(f32[48,768]{1,0:T(8,128)S(1)} %add.199.left_ref) | copy-start | bytes 442372
  357.3 9.3 %collective-permute-start.35 = (f32[48,768]{1,0:T(8,128)S(1)}, f32[48,768]{1,0:T(8,128)S(1)}, u32[]{:S(2)}, u32[]{:S(2)}) collective-permute-start(f32[48,768]{1,0:T(8,128)S(1)} %add.199.left_ref), channel_id=1, source_target_pairs={{0,16},{4,20},{8,24},{12,28},{16,0},{20,4},{24,8},{28,12},{1,17},{... | collective-permute-start | bytes 442376 | tf_op jit(solution)/shard_map/ppermute | solution.py:573
  363.1 11.6 %collective-permute-start.40 = (bf16[384,640]{1,0:T(8,128)(2,1)S(1)}, bf16[384,640]{1,0:T(8,128)(2,1)S(1)}, u32[]{:S(2)}, u32[]{:S(2)}) collective-permute-start(bf16[384,640]{1,0:T(8,128)(2,1)S(1)} %pad_maximum_fusion.8), channel_id=1, source_target_pairs={{0,4},{4,0},{8,12},{12,8},{16,20},{20,16},{24,28},{28,24},{1,5},{5... | collective-permute-start | bytes 1474568 | tf_op jit(solution)/shard_map/ppermute | solution.py:573
  (13 other events, 13.3 us)
